TPU v7x, 32 devices: a whole 2x2x4 slice. The times are simulated.
32 devices in a mesh: mesh: 4 (over y, x), harm: 8 (over z, core).
Axes of the slice: x: 2, y: 2, z: 4, core: 2. Of those that a mesh axis runs over, the one named last changes fastest.
Arguments:
- current_pattern: float32 [128, 4096], P('mesh'), may hold values from -6 to 6
- conductivity: float32 [128, 4096], P('mesh'), may hold values from 0.5 to 8
- cooling: float32 [128, 4096], P('mesh'), may hold values from 0.05 to 0.5
- harm_order: int32 [8], P('harm'), may hold values from 8 to 64
- harm_amp: int32 [8], P('harm'), may hold values from 1 to 4
- block_counts: int32 [8], P('harm'), may hold values from 1 to 32, as said below
Outputs:
- averaged_dissipation: float32 [128, 4096], P('mesh', 'harm')
- thermal_increase: float32 [128, 4096], P('mesh', 'harm')
Inputs may be any that keep to these rules, and one draw needn't show every extreme that they name: `block_counts`: some harmonic has block count 32.
All inputs are finite; a program needn't handle non-finite values.
Results may differ from a plain program's by a relative error of at most 0.00002.
Values sent between devices are 32-bit elements; how exact they have to be, the bound alone decides.
No kernel may reach another device: no remote copies, remote signals or barrier semaphores. Data moves between devices by JAX's collectives and lax.ppermute only.
A program may use at most 64 MiB of HBM per device.

v0:
```python
import jax
import jax.numpy as jnp
from jax import lax
from jax.sharding import PartitionSpec as P

BLK = 128
EDDY_SWEEPS = 3
HEAT_SWEEPS = 4


base_freq = 0.1


def padded(value, sides, width):
    for axis, dim in sides:
        size, length = (lax.axis_size(axis), value.shape[dim])
        up = [(i, (i + 1) % size) for i in range(size - 1)]
        down = [(j, i) for i, j in up]
        last = lax.slice_in_dim(value, length - width, length, axis=dim)
        initial = lax.slice_in_dim(value, 0, width, axis=dim)
        before = lax.ppermute(last, axis, up)
        after = lax.ppermute(initial, axis, down)
        value = jnp.concatenate([before, value, after], axis=dim)
    return value


def bordered_lateral_margin(field):
    widths = [(0, 0)] * (field.ndim - 1) + [(1, 1)]
    return jnp.pad(field, widths)


def eddy_loss(cols, current_pattern, conductivity, omega, amp, count):
    columns = jnp.arange(cols)
    mask = (columns < count * BLK).astype(jnp.float32)[None, :]
    source = amp * current_pattern * mask
    product = omega * conductivity
    denom = 16.0 + product * product
    inv_re = 4.0 / denom
    inv_im = -product / denom
    potential = jnp.stack([source * inv_re, source * inv_im])
    for sweep in range(EDDY_SWEEPS - 1):
        extended_subdomain = padded(potential, (("mesh", 1),), 1)
        outer_margins = bordered_lateral_margin(potential)
        nearby_nodes = (
            extended_subdomain[:, 2:, :]
            + extended_subdomain[:, :-2, :]
            + outer_margins[:, :, 2:]
            + outer_margins[:, :, :-2]
        )
        near_re = source + nearby_nodes[0]
        near_im = nearby_nodes[1]
        potential = jnp.stack(
            [
                mask * (near_re * inv_re - near_im * inv_im),
                mask * (near_re * inv_im + near_im * inv_re),
            ]
        )
    loss = (
        0.5
        * omega
        * omega
        * conductivity
        * (potential[0] * potential[0] + potential[1] * potential[1])
    )
    return loss


def on_device(current_pattern, conductivity, cooling, harm_order, harm_amp, block_counts):
    harmonics = lax.axis_size("harm")
    omega = base_freq * harm_order[0].astype(jnp.float32)
    amp = harm_amp[0].astype(jnp.float32)
    count = block_counts[0]
    width = current_pattern.shape[1]
    local_loss = eddy_loss(width, current_pattern, conductivity, omega, amp, count)
    piece_ratio = width // harmonics
    offset_index = lax.axis_index("harm") * piece_ratio
    entire_dissipation_map = lax.psum(local_loss, "harm") / harmonics
    inverted_weight = 1.0 / (4.0 + cooling)
    thermal_increase = entire_dissipation_map * inverted_weight
    for sweep in range(HEAT_SWEEPS - 1):
        extended_subdomain = padded(thermal_increase, (("mesh", 0),), 1)
        outer_margins = bordered_lateral_margin(thermal_increase)
        nearby_nodes = (
            extended_subdomain[2:, :]
            + extended_subdomain[:-2, :]
            + outer_margins[:, 2:]
            + outer_margins[:, :-2]
        )
        thermal_increase = (entire_dissipation_map + nearby_nodes) * inverted_weight
    averaged_dissipation = lax.dynamic_slice_in_dim(
        entire_dissipation_map, offset_index, piece_ratio, 1
    )
    return (
        averaged_dissipation,
        lax.dynamic_slice_in_dim(thermal_increase, offset_index, piece_ratio, 1),
    )


def solution(mesh):
    return jax.shard_map(
        on_device,
        mesh=mesh,
        in_specs=(
            P("mesh", None),
            P("mesh", None),
            P("mesh", None),
            P("harm"),
            P("harm"),
            P("harm"),
        ),
        out_specs=(P("mesh", "harm"), P("mesh", "harm")),
        check_vma=False,
    )
```

profile of v0, /device:TPU:0, one launch (start us, length us, event | category | flops | bytes accessed | tf_op | source)
XLA Modules:
  0.0 124.1 jit_solution(10794816148529985782)
XLA Ops:
  7.2 0.0 all-reduce.7.cloned.1.call-start
  9.2 1.4 %multiply_bitcast_fusion.2 = (f32[1,32,4096]{2,1,0:T(8,128)S(1)}, f32[1,32,4096]{2,1,0:T(8,128)S(1)}) fusion(f32[32,4096]{1,0:T(8,128)} %param.6, f32[]{:T(128)} %bitcast.2, f32[4096]{0:T(1024)S(1)} %fusion.30, f32[32,4096]{1,0:T(8,128)} %param.7, f32[]{:T(128)} %bitcast.3), kind=kLoop, calls=%fused_computation.52 | loop fusion | flops 1310720 | bytes 2113544 | tf_op jit(solution)/shard_map/stack | solution.py:40
  10.6 1.3 %collective-permute-start = (f32[2,1,4096]{2,1,0:T(1,128)S(1)}, f32[2,1,4096]{2,1,0:T(1,128)S(1)}, u32[]{:S(2)}, u32[]{:S(2)}) collective-permute-start(f32[2,1,4096]{2,1,0:T(1,128)S(1)} %get-tuple-element.10), channel_id=1, source_target_pairs={{8,0},{16,8},{24,16},{9,1},{17,9},{25,17},{10,2},{18,10},{26,18},{... | collective-permute-start | bytes 98312 | tf_op jit(solution)/shard_map/ppermute | solution.py:22
  11.9 5.5 %collective-permute-start.1 = (f32[2,1,4096]{2,1,0:T(1,128)S(1)}, f32[2,1,4096]{2,1,0:T(1,128)S(1)}, u32[]{:S(2)}, u32[]{:S(2)}) collective-permute-start(f32[2,1,4096]{2,1,0:T(1,128)S(1)} %get-tuple-element.11), channel_id=1, source_target_pairs={{0,8},{8,16},{16,24},{1,9},{9,17},{17,25},{2,10},{10,18},{18,26},{... | collective-permute-start | bytes 98312 | tf_op jit(solution)/shard_map/ppermute | solution.py:21
  17.4 0.1 pad_maximum_fusion
  17.5 0.0 copy-start.2
  17.5 0.0 copy-start.3
  17.5 0.0 collective-permute-done
  17.5 1.5 %collective-permute-done.1 = f32[2,1,4096]{2,1,0:T(1,128)S(1)} collective-permute-done((f32[2,1,4096]{2,1,0:T(1,128)S(1)}, f32[2,1,4096]{2,1,0:T(1,128)S(1)}, u32[]{:S(2)}, u32[]{:S(2)}) %collective-permute-start.1) | collective-permute-done | bytes 32800 | tf_op jit(solution)/shard_map/ppermute | solution.py:21
  19.0 0.7 fusion.5
  19.7 0.0 copy-done.2
  19.7 0.0 copy-done.3
  19.7 0.3 multiply_bitcast_fusion
  20.1 1.3 %collective-permute-start.2 = (f32[2,1,4096]{2,1,0:T(1,128)S(1)}, f32[2,1,4096]{2,1,0:T(1,128)S(1)}, u32[]{:S(2)}, u32[]{:S(2)}) collective-permute-start(f32[2,1,4096]{2,1,0:T(1,128)S(1)} %get-tuple-element.8), channel_id=1, source_target_pairs={{8,0},{16,8},{24,16},{9,1},{17,9},{25,17},{10,2},{18,10},{26,18},{... | collective-permute-start | bytes 98312 | tf_op jit(solution)/shard_map/ppermute | solution.py:22
  21.4 5.4 %collective-permute-start.3 = (f32[2,1,4096]{2,1,0:T(1,128)S(1)}, f32[2,1,4096]{2,1,0:T(1,128)S(1)}, u32[]{:S(2)}, u32[]{:S(2)}) collective-permute-start(f32[2,1,4096]{2,1,0:T(1,128)S(1)} %get-tuple-element.9), channel_id=1, source_target_pairs={{0,8},{8,16},{16,24},{1,9},{9,17},{17,25},{2,10},{10,18},{18,26},{... | collective-permute-start | bytes 98312 | tf_op jit(solution)/shard_map/ppermute | solution.py:21
  26.8 0.1 pad_maximum_fusion.1
  26.9 0.0 collective-permute-done.2
  26.9 1.5 %collective-permute-done.3 = f32[2,1,4096]{2,1,0:T(1,128)S(1)} collective-permute-done((f32[2,1,4096]{2,1,0:T(1,128)S(1)}, f32[2,1,4096]{2,1,0:T(1,128)S(1)}, u32[]{:S(2)}, u32[]{:S(2)}) %collective-permute-start.3) | collective-permute-done | bytes 32800 | tf_op jit(solution)/shard_map/ppermute | solution.py:21
  28.4 0.7 fusion.2
  29.1 0.0 copy-start
  29.1 1.2 add_multiply_fusion
  30.3 0.0 all-reduce.7.cloned.1.call-update
  30.3 60.6 %all-reduce.7.cloned.1.call-done = f32[32,4096]{1,0:T(8,128)} async-done(((f32[32,4096]{1,0:T(8,128)}), f32[32,4096]{1,0:T(8,128)}) %all-reduce.7.cloned.1.call-update) | async-done | bytes 524304 | tf_op jit(solution)/shard_map/psum | solution.py:77
  90.9 0.0 copy-done
  90.9 0.0 copy-start.1
  90.9 1.2 broadcast_multiply_fusion
  92.2 1.3 %collective-permute-start.4 = (f32[1,4096]{1,0:T(1,128)S(1)}, f32[1,4096]{1,0:T(1,128)S(1)}, u32[]{:S(2)}, u32[]{:S(2)}) collective-permute-start(f32[1,4096]{1,0:T(1,128)S(1)} %get-tuple-element.21), channel_id=1, source_target_pairs={{8,0},{16,8},{24,16},{9,1},{17,9},{25,17},{10,2},{18,10},{26,18},{... | collective-permute-start | bytes 49160 | tf_op jit(solution)/shard_map/ppermute | solution.py:22
  93.5 4.5 %collective-permute-start.5 = (f32[1,4096]{1,0:T(1,128)S(1)}, f32[1,4096]{1,0:T(1,128)S(1)}, u32[]{:S(2)}, u32[]{:S(2)}) collective-permute-start(f32[1,4096]{1,0:T(1,128)S(1)} %get-tuple-element.22), channel_id=1, source_target_pairs={{0,8},{8,16},{16,24},{1,9},{9,17},{17,25},{2,10},{10,18},{18,26},{... | collective-permute-start | bytes 49160 | tf_op jit(solution)/shard_map/ppermute | solution.py:21
  98.1 0.0 collective-permute-done.4
  98.1 1.4 %collective-permute-done.5 = f32[1,4096]{1,0:T(1,128)S(1)} collective-permute-done((f32[1,4096]{1,0:T(1,128)S(1)}, f32[1,4096]{1,0:T(1,128)S(1)}, u32[]{:S(2)}, u32[]{:S(2)}) %collective-permute-start.5) | collective-permute-done | bytes 16416 | tf_op jit(solution)/shard_map/ppermute | solution.py:21
  99.5 0.0 copy-done.1
  99.5 0.4 fusion.15
  99.9 1.3 %collective-permute-start.6 = (f32[1,4096]{1,0:T(1,128)S(1)}, f32[1,4096]{1,0:T(1,128)S(1)}, u32[]{:S(2)}, u32[]{:S(2)}) collective-permute-start(f32[1,4096]{1,0:T(1,128)S(1)} %get-tuple-element.19), channel_id=1, source_target_pairs={{8,0},{16,8},{24,16},{9,1},{17,9},{25,17},{10,2},{18,10},{26,18},{... | collective-permute-start | bytes 49160 | tf_op jit(solution)/shard_map/ppermute | solution.py:22
  101.2 4.9 %collective-permute-start.7 = (f32[1,4096]{1,0:T(1,128)S(1)}, f32[1,4096]{1,0:T(1,128)S(1)}, u32[]{:S(2)}, u32[]{:S(2)}) collective-permute-start(f32[1,4096]{1,0:T(1,128)S(1)} %get-tuple-element.20), channel_id=1, source_target_pairs={{0,8},{8,16},{16,24},{1,9},{9,17},{17,25},{2,10},{10,18},{18,26},{... | collective-permute-start | bytes 49160 | tf_op jit(solution)/shard_map/ppermute | solution.py:21
  106.1 0.0 collective-permute-done.6
  106.1 1.4 %collective-permute-done.7 = f32[1,4096]{1,0:T(1,128)S(1)} collective-permute-done((f32[1,4096]{1,0:T(1,128)S(1)}, f32[1,4096]{1,0:T(1,128)S(1)}, u32[]{:S(2)}, u32[]{:S(2)}) %collective-permute-start.7) | collective-permute-done | bytes 16416 | tf_op jit(solution)/shard_map/ppermute | solution.py:21
  107.5 0.3 fusion.10
  107.9 1.3 %collective-permute-start.8 = (f32[1,4096]{1,0:T(1,128)S(1)}, f32[1,4096]{1,0:T(1,128)S(1)}, u32[]{:S(2)}, u32[]{:S(2)}) collective-permute-start(f32[1,4096]{1,0:T(1,128)S(1)} %get-tuple-element.18), channel_id=1, source_target_pairs={{8,0},{16,8},{24,16},{9,1},{17,9},{25,17},{10,2},{18,10},{26,18},{... | collective-permute-start | bytes 49160 | tf_op jit(solution)/shard_map/ppermute | solution.py:22
  109.2 5.9 %collective-permute-start.9 = (f32[1,4096]{1,0:T(1,128)S(1)}, f32[1,4096]{1,0:T(1,128)S(1)}, u32[]{:S(2)}, u32[]{:S(2)}) collective-permute-start(f32[1,4096]{1,0:T(1,128)S(1)} %get-tuple-element.17), channel_id=1, source_target_pairs={{0,8},{8,16},{16,24},{1,9},{9,17},{17,25},{2,10},{10,18},{18,26},{... | collective-permute-start | bytes 49160 | tf_op jit(solution)/shard_map/ppermute | solution.py:21
  115.1 0.3 pad_slice_fusion.9
  115.4 0.0 collective-permute-done.8
  115.4 1.1 collective-permute-done.9
  116.5 0.7 fusion.24
  (6 shorter events, 0.2 us)
Async XLA Ops:
  7.2 83.8 %all-reduce.7.cloned.1.call-start = ((), (), s32[]{:S(2)}) async-start(), calls=%async_computation | async-start | bytes 1048576 | tf_op jit(solution)/shard_map/psum | solution.py:77
  10.6 6.9 %collective-permute-start = (f32[2,1,4096]{2,1,0:T(1,128)S(1)}, f32[2,1,4096]{2,1,0:T(1,128)S(1)}, u32[]{:S(2)}, u32[]{:S(2)}) collective-permute-start(f32[2,1,4096]{2,1,0:T(1,128)S(1)} %get-tuple-element.10), channel_id=1, source_target_pairs={{8,0},{16,8},{24,16},{9,1},{17,9},{25,17},{10,2},{18,10},{26,18},{... | collective-permute-start | bytes 98312 | tf_op jit(solution)/shard_map/ppermute | solution.py:22
  11.9 7.1 %collective-permute-start.1 = (f32[2,1,4096]{2,1,0:T(1,128)S(1)}, f32[2,1,4096]{2,1,0:T(1,128)S(1)}, u32[]{:S(2)}, u32[]{:S(2)}) collective-permute-start(f32[2,1,4096]{2,1,0:T(1,128)S(1)} %get-tuple-element.11), channel_id=1, source_target_pairs={{0,8},{8,16},{16,24},{1,9},{9,17},{17,25},{2,10},{10,18},{18,26},{... | collective-permute-start | bytes 98312 | tf_op jit(solution)/shard_map/ppermute | solution.py:21
  17.5 2.2 %copy-start.2 = (f32[32,4096]{1,0:T(8,128)S(1)}, f32[32,4096]{1,0:T(8,128)}, u32[]{:S(2)}) copy-start(f32[32,4096]{1,0:T(8,128)} %param.6) | copy-start | bytes 1572868
  17.5 2.2 %copy-start.3 = (f32[32,4096]{1,0:T(8,128)S(1)}, f32[32,4096]{1,0:T(8,128)}, u32[]{:S(2)}) copy-start(f32[32,4096]{1,0:T(8,128)} %param.7) | copy-start | bytes 1572868
  20.1 6.8 %collective-permute-start.2 = (f32[2,1,4096]{2,1,0:T(1,128)S(1)}, f32[2,1,4096]{2,1,0:T(1,128)S(1)}, u32[]{:S(2)}, u32[]{:S(2)}) collective-permute-start(f32[2,1,4096]{2,1,0:T(1,128)S(1)} %get-tuple-element.8), channel_id=1, source_target_pairs={{8,0},{16,8},{24,16},{9,1},{17,9},{25,17},{10,2},{18,10},{26,18},{... | collective-permute-start | bytes 98312 | tf_op jit(solution)/shard_map/ppermute | solution.py:22
  21.4 7.0 %collective-permute-start.3 = (f32[2,1,4096]{2,1,0:T(1,128)S(1)}, f32[2,1,4096]{2,1,0:T(1,128)S(1)}, u32[]{:S(2)}, u32[]{:S(2)}) collective-permute-start(f32[2,1,4096]{2,1,0:T(1,128)S(1)} %get-tuple-element.9), channel_id=1, source_target_pairs={{0,8},{8,16},{16,24},{1,9},{9,17},{17,25},{2,10},{10,18},{18,26},{... | collective-permute-start | bytes 98312 | tf_op jit(solution)/shard_map/ppermute | solution.py:21
  29.1 61.9 %copy-start = (f32[32,4096]{1,0:T(8,128)S(1)}, f32[32,4096]{1,0:T(8,128)}, u32[]{:S(2)}) copy-start(f32[32,4096]{1,0:T(8,128)} %param.8) | copy-start | bytes 1572868
  90.9 8.5 %copy-start.1 = (f32[32,4096]{1,0:T(8,128)S(1)}, f32[32,4096]{1,0:T(8,128)}, u32[]{:S(2)}) copy-start(f32[32,4096]{1,0:T(8,128)} %all-reduce.7.cloned.1.call-done) | copy-start | bytes 1572868
  92.2 5.9 %collective-permute-start.4 = (f32[1,4096]{1,0:T(1,128)S(1)}, f32[1,4096]{1,0:T(1,128)S(1)}, u32[]{:S(2)}, u32[]{:S(2)}) collective-permute-start(f32[1,4096]{1,0:T(1,128)S(1)} %get-tuple-element.21), channel_id=1, source_target_pairs={{8,0},{16,8},{24,16},{9,1},{17,9},{25,17},{10,2},{18,10},{26,18},{... | collective-permute-start | bytes 49160 | tf_op jit(solution)/shard_map/ppermute | solution.py:22
  93.5 6.0 %collective-permute-start.5 = (f32[1,4096]{1,0:T(1,128)S(1)}, f32[1,4096]{1,0:T(1,128)S(1)}, u32[]{:S(2)}, u32[]{:S(2)}) collective-permute-start(f32[1,4096]{1,0:T(1,128)S(1)} %get-tuple-element.22), channel_id=1, source_target_pairs={{0,8},{8,16},{16,24},{1,9},{9,17},{17,25},{2,10},{10,18},{18,26},{... | collective-permute-start | bytes 49160 | tf_op jit(solution)/shard_map/ppermute | solution.py:21
  99.9 6.2 %collective-permute-start.6 = (f32[1,4096]{1,0:T(1,128)S(1)}, f32[1,4096]{1,0:T(1,128)S(1)}, u32[]{:S(2)}, u32[]{:S(2)}) collective-permute-start(f32[1,4096]{1,0:T(1,128)S(1)} %get-tuple-element.19), channel_id=1, source_target_pairs={{8,0},{16,8},{24,16},{9,1},{17,9},{25,17},{10,2},{18,10},{26,18},{... | collective-permute-start | bytes 49160 | tf_op jit(solution)/shard_map/ppermute | solution.py:22
  101.2 6.3 %collective-permute-start.7 = (f32[1,4096]{1,0:T(1,128)S(1)}, f32[1,4096]{1,0:T(1,128)S(1)}, u32[]{:S(2)}, u32[]{:S(2)}) collective-permute-start(f32[1,4096]{1,0:T(1,128)S(1)} %get-tuple-element.20), channel_id=1, source_target_pairs={{0,8},{8,16},{16,24},{1,9},{9,17},{17,25},{2,10},{10,18},{18,26},{... | collective-permute-start | bytes 49160 | tf_op jit(solution)/shard_map/ppermute | solution.py:21
  107.9 7.5 %collective-permute-start.8 = (f32[1,4096]{1,0:T(1,128)S(1)}, f32[1,4096]{1,0:T(1,128)S(1)}, u32[]{:S(2)}, u32[]{:S(2)}) collective-permute-start(f32[1,4096]{1,0:T(1,128)S(1)} %get-tuple-element.18), channel_id=1, source_target_pairs={{8,0},{16,8},{24,16},{9,1},{17,9},{25,17},{10,2},{18,10},{26,18},{... | collective-permute-start | bytes 49160 | tf_op jit(solution)/shard_map/ppermute | solution.py:22
  109.2 7.3 %collective-permute-start.9 = (f32[1,4096]{1,0:T(1,128)S(1)}, f32[1,4096]{1,0:T(1,128)S(1)}, u32[]{:S(2)}, u32[]{:S(2)}) collective-permute-start(f32[1,4096]{1,0:T(1,128)S(1)} %get-tuple-element.17), channel_id=1, source_target_pairs={{0,8},{8,16},{16,24},{1,9},{9,17},{17,25},{2,10},{10,18},{18,26},{... | collective-permute-start | bytes 49160 | tf_op jit(solution)/shard_map/ppermute | solution.py:21
Sparse Core Ops, SparseCore 0:
  30.4 60.4 all-reduce.6
where the time goes:
time: 126 us; the launch traced here: 124 us
  waiting for transfers between devices  67.5 us (54%)
  starting transfers between devices  32.8 us (26%)
  between operations  16.2 us (13%)
  other arithmetic  7.17 us (6%)
    psum x1, waiting for transfers between devices, on_device(): entire_dissipation_map = lax.psum(local_loss, 'harm') / harmonics  60.6 us
    ppermute x5, starting transfers between devices, padded(): before = lax.ppermute(last, axis, up)  26.3 us
    ppermute x5, waiting for transfers between devices, padded(): before = lax.ppermute(last, axis, up)  6.86 us
    ppermute x5, starting transfers between devices, padded(): after = lax.ppermute(initial, axis, down)  6.46 us
  transfers between devices with their start and end apart: 11, of which 6 were waited for; matrix products, arithmetic and copies ran while one was open for 0% of the time, Pallas kernels for 0%

commit v1 on v0

v1 whole, which is shorter than its diff:
```python
import functools

import jax
import jax.numpy as jnp
from jax import lax
from jax.experimental import pallas as pl
from jax.experimental.pallas import tpu as pltpu
from jax.sharding import PartitionSpec as P

LANES = 128
HALF = 64
TILE = 8
BASE_FREQ = 0.1
MARGIN = 5
F32 = jnp.float32


def lane_iota(rows=TILE):
    return lax.broadcasted_iota(jnp.int32, (rows, LANES), 1)


def sublane_iota():
    return lax.broadcasted_iota(jnp.int32, (TILE, LANES), 0)


def side_tile(buf, rows, left, right):
    lanes = lane_iota(rows.size if hasattr(rows, "size") else rows.stop - rows.start)
    after = buf[rows, pl.ds(pl.multiple_of(right, LANES), LANES)]
    before = buf[rows, pl.ds(pl.multiple_of(left, LANES), LANES)]
    return jnp.where(lanes < HALF, after, before)


def window(start, size, total):
    begin = jnp.clip(start - LANES, 0, total - size)
    return pl.multiple_of(begin, LANES)


def pack_kernel(order, amp, count, cur, con, coo, own, other, params, buf, sems, *, width):
    slab, total = cur.shape
    h = lax.axis_index("harm")
    core = lax.rem(h, 2)
    size = buf.shape[2]
    first = (h - core) * width
    begin = window(first, size, total)
    row = pl.multiple_of(jnp.where(core == 0, slab - TILE, 0), TILE)
    copies = [
        pltpu.make_async_copy(
            ref.at[pl.ds(row, TILE), pl.ds(begin, size)], buf.at[i], sems.at[i]
        )
        for i, ref in enumerate((cur, con, coo))
    ]
    for copy in copies:
        copy.start()
    rows = lax.broadcasted_iota(jnp.int32, params.shape, 0)
    lanes = lax.broadcasted_iota(jnp.int32, params.shape, 1)
    value = jnp.where(
        lanes == 0, order[0], jnp.where(lanes == 1, amp[0], count[0])
    ).astype(F32)
    params[...] = jnp.where((rows == h) & (lanes < 3), value, 0.0)
    for copy in copies:
        copy.wait()
    sub = sublane_iota()
    goes_up = core == 0
    shift = jnp.where(goes_up, 3, 5)
    take_cur = jnp.where(goes_up, sub - 3, 4 - sub) >= 0
    for target, out in ((core, own), (1 - core, other)):
        offset = first + target * width - begin
        left = jnp.maximum(offset - LANES, 0)
        right = jnp.minimum(offset + width, size - LANES)
        pieces = []
        for j in range(width // LANES):
            at = pl.ds(pl.multiple_of(offset + j * LANES, LANES), LANES)
            pieces.append([buf[i, :, at] for i in range(3)])
        pieces.append(
            [side_tile(buf.at[i], slice(0, TILE), left, right) for i in range(3)]
        )
        for j, (a, b, c) in enumerate(pieces):
            at = slice(j * LANES, (j + 1) * LANES)
            out[:TILE, at] = jnp.where(take_cur, a, pltpu.roll(c, shift, 0))
            out[TILE:, at] = b


def gather_kernel(cur, con, coo, cur_out, con_out, coo_out, buf, sems, *, width):
    slab, total = cur.shape
    h = lax.axis_index("harm")
    size = buf.shape[2]
    begin = window(h * width, size, total)
    copies = [
        pltpu.make_async_copy(ref.at[:, pl.ds(begin, size)], buf.at[i], sems.at[i])
        for i, ref in enumerate((cur, con, coo))
    ]
    for copy in copies:
        copy.start()
    offset = h * width - begin
    left = jnp.maximum(offset - LANES, 0)
    right = jnp.minimum(offset + width, size - LANES)
    for i, out in enumerate((cur_out, con_out, coo_out)):
        copies[i].wait()
        out[:, :width] = buf[i, :, pl.ds(pl.multiple_of(offset, LANES), width)]
        out[:, width:] = side_tile(buf.at[i], slice(0, slab), left, right)


def sides(tiles, lanes):
    n = len(tiles)
    back = [pltpu.roll(t, 1, 1) for t in tiles]
    fore = [pltpu.roll(t, LANES - 1, 1) for t in tiles]
    return [
        jnp.where(lanes == 0, back[j - 1], back[j])
        + jnp.where(lanes == LANES - 1, fore[(j + 1) % n], fore[j])
        for j in range(n)
    ]


def fold_harmonics(rows, sub):
    level = list(rows)
    for half in (4, 2, 1):
        low = (sub & half) == 0
        merged = []
        for i in range(half):
            a, b = level[i], level[i + half]
            if a is None and b is None:
                merged.append(None)
                continue
            a = jnp.zeros((TILE, LANES), F32) if a is None else a
            b = jnp.zeros((TILE, LANES), F32) if b is None else b
            keep = jnp.where(low, a, b)
            move = jnp.where(low, b, a)
            merged.append(keep + jnp.where(low, pltpu.roll(move, TILE - half, 0), pltpu.roll(move, half, 0)))
        level = merged
    return level[0]


def loss_kernel(
    p0, p1, cur, con, coo, near, far, diss, heat,
    xcur, xcon, xcoo, rr, gg, ss, ra, ha, rb, hb, qq, *, width, harmonics,
):
    slab = cur.shape[0]
    nt = width // LANES + 1
    top, bottom = TILE, TILE + slab
    ext = slab + 2 * TILE
    h = lax.axis_index("harm")
    m = lax.axis_index("mesh")
    last_h = lax.axis_size("harm") - 1
    last_m = lax.axis_size("mesh") - 1
    core = lax.rem(h, 2)
    lanes, sub = lane_iota(), sublane_iota()
    xcur[top:bottom, :] = cur[...]
    xcon[top:bottom, :] = con[...]
    xcoo[top:bottom, :] = coo[...]

    def edges(up, down):
        xcur[0:TILE, :] = up[:TILE, :]
        xcon[0:TILE, :] = up[TILE:, :]
        xcoo[0:TILE, :] = pltpu.roll(up[:TILE, :], TILE - 3, 0)
        xcur[bottom:ext, :] = down[:TILE, :]
        xcon[bottom:ext, :] = down[TILE:, :]
        xcoo[bottom:ext, :] = pltpu.roll(down[:TILE, :], TILE - 5, 0)

    @pl.when(core == 0)
    def _():
        edges(near, far)

    @pl.when(core == 1)
    def _():
        edges(far, near)

    has_up = (m > 0).astype(F32)
    has_down = (m < last_m).astype(F32)
    has_left = (h > 0).astype(F32)
    has_right = (h < last_h).astype(F32)
    col_tile = (h * (width // LANES)).astype(F32)
    zero = jnp.zeros((TILE, LANES), F32)

    for group in range((harmonics + TILE - 1) // TILE):
        at = slice(group * TILE, (group + 1) * TILE)
        par = jnp.maximum(p0[at, :], p1[at, :])
        order = jnp.broadcast_to(par[:, 0:1], (TILE, LANES))
        amp = jnp.broadcast_to(par[:, 1:2], (TILE, LANES))
        count = jnp.broadcast_to(par[:, 2:3], (TILE, LANES))
        omega = BASE_FREQ * order
        quarter = 0.25 * omega
        weight = (0.5 / harmonics) * omega * amp * amp
        masks = [
            jnp.where(count > col_tile + j, 0.25, 0.0) for j in range(nt - 1)
        ]
        masks.append(
            jnp.where(
                lanes < HALF,
                jnp.where(count > col_tile + (nt - 1), 0.25 * has_right, 0.0),
                jnp.where(count > col_tile - 1, 0.25 * has_left, 0.0),
            )
        )

        def start_rows(base, subs, scale):
            scaled = masks if scale is None else [k * scale for k in masks]
            for j in range(nt):
                col = slice(j * LANES, (j + 1) * LANES)
                a = xcur[pl.ds(base, TILE), col]
                b = xcon[pl.ds(base, TILE), col]
                for s in subs:
                    src = jnp.broadcast_to(a[s : s + 1, :], (TILE, LANES))
                    g = quarter * jnp.broadcast_to(b[s : s + 1, :], (TILE, LANES))
                    d = 1.0 + g * g
                    r = pl.reciprocal(d, approx=True)
                    r = r * (2.0 - d * r)
                    r = r * scaled[j]
                    re = src * r
                    rr[base + s, :, col] = r
                    gg[base + s, :, col] = g
                    ss[base + s, :, col] = src
                    ra[base + s, :, col] = re
                    ha[base + s, :, col] = g * re

        start_rows(0, range(TILE - MARGIN, TILE), has_up)
        start_rows(bottom, range(MARGIN), has_down)

        def start_body(i, carry):
            start_rows(pl.multiple_of(top + i * TILE, TILE), range(TILE), None)
            return carry

        lax.fori_loop(0, slab // TILE, start_body, 0)

        def load(ref, row):
            return [ref[row, :, j * LANES : (j + 1) * LANES] for j in range(nt)]

        def near_sum(ref, row):
            mid = sides(load(ref, row), lanes)
            return [
                x + (u + v)
                for x, u, v in zip(mid, load(ref, row - 1), load(ref, row + 1))
            ]

        def sweep_rows(base, subs):
            for s in subs:
                row = base + s
                nr, nh = near_sum(ra, row), near_sum(ha, row)
                r, g, src = load(rr, row), load(gg, row), load(ss, row)
                for j in range(nt):
                    col = slice(j * LANES, (j + 1) * LANES)
                    x = src[j] + nr[j]
                    rb[row, :, col] = r[j] * (x - g[j] * nh[j])
                    hb[row, :, col] = r[j] * (g[j] * x + nh[j])

        def sweep_body(i, carry):
            sweep_rows(TILE - MARGIN + 1 + i * TILE, range(TILE))
            return carry

        lax.fori_loop(0, (slab + 2 * (MARGIN - 1)) // TILE, sweep_body, 0)

        def loss_rows(base, subs):
            rows = [[None] * TILE for _ in range(nt)]
            for s in subs:
                row = base + s
                nr, nh = near_sum(rb, row), near_sum(hb, row)
                r, g, src = load(rr, row), load(gg, row), load(ss, row)
                for j in range(nt):
                    x = src[j] + nr[j]
                    rows[j][s] = (weight * g[j] * r[j]) * (x * x + nh[j] * nh[j])
            for j in range(nt):
                col = slice(j * LANES, (j + 1) * LANES)
                total = fold_harmonics(rows[j], sub)
                if group:
                    total = qq[pl.ds(base, TILE), col] + total
                qq[pl.ds(base, TILE), col] = total

        loss_rows(0, range(TILE - MARGIN + 2, TILE))
        loss_rows(bottom, range(MARGIN - 2))

        def loss_body(i, carry):
            loss_rows(pl.multiple_of(top + i * TILE, TILE), range(TILE))
            return carry

        lax.fori_loop(0, slab // TILE, loss_body, 0)

    ntile = ext // TILE
    side = jnp.where(lanes < HALF, has_right, has_left)
    q = [[qq[i * TILE : (i + 1) * TILE, j * LANES : (j + 1) * LANES] for j in range(nt)] for i in range(ntile)]
    rec = []
    for i in range(ntile):
        line = []
        for j in range(nt):
            w = 1.0 / (4.0 + xcoo[i * TILE : (i + 1) * TILE, j * LANES : (j + 1) * LANES])
            if i == 0:
                w = w * has_up
            if i == ntile - 1:
                w = w * has_down
            if j == nt - 1:
                w = w * side
            line.append(w)
        rec.append(line)
    t = [[q[i][j] * rec[i][j] for j in range(nt)] for i in range(ntile)]
    for _ in range(3):
        back = [[pltpu.roll(x, 1, 0) for x in line] for line in t]
        fore = [[pltpu.roll(x, TILE - 1, 0) for x in line] for line in t]
        new = []
        for i in range(ntile):
            mid = sides(t[i], lanes)
            line = []
            for j in range(nt):
                above = jnp.where(sub == 0, back[i - 1][j], back[i][j])
                below = jnp.where(sub == TILE - 1, fore[(i + 1) % ntile][j], fore[i][j])
                line.append((q[i][j] + (mid[j] + (above + below))) * rec[i][j])
            new.append(line)
        t = new
    for i in range(1, ntile - 1):
        for j in range(nt - 1):
            at = (slice((i - 1) * TILE, i * TILE), slice(j * LANES, (j + 1) * LANES))
            diss[at] = q[i][j]
            heat[at] = t[i][j]


def on_device(current_pattern, conductivity, cooling, harm_order, harm_amp, block_counts):
    slab, total = current_pattern.shape
    harm, mesh = lax.axis_size("harm"), lax.axis_size("mesh")
    width = total // harm
    wide = width + LANES
    chips = harm // 2
    held = -(-harm // TILE) * TILE
    any_space = pl.BlockSpec(memory_space=pl.ANY)
    vmem = pl.BlockSpec(memory_space=pltpu.VMEM)
    smem = pl.BlockSpec(memory_space=pltpu.SMEM)
    shape = lambda *s: jax.ShapeDtypeStruct(s, F32)
    fields = (current_pattern, conductivity, cooling)

    own, other, params = pl.pallas_call(
        functools.partial(pack_kernel, width=width),
        out_shape=(shape(2 * TILE, wide), shape(2 * TILE, wide), shape(held, LANES)),
        in_specs=[smem] * 3 + [any_space] * 3,
        out_specs=(vmem,) * 3,
        scratch_shapes=[
            pltpu.VMEM((3, TILE, min(2 * width + 2 * LANES, total)), F32),
            pltpu.SemaphoreType.DMA((3,)),
        ],
        name="pack",
    )(harm_order, harm_amp, block_counts, *fields)

    axes = ("mesh", "harm")

    def permute(value, target):
        pairs = []
        for m in range(mesh):
            for z in range(chips):
                for c in range(2):
                    tm, tz, tc = target(m, z, c)
                    pairs.append(
                        (m * harm + z * 2 + c, (tm % mesh) * harm + (tz % chips) * 2 + tc)
                    )
        return lax.ppermute(value, axes, pairs)

    def swap(value):
        return permute(value, lambda m, z, c: (m, z, 1 - c))

    def beside(m, z, c):
        return m + (1 - 2 * c), z, c

    got = permute(own, beside)
    pass_on = permute(other, beside)
    params = jnp.maximum(params, swap(params))
    steps = list(range(1, chips))
    if len(steps) % 2:
        steps.append(1)
    power = chips & (chips - 1) == 0
    known = params
    for a, b in zip(steps[::2], steps[1::2]):
        def hop(m, z, c, a=a, b=b):
            k = (a, b)[c]
            return m, (z ^ k if power else z + k), c
        known = jnp.maximum(known, permute(params, hop))
    known_too = swap(known)
    passed = swap(pass_on)

    tile_cur, tile_con, tile_coo = pl.pallas_call(
        functools.partial(gather_kernel, width=width),
        out_shape=(shape(slab, wide),) * 3,
        in_specs=[any_space] * 3,
        out_specs=(vmem,) * 3,
        scratch_shapes=[
            pltpu.VMEM((3, slab, min(width + 2 * LANES, total)), F32),
            pltpu.SemaphoreType.DMA((3,)),
        ],
        name="gather",
    )(*fields)

    ext = slab + 2 * TILE
    flat = pltpu.VMEM((ext, wide), F32)
    deep = pltpu.VMEM((ext, TILE, wide), F32)
    return pl.pallas_call(
        functools.partial(loss_kernel, width=width, harmonics=harm),
        out_shape=(shape(slab, width),) * 2,
        in_specs=[vmem] * 7,
        out_specs=(vmem,) * 2,
        scratch_shapes=[flat] * 3 + [deep] * 7 + [flat],
        compiler_params=pltpu.CompilerParams(vmem_limit_bytes=24 * 2**20),
        name="losses",
    )(known, known_too, tile_cur, tile_con, tile_coo, got, passed)


def solution(mesh):
    return jax.shard_map(
        on_device,
        mesh=mesh,
        in_specs=(P("mesh", None),) * 3 + (P("harm"),) * 3,
        out_specs=(P("mesh", "harm"), P("mesh", "harm")),
        check_vma=False,
    )
```

time: 126 us -> 25.3 us (0.20); the launches traced: 124 us -> 24.8 us
  waiting for transfers between devices: 67.5 us -> 3.32 us
  starting transfers between devices: 32.8 us -> 8.43 us
  between operations: 16.2 us -> 2.62 us
  Pallas kernels: 0 us -> 7.13 us
  other arithmetic: 7.17 us -> 0.68 us
  local copies, waits for them, and re-layouts: 0.44 us -> 2.65 us
    psum x1 -> x0, waiting for transfers between devices: 60.6 us -> none  [on_device(): entire_dissipation_map = lax.psum(local_loss, 'harm') / harmonics]
    ppermute x10 -> x7, starting transfers between devices: 32.7 us -> 8.43 us  [permute(): return lax.ppermute(value, axes, pairs)]
    pallas_call x0 -> x3, Pallas kernels: none -> 7.13 us  [the longest x1 3.88 us: on_device(): pl.pallas_call(functools.partial(loss_kernel, width=width, harmonics=harm...]
    ppermute x10 -> x7, waiting for transfers between devices: 6.87 us -> 3.32 us  [permute(): return lax.ppermute(value, axes, pairs)]
    mul x4 -> x0, other arithmetic: 2.65 us -> none  [the longest x3 1.44 us: on_device(): thermal_increase = (entire_dissipation_map + nearby_nodes) * inverted_weight]
    unnamed x8 -> x6, local copies, waits for them, and re-layouts: 0.02 us -> 2.65 us
    another operation x6 -> x0, other arithmetic: 1.95 us -> none  [the longest x3 1.52 us: eddy_loss(): potential = jnp.stack([source * inv_re, source * inv_im])]
    add x2 -> x0, other arithmetic: 1.35 us -> none  [eddy_loss(): extended_subdomain[:, 2:, :] + extended_subdomain[:, :-2, :]]
  transfers between devices with their start and end apart: 11 -> 7, of which waited for: 6 -> 3; matrix products, arithmetic and copies ran while one was open for 0% -> 3% of each run, Pallas kernels for 0% -> 7%
where the time goes in v1:
time: 25.3 us; the launch traced here: 24.8 us
  starting transfers between devices  8.43 us (33%)
  Pallas kernels  7.13 us (28%)
  waiting for transfers between devices  3.32 us (13%)
  local copies, waits for them, and re-layouts  2.65 us (10%)
  between operations  2.62 us (10%)
  other arithmetic  0.68 us (3%)
    ppermute x7, starting transfers between devices, permute(): return lax.ppermute(value, axes, pairs)  8.43 us
    pallas_call x1, Pallas kernels, on_device(): pl.pallas_call(functools.partial(loss_kernel, width=width, harmonics=harm...  3.88 us
    ppermute x7, waiting for transfers between devices, permute(): return lax.ppermute(value, axes, pairs)  3.32 us
    unnamed x6, local copies, waits for them, and re-layouts  2.65 us
    pallas_call x1, Pallas kernels, on_device(): pl.pallas_call(functools.partial(gather_kernel, width=width), out_shape=(...  1.73 us
    pallas_call x1, Pallas kernels, on_device(): pl.pallas_call(functools.partial(pack_kernel, width=width), out_shape=(sh...  1.51 us
    max x1, other arithmetic, on_device(): params = jnp.maximum(params, swap(params))  0.68 us
  transfers between devices with their start and end apart: 7, of which 3 were waited for; matrix products, arithmetic and copies ran while one was open for 3% of the time, Pallas kernels for 7%

profile of v1, /device:TPU:0, one launch (start us, length us, event | category | flops | bytes accessed | tf_op | source)
XLA Modules:
  0.0 24.8 jit_solution(18151007070062634881)
XLA Ops:
  2.6 1.5 %pack.1 = (f32[16,640]{1,0:T(8,128)}, f32[16,640]{1,0:T(8,128)}, f32[8,128]{1,0:T(8,128)}) custom-call(s32[1]{0:T(128)S(6)} %copy.8.order, s32[1]{0:T(128)S(6)} %copy.9.amp, s32[1]{0:T(128)S(6)} %copy.10.count, f32[32,4096]{1,0:T(8,128)} %cur.3, f32[32,4096]{1,0:T(8,128)} %con.3, f32[32,4096]{1,0:T(8,128)} %coo.3), custom_call_target="tpu_custom_call" | custom-call | tf_op jit(solution)/shard_map/pack/pallas_call | solution.py:325
  4.1 3.0 %collective-permute-start.5 = (f32[16,640]{1,0:T(8,128)}, f32[16,640]{1,0:T(8,128)S(1)}, u32[]{:S(2)}, u32[]{:S(2)}) collective-permute-start(f32[16,640]{1,0:T(8,128)} %get-tuple-element.13), channel_id=1, source_target_pairs={{0,8},{1,25},{2,10},{3,27},{4,12},{5,29},{6,14},{7,31},{8,16},{9,1... | collective-permute-start | bytes 122888 | tf_op jit(solution)/shard_map/ppermute | solution.py:348
  7.1 0.5 %collective-permute-start = (f32[8,128]{1,0:T(8,128)}, f32[8,128]{1,0:T(8,128)S(1)}, u32[]{:S(2)}, u32[]{:S(2)}) collective-permute-start(f32[8,128]{1,0:T(8,128)} %get-tuple-element.8), channel_id=1, source_target_pairs={{0,1},{1,0},{2,3},{3,2},{4,5},{5,4},{6,7},{7,6},{8,9},{9,8},{10,11... | collective-permute-start | bytes 12296 | tf_op jit(solution)/shard_map/ppermute | solution.py:348
  7.6 1.0 %collective-permute-done = f32[8,128]{1,0:T(8,128)S(1)} collective-permute-done((f32[8,128]{1,0:T(8,128)}, f32[8,128]{1,0:T(8,128)S(1)}, u32[]{:S(2)}, u32[]{:S(2)}) %collective-permute-start) | collective-permute-done | bytes 4128 | tf_op jit(solution)/shard_map/ppermute | solution.py:348
  8.6 0.7 %max.9 = f32[8,128]{1,0:T(8,128)S(1)} maximum(f32[8,128]{1,0:T(8,128)} %get-tuple-element.8, f32[8,128]{1,0:T(8,128)S(1)} %collective-permute-done) | non-fusion elementwise | flops 1024 | bytes 12288 | tf_op jit(solution)/shard_map/max | solution.py:358
  9.3 3.6 %collective-permute-start.2 = (f32[8,128]{1,0:T(8,128)S(1)}, f32[8,128]{1,0:T(8,128)S(1)}, u32[]{:S(2)}, u32[]{:S(2)}) collective-permute-start(f32[8,128]{1,0:T(8,128)S(1)} %max.9), channel_id=1, source_target_pairs={{0,6},{1,3},{2,4},{3,1},{4,2},{5,7},{6,0},{7,5},{8,14},{9,11},{10,... | collective-permute-start | bytes 12296 | tf_op jit(solution)/shard_map/ppermute | solution.py:348
  12.9 0.0 collective-permute-start.1
  12.9 1.3 %collective-permute-start.4 = (f32[16,640]{1,0:T(8,128)}, f32[16,640]{1,0:T(8,128)S(1)}, u32[]{:S(2)}, u32[]{:S(2)}) collective-permute-start(f32[16,640]{1,0:T(8,128)} %get-tuple-element.12), channel_id=1, source_target_pairs={{0,8},{1,25},{2,10},{3,27},{4,12},{5,29},{6,14},{7,31},{8,16},{9,1... | collective-permute-start | bytes 122888 | tf_op jit(solution)/shard_map/ppermute | solution.py:348
  14.2 0.0 collective-permute-done.5
  14.2 0.0 collective-permute-start.6
  14.2 0.5 %collective-permute-done.2 = f32[8,128]{1,0:T(8,128)S(1)} collective-permute-done((f32[8,128]{1,0:T(8,128)S(1)}, f32[8,128]{1,0:T(8,128)S(1)}, u32[]{:S(2)}, u32[]{:S(2)}) %collective-permute-start.2) | collective-permute-done | bytes 4128 | tf_op jit(solution)/shard_map/ppermute | solution.py:348
  14.7 1.8 %collective-permute-done.1 = f32[8,128]{1,0:T(8,128)S(1)} collective-permute-done((f32[8,128]{1,0:T(8,128)S(1)}, f32[8,128]{1,0:T(8,128)S(1)}, u32[]{:S(2)}, u32[]{:S(2)}) %collective-permute-start.1) | collective-permute-done | bytes 4128 | tf_op jit(solution)/shard_map/ppermute | solution.py:348
  16.5 0.0 collective-permute-start.3
  16.5 1.7 %gather.1 = (f32[32,640]{1,0:T(8,128)}, f32[32,640]{1,0:T(8,128)}, f32[32,640]{1,0:T(8,128)}) custom-call(f32[32,4096]{1,0:T(8,128)} %cur.3, f32[32,4096]{1,0:T(8,128)} %con.3, f32[32,4096]{1,0:T(8,128)} %coo.3), custom_call_target="tpu_custom_call" | custom-call | tf_op jit(solution)/shard_map/gather/pallas_call | solution.py:372
  18.3 0.0 collective-permute-done.3.p1
  18.3 0.0 collective-permute-done.4.near
  18.3 0.0 collective-permute-done.6.far
  18.3 0.0 copy-start
  18.3 0.9 %copy-done = f32[32,640]{1,0:T(8,128)S(1)} copy-done((f32[32,640]{1,0:T(8,128)S(1)}, f32[32,640]{1,0:T(8,128)}, u32[]{:S(2)}) %copy-start) | copy-done | bytes 81944
  19.2 0.0 copy-start.1
  19.2 0.9 %copy-done.1 = f32[32,640]{1,0:T(8,128)S(1)} copy-done((f32[32,640]{1,0:T(8,128)S(1)}, f32[32,640]{1,0:T(8,128)}, u32[]{:S(2)}) %copy-start.1) | copy-done | bytes 81944
  20.1 0.0 copy-start.2
  20.1 0.9 %copy-done.2 = f32[32,640]{1,0:T(8,128)S(1)} copy-done((f32[32,640]{1,0:T(8,128)S(1)}, f32[32,640]{1,0:T(8,128)}, u32[]{:S(2)}) %copy-start.2) | copy-done | bytes 81944
  21.0 3.9 %losses.1 = (f32[32,512]{1,0:T(8,128)}, f32[32,512]{1,0:T(8,128)}) custom-call(f32[8,128]{1,0:T(8,128)S(1)} %maximum_maximum_fusion.p0, f32[8,128]{1,0:T(8,128)S(1)} %collective-permute-done.3.p1, f32[32,640]{1,0:T(8,128)S(1)} %copy-done, f32[32,640]{1,0:T(8,128)S(1)} %copy-done.1, f32[32,640]{1,0:T(8,128)S(1)} %copy-done.2, ...), custom_call_target="tpu_custom_call" | custom-call | tf_op jit(solution)/shard_map/losses/pallas_call | solution.py:387
  (1 shorter events, 0.0 us)
Async XLA Ops:
  4.1 10.1 %collective-permute-start.5 = (f32[16,640]{1,0:T(8,128)}, f32[16,640]{1,0:T(8,128)S(1)}, u32[]{:S(2)}, u32[]{:S(2)}) collective-permute-start(f32[16,640]{1,0:T(8,128)} %get-tuple-element.13), channel_id=1, source_target_pairs={{0,8},{1,25},{2,10},{3,27},{4,12},{5,29},{6,14},{7,31},{8,16},{9,1... | collective-permute-start | bytes 122888 | tf_op jit(solution)/shard_map/ppermute | solution.py:348
  7.1 1.5 %collective-permute-start = (f32[8,128]{1,0:T(8,128)}, f32[8,128]{1,0:T(8,128)S(1)}, u32[]{:S(2)}, u32[]{:S(2)}) collective-permute-start(f32[8,128]{1,0:T(8,128)} %get-tuple-element.8), channel_id=1, source_target_pairs={{0,1},{1,0},{2,3},{3,2},{4,5},{5,4},{6,7},{7,6},{8,9},{9,8},{10,11... | collective-permute-start | bytes 12296 | tf_op jit(solution)/shard_map/ppermute | solution.py:348
  9.3 5.4 %collective-permute-start.2 = (f32[8,128]{1,0:T(8,128)S(1)}, f32[8,128]{1,0:T(8,128)S(1)}, u32[]{:S(2)}, u32[]{:S(2)}) collective-permute-start(f32[8,128]{1,0:T(8,128)S(1)} %max.9), channel_id=1, source_target_pairs={{0,6},{1,3},{2,4},{3,1},{4,2},{5,7},{6,0},{7,5},{8,14},{9,11},{10,... | collective-permute-start | bytes 12296 | tf_op jit(solution)/shard_map/ppermute | solution.py:348
  12.9 3.6 %collective-permute-start.1 = (f32[8,128]{1,0:T(8,128)S(1)}, f32[8,128]{1,0:T(8,128)S(1)}, u32[]{:S(2)}, u32[]{:S(2)}) collective-permute-start(f32[8,128]{1,0:T(8,128)S(1)} %max.9), channel_id=1, source_target_pairs={{0,2},{1,5},{2,0},{3,7},{4,6},{5,1},{6,4},{7,3},{8,10},{9,13},{10,... | collective-permute-start | bytes 12296 | tf_op jit(solution)/shard_map/ppermute | solution.py:348
  12.9 5.4 %collective-permute-start.4 = (f32[16,640]{1,0:T(8,128)}, f32[16,640]{1,0:T(8,128)S(1)}, u32[]{:S(2)}, u32[]{:S(2)}) collective-permute-start(f32[16,640]{1,0:T(8,128)} %get-tuple-element.12), channel_id=1, source_target_pairs={{0,8},{1,25},{2,10},{3,27},{4,12},{5,29},{6,14},{7,31},{8,16},{9,1... | collective-permute-start | bytes 122888 | tf_op jit(solution)/shard_map/ppermute | solution.py:348
  14.2 4.0 %collective-permute-start.6 = (f32[16,640]{1,0:T(8,128)S(1)}, f32[16,640]{1,0:T(8,128)S(1)}, u32[]{:S(2)}, u32[]{:S(2)}) collective-permute-start(f32[16,640]{1,0:T(8,128)S(1)} %collective-permute-done.5), channel_id=1, source_target_pairs={{0,1},{1,0},{2,3},{3,2},{4,5},{5,4},{6,7},{7,6},{8,9},{9,8},{10,11... | collective-permute-start | bytes 122888 | tf_op jit(solution)/shard_map/ppermute | solution.py:348
  16.5 1.7 %collective-permute-start.3 = (f32[8,128]{1,0:T(8,128)S(1)}, f32[8,128]{1,0:T(8,128)S(1)}, u32[]{:S(2)}, u32[]{:S(2)}) collective-permute-start(f32[8,128]{1,0:T(8,128)S(1)} %maximum_maximum_fusion.p0), channel_id=1, source_target_pairs={{0,1},{1,0},{2,3},{3,2},{4,5},{5,4},{6,7},{7,6},{8,9},{9,8},{10,11... | collective-permute-start | bytes 12296 | tf_op jit(solution)/shard_map/ppermute | solution.py:348
  18.3 0.9 %copy-start = (f32[32,640]{1,0:T(8,128)S(1)}, f32[32,640]{1,0:T(8,128)}, u32[]{:S(2)}) copy-start(f32[32,640]{1,0:T(8,128)} %get-tuple-element.9.cur) | copy-start | bytes 245764
  19.2 0.9 %copy-start.1 = (f32[32,640]{1,0:T(8,128)S(1)}, f32[32,640]{1,0:T(8,128)}, u32[]{:S(2)}) copy-start(f32[32,640]{1,0:T(8,128)} %get-tuple-element.10.con) | copy-start | bytes 245764
  20.1 0.9 %copy-start.2 = (f32[32,640]{1,0:T(8,128)S(1)}, f32[32,640]{1,0:T(8,128)}, u32[]{:S(2)}) copy-start(f32[32,640]{1,0:T(8,128)} %get-tuple-element.11.coo) | copy-start | bytes 245764

commit v2 on v1

--- a/solution.py
+++ b/solution.py
@@ -35,7 +35,17 @@
     return pl.multiple_of(begin, LANES)
 
 
-def pack_kernel(order, amp, count, cur, con, coo, own, other, params, buf, sems, *, width):
+def params_kernel(order, amp, count, params):
+    h = lax.axis_index("harm")
+    rows = lax.broadcasted_iota(jnp.int32, params.shape, 0)
+    lanes = lax.broadcasted_iota(jnp.int32, params.shape, 1)
+    value = jnp.where(
+        lanes == 0, order[0], jnp.where(lanes == 1, amp[0], count[0])
+    ).astype(F32)
+    params[...] = jnp.where((rows == h) & (lanes < 3), value, 0.0)
+
+
+def pack_kernel(after, cur, con, coo, out, cur_out, con_out, coo_out, buf, held, sems, *, width):
     slab, total = cur.shape
     h = lax.axis_index("harm")
     core = lax.rem(h, 2)
@@ -51,19 +61,23 @@
     ]
     for copy in copies:
         copy.start()
-    rows = lax.broadcasted_iota(jnp.int32, params.shape, 0)
-    lanes = lax.broadcasted_iota(jnp.int32, params.shape, 1)
-    value = jnp.where(
-        lanes == 0, order[0], jnp.where(lanes == 1, amp[0], count[0])
-    ).astype(F32)
-    params[...] = jnp.where((rows == h) & (lanes < 3), value, 0.0)
-    for copy in copies:
-        copy.wait()
+    size_own = held.shape[2]
+    begin_own = window(h * width, size_own, total)
+    own = [
+        pltpu.make_async_copy(
+            ref.at[:, pl.ds(begin_own, size_own)], held.at[i], sems.at[3 + i]
+        )
+        for i, ref in enumerate((cur, con, coo))
+    ]
+    for copy in own:
+        copy.start()
     sub = sublane_iota()
     goes_up = core == 0
     shift = jnp.where(goes_up, 3, 5)
     take_cur = jnp.where(goes_up, sub - 3, 4 - sub) >= 0
-    for target, out in ((core, own), (1 - core, other)):
+    for copy in copies:
+        copy.wait()
+    for part, target in enumerate((core, 1 - core)):
         offset = first + target * width - begin
         left = jnp.maximum(offset - LANES, 0)
         right = jnp.minimum(offset + width, size - LANES)
@@ -74,30 +88,22 @@
         pieces.append(
             [side_tile(buf.at[i], slice(0, TILE), left, right) for i in range(3)]
         )
+        base = part * 2 * TILE
         for j, (a, b, c) in enumerate(pieces):
             at = slice(j * LANES, (j + 1) * LANES)
-            out[:TILE, at] = jnp.where(take_cur, a, pltpu.roll(c, shift, 0))
-            out[TILE:, at] = b
-
-
-def gather_kernel(cur, con, coo, cur_out, con_out, coo_out, buf, sems, *, width):
-    slab, total = cur.shape
-    h = lax.axis_index("harm")
-    size = buf.shape[2]
-    begin = window(h * width, size, total)
-    copies = [
-        pltpu.make_async_copy(ref.at[:, pl.ds(begin, size)], buf.at[i], sems.at[i])
-        for i, ref in enumerate((cur, con, coo))
-    ]
-    for copy in copies:
-        copy.start()
-    offset = h * width - begin
+            out[base : base + TILE, at] = jnp.where(take_cur, a, pltpu.roll(c, shift, 0))
+            out[base + TILE : base + 2 * TILE, at] = b
+    offset = h * width - begin_own
     left = jnp.maximum(offset - LANES, 0)
-    right = jnp.minimum(offset + width, size - LANES)
-    for i, out in enumerate((cur_out, con_out, coo_out)):
-        copies[i].wait()
-        out[:, :width] = buf[i, :, pl.ds(pl.multiple_of(offset, LANES), width)]
-        out[:, width:] = side_tile(buf.at[i], slice(0, slab), left, right)
+    right = jnp.minimum(offset + width, size_own - LANES)
+    for i, tile in enumerate((cur_out, con_out, coo_out)):
+        own[i].wait()
+        tile[:, :width] = held[i, :, pl.ds(pl.multiple_of(offset, LANES), width)]
+        tile[:, width:] = side_tile(held.at[i], slice(0, slab), left, right)
+
+
+def pass_kernel(after, got, passed):
+    passed[...] = got[2 * TILE :, :]
 
 
 def sides(tiles, lanes):
@@ -131,7 +137,7 @@
 
 
 def loss_kernel(
-    p0, p1, cur, con, coo, near, far, diss, heat,
+    par_ref, cur, con, coo, near, far, diss, heat,
     xcur, xcon, xcoo, rr, gg, ss, ra, ha, rb, hb, qq, *, width, harmonics,
 ):
     slab = cur.shape[0]
@@ -150,10 +156,10 @@
 
     def edges(up, down):
         xcur[0:TILE, :] = up[:TILE, :]
-        xcon[0:TILE, :] = up[TILE:, :]
+        xcon[0:TILE, :] = up[TILE : 2 * TILE, :]
         xcoo[0:TILE, :] = pltpu.roll(up[:TILE, :], TILE - 3, 0)
         xcur[bottom:ext, :] = down[:TILE, :]
-        xcon[bottom:ext, :] = down[TILE:, :]
+        xcon[bottom:ext, :] = down[TILE : 2 * TILE, :]
         xcoo[bottom:ext, :] = pltpu.roll(down[:TILE, :], TILE - 5, 0)
 
     @pl.when(core == 0)
@@ -173,7 +179,7 @@
 
     for group in range((harmonics + TILE - 1) // TILE):
         at = slice(group * TILE, (group + 1) * TILE)
-        par = jnp.maximum(p0[at, :], p1[at, :])
+        par = par_ref[at, :]
         order = jnp.broadcast_to(par[:, 0:1], (TILE, LANES))
         amp = jnp.broadcast_to(par[:, 1:2], (TILE, LANES))
         count = jnp.broadcast_to(par[:, 2:3], (TILE, LANES))
@@ -322,17 +328,30 @@
     shape = lambda *s: jax.ShapeDtypeStruct(s, F32)
     fields = (current_pattern, conductivity, cooling)
 
-    own, other, params = pl.pallas_call(
+    small = pltpu.CompilerParams(vmem_limit_bytes=4 * 2**20)
+    in_hbm = lambda x: pltpu.with_memory_space_constraint(x, pltpu.HBM)
+    held_vmem = lambda *s: pltpu.VMEM(s, F32)
+    params = pl.pallas_call(
+        params_kernel,
+        out_shape=held_vmem(held, LANES),
+        in_specs=[smem] * 3,
+        out_specs=vmem,
+        compiler_params=small,
+        name="params",
+    )(harm_order, harm_amp, block_counts)
+    edges, tile_cur, tile_con, tile_coo = pl.pallas_call(
         functools.partial(pack_kernel, width=width),
-        out_shape=(shape(2 * TILE, wide), shape(2 * TILE, wide), shape(held, LANES)),
-        in_specs=[smem] * 3 + [any_space] * 3,
-        out_specs=(vmem,) * 3,
+        out_shape=(held_vmem(4 * TILE, wide),) + (held_vmem(slab, wide),) * 3,
+        in_specs=[any_space] * 4,
+        out_specs=(vmem,) * 4,
         scratch_shapes=[
             pltpu.VMEM((3, TILE, min(2 * width + 2 * LANES, total)), F32),
-            pltpu.SemaphoreType.DMA((3,)),
+            pltpu.VMEM((3, slab, min(width + 2 * LANES, total)), F32),
+            pltpu.SemaphoreType.DMA((6,)),
         ],
+        compiler_params=small,
         name="pack",
-    )(harm_order, harm_amp, block_counts, *fields)
+    )(params, *map(in_hbm, fields))
 
     axes = ("mesh", "harm")
 
@@ -353,33 +372,34 @@
     def beside(m, z, c):
         return m + (1 - 2 * c), z, c
 
-    got = permute(own, beside)
-    pass_on = permute(other, beside)
-    params = jnp.maximum(params, swap(params))
-    steps = list(range(1, chips))
-    if len(steps) % 2:
-        steps.append(1)
-    power = chips & (chips - 1) == 0
-    known = params
-    for a, b in zip(steps[::2], steps[1::2]):
-        def hop(m, z, c, a=a, b=b):
-            k = (a, b)[c]
-            return m, (z ^ k if power else z + k), c
-        known = jnp.maximum(known, permute(params, hop))
-    known_too = swap(known)
-    passed = swap(pass_on)
-
-    tile_cur, tile_con, tile_coo = pl.pallas_call(
-        functools.partial(gather_kernel, width=width),
-        out_shape=(shape(slab, wide),) * 3,
-        in_specs=[any_space] * 3,
-        out_specs=(vmem,) * 3,
-        scratch_shapes=[
-            pltpu.VMEM((3, slab, min(width + 2 * LANES, total)), F32),
-            pltpu.SemaphoreType.DMA((3,)),
-        ],
-        name="gather",
-    )(*fields)
+    known = jnp.maximum(params, swap(params))
+    stages = [known]
+    edges, known = lax.optimization_barrier((edges, known))
+    got = permute(edges, beside)
+    if chips & (chips - 1) == 0:
+        step = 1
+        while step < chips:
+            known = jnp.maximum(
+                known, permute(known, lambda m, z, c: (m, z ^ step, c))
+            )
+            stages.append(known)
+            step *= 2
+    else:
+        table = known
+        for step in range(1, chips):
+            known = jnp.maximum(
+                known, permute(table, lambda m, z, c: (m, z + step, c))
+            )
+            stages.append(known)
+    passed = pl.pallas_call(
+        pass_kernel,
+        out_shape=held_vmem(2 * TILE, wide),
+        in_specs=[any_space, vmem],
+        out_specs=vmem,
+        compiler_params=small,
+        name="pass_on",
+    )(stages[min(1, len(stages) - 1)], got)
+    far = swap(passed)
 
     ext = slab + 2 * TILE
     flat = pltpu.VMEM((ext, wide), F32)
@@ -387,12 +407,12 @@
     return pl.pallas_call(
         functools.partial(loss_kernel, width=width, harmonics=harm),
         out_shape=(shape(slab, width),) * 2,
-        in_specs=[vmem] * 7,
+        in_specs=[vmem] * 6,
         out_specs=(vmem,) * 2,
         scratch_shapes=[flat] * 3 + [deep] * 7 + [flat],
-        compiler_params=pltpu.CompilerParams(vmem_limit_bytes=24 * 2**20),
+        compiler_params=pltpu.CompilerParams(vmem_limit_bytes=12 * 2**20),
         name="losses",
-    )(known, known_too, tile_cur, tile_con, tile_coo, got, passed)
+    )(known, tile_cur, tile_con, tile_coo, got, far)
 
 
 def solution(mesh):

time: 25.3 us -> 19.7 us (0.78); the launches traced: 24.8 us -> 19.5 us
  local copies, waits for them, and re-layouts: 2.65 us -> 0 us
  Pallas kernels: 7.13 us -> 5.02 us
  waiting for transfers between devices: 3.32 us -> 4.47 us
  starting transfers between devices: 8.43 us -> 7.4 us
  other arithmetic: 0.68 us -> 0.01 us
    unnamed x6 -> x0, local copies, waits for them, and re-layouts: 2.65 us -> none
    pallas_call x2 -> x3, Pallas kernels: 3.25 us -> 1.14 us  [the longest x1 1.12 us: on_device(): pl.pallas_call(functools.partial(pack_kernel, width=width), out_shape=(he...]
    ppermute x7 -> x5, waiting for transfers between devices: 3.32 us -> 4.47 us  [permute(): return lax.ppermute(value, axes, pairs)]
    ppermute x7 -> x5, starting transfers between devices: 8.43 us -> 7.4 us  [permute(): return lax.ppermute(value, axes, pairs)]
    max x2 -> x3, other arithmetic: 0.68 us -> 0.01 us  [the longest x2 0.01 us: on_device(): known = jnp.maximum(known, permute(known, lambda m, z, c: (m, z ^ step, c)))]
  transfers between devices with their start and end apart: 7 -> 5, of which waited for: 3 -> 3; matrix products, arithmetic and copies ran while one was open for 3% -> 0% of each run, Pallas kernels for 7% -> 6%
where the time goes in v2:
time: 19.7 us; the launch traced here: 19.5 us
  starting transfers between devices  7.4 us (38%)
  Pallas kernels  5.02 us (25%)
  waiting for transfers between devices  4.47 us (23%)
  between operations  2.6 us (13%)
    ppermute x5, starting transfers between devices, permute(): return lax.ppermute(value, axes, pairs)  7.4 us
    ppermute x5, waiting for transfers between devices, permute(): return lax.ppermute(value, axes, pairs)  4.47 us
    pallas_call x1, Pallas kernels, on_device(): pl.pallas_call(functools.partial(loss_kernel, width=width, harmonics=harm...  3.88 us
    pallas_call x1, Pallas kernels, on_device(): pl.pallas_call(functools.partial(pack_kernel, width=width), out_shape=(he...  1.12 us
  transfers between devices with their start and end apart: 5, of which 3 were waited for; matrix products, arithmetic and copies ran while one was open for 0% of the time, Pallas kernels for 6%

profile of v2, /device:TPU:0, one launch (start us, length us, event | category | flops | bytes accessed | tf_op | source)
XLA Modules:
  0.0 19.5 jit_solution(7420428293810806092)
XLA Ops:
  2.6 0.5 %collective-permute-start = (f32[8,128]{1,0:T(8,128)S(1)}, f32[8,128]{1,0:T(8,128)S(1)}, u32[]{:S(2)}, u32[]{:S(2)}) collective-permute-start(f32[8,128]{1,0:T(8,128)S(1)} %params.1.after), channel_id=1, source_target_pairs={{0,1},{1,0},{2,3},{3,2},{4,5},{5,4},{6,7},{7,6},{8,9},{9,8},{10,11... | collective-permute-start | bytes 12296 | tf_op jit(solution)/shard_map/ppermute | solution.py:367
  3.1 1.1 %pack.1 = (f32[32,640]{1,0:T(8,128)S(1)}, f32[32,640]{1,0:T(8,128)S(1)}, f32[32,640]{1,0:T(8,128)S(1)}, f32[32,640]{1,0:T(8,128)S(1)}) custom-call(f32[8,128]{1,0:T(8,128)S(1)} %params.1.after, f32[32,4096]{1,0:T(8,128)} %cur.1, f32[32,4096]{1,0:T(8,128)} %con.1, f32[32,4096]{1,0:T(8,128)} %coo.1), custom_call_target="tpu_custom_call" | custom-call | tf_op jit(solution)/shard_map/pack/pallas_call | solution.py:342
  4.2 0.0 collective-permute-done
  4.3 2.6 %collective-permute-start.3 = (f32[32,640]{1,0:T(8,128)S(1)}, f32[32,640]{1,0:T(8,128)S(1)}, u32[]{:S(2)}, u32[]{:S(2)}) collective-permute-start(f32[32,640]{1,0:T(8,128)S(1)} %get-tuple-element.13), channel_id=1, source_target_pairs={{0,8},{1,25},{2,10},{3,27},{4,12},{5,29},{6,14},{7,31},{8,16},{9,1... | collective-permute-start | bytes 245768 | tf_op jit(solution)/shard_map/ppermute | solution.py:367
  6.8 1.6 %collective-permute-start.1 = (f32[8,128]{1,0:T(8,128)S(1)}, f32[8,128]{1,0:T(8,128)S(1)}, u32[]{:S(2)}, u32[]{:S(2)}) collective-permute-start(f32[8,128]{1,0:T(8,128)S(1)} %max.9), channel_id=1, source_target_pairs={{0,2},{1,3},{2,0},{3,1},{4,6},{5,7},{6,4},{7,5},{8,10},{9,11},{10,... | collective-permute-start | bytes 12296 | tf_op jit(solution)/shard_map/ppermute | solution.py:367
  8.4 2.0 %collective-permute-done.1 = f32[8,128]{1,0:T(8,128)S(1)} collective-permute-done((f32[8,128]{1,0:T(8,128)S(1)}, f32[8,128]{1,0:T(8,128)S(1)}, u32[]{:S(2)}, u32[]{:S(2)}) %collective-permute-start.1) | collective-permute-done | bytes 4128 | tf_op jit(solution)/shard_map/ppermute | solution.py:367
  10.4 0.6 %collective-permute-done.3.got.near = f32[32,640]{1,0:T(8,128)S(1)} collective-permute-done((f32[32,640]{1,0:T(8,128)S(1)}, f32[32,640]{1,0:T(8,128)S(1)}, u32[]{:S(2)}, u32[]{:S(2)}) %collective-permute-start.3) | collective-permute-done | bytes 81952 | tf_op jit(solution)/shard_map/ppermute | solution.py:367
  11.0 0.0 collective-permute-start.4
  11.0 2.7 %collective-permute-start.2 = (f32[8,128]{1,0:T(8,128)S(1)}, f32[8,128]{1,0:T(8,128)S(1)}, u32[]{:S(2)}, u32[]{:S(2)}) collective-permute-start(f32[8,128]{1,0:T(8,128)S(1)} %max.10.after), channel_id=1, source_target_pairs={{0,4},{1,5},{2,6},{3,7},{4,0},{5,1},{6,2},{7,3},{8,12},{9,13},{10,... | collective-permute-start | bytes 12296 | tf_op jit(solution)/shard_map/ppermute | solution.py:367
  13.8 1.8 %collective-permute-done.2 = f32[8,128]{1,0:T(8,128)S(1)} collective-permute-done((f32[8,128]{1,0:T(8,128)S(1)}, f32[8,128]{1,0:T(8,128)S(1)}, u32[]{:S(2)}, u32[]{:S(2)}) %collective-permute-start.2) | collective-permute-done | bytes 4128 | tf_op jit(solution)/shard_map/ppermute | solution.py:367
  15.6 0.0 collective-permute-done.4.far
  15.6 3.9 %losses.1 = (f32[32,512]{1,0:T(8,128)}, f32[32,512]{1,0:T(8,128)}) custom-call(f32[8,128]{1,0:T(8,128)S(1)} %max.11.par_ref, f32[32,640]{1,0:T(8,128)S(1)} %get-tuple-element.10.cur, f32[32,640]{1,0:T(8,128)S(1)} %get-tuple-element.11.con, f32[32,640]{1,0:T(8,128)S(1)} %get-tuple-element.12.coo, f32[32,640]{1,0:T(8,128)S(1)} %collective-permute-done.3.got.near, ...), custom_call_target="tpu_custom_call" | custom-call | tf_op jit(solution)/shard_map/losses/pallas_call | solution.py:407
  (5 shorter events, 0.0 us)
Async XLA Ops:
  2.6 1.7 %collective-permute-start = (f32[8,128]{1,0:T(8,128)S(1)}, f32[8,128]{1,0:T(8,128)S(1)}, u32[]{:S(2)}, u32[]{:S(2)}) collective-permute-start(f32[8,128]{1,0:T(8,128)S(1)} %params.1.after), channel_id=1, source_target_pairs={{0,1},{1,0},{2,3},{3,2},{4,5},{5,4},{6,7},{7,6},{8,9},{9,8},{10,11... | collective-permute-start | bytes 12296 | tf_op jit(solution)/shard_map/ppermute | solution.py:367
  4.3 6.8 %collective-permute-start.3 = (f32[32,640]{1,0:T(8,128)S(1)}, f32[32,640]{1,0:T(8,128)S(1)}, u32[]{:S(2)}, u32[]{:S(2)}) collective-permute-start(f32[32,640]{1,0:T(8,128)S(1)} %get-tuple-element.13), channel_id=1, source_target_pairs={{0,8},{1,25},{2,10},{3,27},{4,12},{5,29},{6,14},{7,31},{8,16},{9,1... | collective-permute-start | bytes 245768 | tf_op jit(solution)/shard_map/ppermute | solution.py:367
  6.8 3.6 %collective-permute-start.1 = (f32[8,128]{1,0:T(8,128)S(1)}, f32[8,128]{1,0:T(8,128)S(1)}, u32[]{:S(2)}, u32[]{:S(2)}) collective-permute-start(f32[8,128]{1,0:T(8,128)S(1)} %max.9), channel_id=1, source_target_pairs={{0,2},{1,3},{2,0},{3,1},{4,6},{5,7},{6,4},{7,5},{8,10},{9,11},{10,... | collective-permute-start | bytes 12296 | tf_op jit(solution)/shard_map/ppermute | solution.py:367
  11.0 4.6 %collective-permute-start.4 = (f32[16,640]{1,0:T(8,128)S(1)}, f32[16,640]{1,0:T(8,128)S(1)}, u32[]{:S(2)}, u32[]{:S(2)}) collective-permute-start(f32[16,640]{1,0:T(8,128)S(1)} %pass_on.1), channel_id=1, source_target_pairs={{0,1},{1,0},{2,3},{3,2},{4,5},{5,4},{6,7},{7,6},{8,9},{9,8},{10,11... | collective-permute-start | bytes 122888 | tf_op jit(solution)/shard_map/ppermute | solution.py:367
  11.0 4.6 %collective-permute-start.2 = (f32[8,128]{1,0:T(8,128)S(1)}, f32[8,128]{1,0:T(8,128)S(1)}, u32[]{:S(2)}, u32[]{:S(2)}) collective-permute-start(f32[8,128]{1,0:T(8,128)S(1)} %max.10.after), channel_id=1, source_target_pairs={{0,4},{1,5},{2,6},{3,7},{4,0},{5,1},{6,2},{7,3},{8,12},{9,13},{10,... | collective-permute-start | bytes 12296 | tf_op jit(solution)/shard_map/ppermute | solution.py:367

commit v3 on v2

--- a/solution.py
+++ b/solution.py
@@ -379,8 +379,9 @@
     if chips & (chips - 1) == 0:
         step = 1
         while step < chips:
+            sent = jnp.tile(known, (1, 2)) if step > 1 else known
             known = jnp.maximum(
-                known, permute(known, lambda m, z, c: (m, z ^ step, c))
+                known, permute(sent, lambda m, z, c: (m, z ^ step, c))[:, :LANES]
             )
             stages.append(known)
             step *= 2

time: 19.7 us -> 17.7 us (0.90)
  waiting for transfers between devices: 4.47 us -> 2.19 us
  starting transfers between devices: 7.4 us -> 7.71 us
    ppermute x5, waiting for transfers between devices: 4.47 us -> 2.19 us  [permute(): return lax.ppermute(value, axes, pairs)]
    ppermute x5, starting transfers between devices: 7.4 us -> 7.71 us  [permute(): return lax.ppermute(value, axes, pairs)]
  transfers between devices with their start and end apart: 5 -> 5, of which waited for: 3 -> 4; matrix products, arithmetic and copies ran while one was open for 0% -> 0% of each run, Pallas kernels for 6% -> 6%
where the time goes in v3:
time: 17.7 us; the launch traced here: 17.5 us
  starting transfers between devices  7.71 us (44%)
  Pallas kernels  5.02 us (28%)
  between operations  2.6 us (15%)
  waiting for transfers between devices  2.19 us (12%)
    ppermute x5, starting transfers between devices, permute(): return lax.ppermute(value, axes, pairs)  7.71 us
    pallas_call x1, Pallas kernels, on_device(): pl.pallas_call(functools.partial(loss_kernel, width=width, harmonics=harm...  3.88 us
    ppermute x5, waiting for transfers between devices, permute(): return lax.ppermute(value, axes, pairs)  2.19 us
    pallas_call x1, Pallas kernels, on_device(): pl.pallas_call(functools.partial(pack_kernel, width=width), out_shape=(he...  1.12 us
  transfers between devices with their start and end apart: 5, of which 4 were waited for; matrix products, arithmetic and copies ran while one was open for 0% of the time, Pallas kernels for 6%

profile of v3, /device:TPU:0, one launch (start us, length us, event | category | flops | bytes accessed | tf_op | source)
XLA Modules:
  0.0 17.5 jit_solution(11688513062461252014)
XLA Ops:
  2.6 0.5 %collective-permute-start = (f32[8,128]{1,0:T(8,128)S(1)}, f32[8,128]{1,0:T(8,128)S(1)}, u32[]{:S(2)}, u32[]{:S(2)}) collective-permute-start(f32[8,128]{1,0:T(8,128)S(1)} %params.1.after), channel_id=1, source_target_pairs={{0,1},{1,0},{2,3},{3,2},{4,5},{5,4},{6,7},{7,6},{8,9},{9,8},{10,11... | collective-permute-start | bytes 12296 | tf_op jit(solution)/shard_map/ppermute | solution.py:367
  3.1 1.1 %pack.1 = (f32[32,640]{1,0:T(8,128)S(1)}, f32[32,640]{1,0:T(8,128)S(1)}, f32[32,640]{1,0:T(8,128)S(1)}, f32[32,640]{1,0:T(8,128)S(1)}) custom-call(f32[8,128]{1,0:T(8,128)S(1)} %params.1.after, f32[32,4096]{1,0:T(8,128)} %cur.1, f32[32,4096]{1,0:T(8,128)} %con.1, f32[32,4096]{1,0:T(8,128)} %coo.1), custom_call_target="tpu_custom_call" | custom-call | tf_op jit(solution)/shard_map/pack/pallas_call | solution.py:342
  4.2 0.0 collective-permute-done
  4.3 2.7 %collective-permute-start.1 = (f32[8,128]{1,0:T(8,128)S(1)}, f32[8,128]{1,0:T(8,128)S(1)}, u32[]{:S(2)}, u32[]{:S(2)}) collective-permute-start(f32[8,128]{1,0:T(8,128)S(1)} %max.9), channel_id=1, source_target_pairs={{0,2},{1,3},{2,0},{3,1},{4,6},{5,7},{6,4},{7,5},{8,10},{9,11},{10,... | collective-permute-start | bytes 12296 | tf_op jit(solution)/shard_map/ppermute | solution.py:367
  6.9 1.5 %collective-permute-start.3 = (f32[32,640]{1,0:T(8,128)S(1)}, f32[32,640]{1,0:T(8,128)S(1)}, u32[]{:S(2)}, u32[]{:S(2)}) collective-permute-start(f32[32,640]{1,0:T(8,128)S(1)} %get-tuple-element.13), channel_id=1, source_target_pairs={{0,8},{1,25},{2,10},{3,27},{4,12},{5,29},{6,14},{7,31},{8,16},{9,1... | collective-permute-start | bytes 245768 | tf_op jit(solution)/shard_map/ppermute | solution.py:367
  8.4 0.1 collective-permute-done.1
  8.5 3.0 %collective-permute-start.2 = (f32[8,256]{1,0:T(8,128)S(1)}, f32[8,256]{1,0:T(8,128)S(1)}, u32[]{:S(2)}, u32[]{:S(2)}) collective-permute-start(f32[8,256]{1,0:T(8,128)S(1)} %broadcast_bitcast_fusion), channel_id=1, source_target_pairs={{0,4},{1,5},{2,6},{3,7},{4,0},{5,1},{6,2},{7,3},{8,12},{9,13},{10,... | collective-permute-start | bytes 24584 | tf_op jit(solution)/shard_map/ppermute | solution.py:367
  11.6 0.9 %collective-permute-done.3.got.near = f32[32,640]{1,0:T(8,128)S(1)} collective-permute-done((f32[32,640]{1,0:T(8,128)S(1)}, f32[32,640]{1,0:T(8,128)S(1)}, u32[]{:S(2)}, u32[]{:S(2)}) %collective-permute-start.3) | collective-permute-done | bytes 81952 | tf_op jit(solution)/shard_map/ppermute | solution.py:367
  12.4 0.0 collective-permute-start.4
  12.4 0.7 %collective-permute-done.2 = f32[8,256]{1,0:T(8,128)S(1)} collective-permute-done((f32[8,256]{1,0:T(8,128)S(1)}, f32[8,256]{1,0:T(8,128)S(1)}, u32[]{:S(2)}, u32[]{:S(2)}) %collective-permute-start.2) | collective-permute-done | bytes 8224 | tf_op jit(solution)/shard_map/ppermute | solution.py:367
  13.2 0.5 %collective-permute-done.4.far = f32[16,640]{1,0:T(8,128)S(1)} collective-permute-done((f32[16,640]{1,0:T(8,128)S(1)}, f32[16,640]{1,0:T(8,128)S(1)}, u32[]{:S(2)}, u32[]{:S(2)}) %collective-permute-start.4) | collective-permute-done | bytes 40992 | tf_op jit(solution)/shard_map/ppermute | solution.py:367
  13.7 3.9 %losses.1 = (f32[32,512]{1,0:T(8,128)}, f32[32,512]{1,0:T(8,128)}) custom-call(f32[8,128]{1,0:T(8,128)S(1)} %slice_maximum_fusion.par_ref, f32[32,640]{1,0:T(8,128)S(1)} %get-tuple-element.10.cur, f32[32,640]{1,0:T(8,128)S(1)} %get-tuple-element.11.con, f32[32,640]{1,0:T(8,128)S(1)} %get-tuple-element.12.coo, f32[32,640]{1,0:T(8,128)S(1)} %collective-permute-done.3.got.near, ...), custom_call_target="tpu_custom_call" | custom-call | tf_op jit(solution)/shard_map/losses/pallas_call | solution.py:408
  (6 shorter events, 0.0 us)
Async XLA Ops:
  2.6 1.7 %collective-permute-start = (f32[8,128]{1,0:T(8,128)S(1)}, f32[8,128]{1,0:T(8,128)S(1)}, u32[]{:S(2)}, u32[]{:S(2)}) collective-permute-start(f32[8,128]{1,0:T(8,128)S(1)} %params.1.after), channel_id=1, source_target_pairs={{0,1},{1,0},{2,3},{3,2},{4,5},{5,4},{6,7},{7,6},{8,9},{9,8},{10,11... | collective-permute-start | bytes 12296 | tf_op jit(solution)/shard_map/ppermute | solution.py:367
  4.3 4.3 %collective-permute-start.1 = (f32[8,128]{1,0:T(8,128)S(1)}, f32[8,128]{1,0:T(8,128)S(1)}, u32[]{:S(2)}, u32[]{:S(2)}) collective-permute-start(f32[8,128]{1,0:T(8,128)S(1)} %max.9), channel_id=1, source_target_pairs={{0,2},{1,3},{2,0},{3,1},{4,6},{5,7},{6,4},{7,5},{8,10},{9,11},{10,... | collective-permute-start | bytes 12296 | tf_op jit(solution)/shard_map/ppermute | solution.py:367
  6.9 5.5 %collective-permute-start.3 = (f32[32,640]{1,0:T(8,128)S(1)}, f32[32,640]{1,0:T(8,128)S(1)}, u32[]{:S(2)}, u32[]{:S(2)}) collective-permute-start(f32[32,640]{1,0:T(8,128)S(1)} %get-tuple-element.13), channel_id=1, source_target_pairs={{0,8},{1,25},{2,10},{3,27},{4,12},{5,29},{6,14},{7,31},{8,16},{9,1... | collective-permute-start | bytes 245768 | tf_op jit(solution)/shard_map/ppermute | solution.py:367
  8.5 4.7 %collective-permute-start.2 = (f32[8,256]{1,0:T(8,128)S(1)}, f32[8,256]{1,0:T(8,128)S(1)}, u32[]{:S(2)}, u32[]{:S(2)}) collective-permute-start(f32[8,256]{1,0:T(8,128)S(1)} %broadcast_bitcast_fusion), channel_id=1, source_target_pairs={{0,4},{1,5},{2,6},{3,7},{4,0},{5,1},{6,2},{7,3},{8,12},{9,13},{10,... | collective-permute-start | bytes 24584 | tf_op jit(solution)/shard_map/ppermute | solution.py:367
  12.4 1.2 %collective-permute-start.4 = (f32[16,640]{1,0:T(8,128)S(1)}, f32[16,640]{1,0:T(8,128)S(1)}, u32[]{:S(2)}, u32[]{:S(2)}) collective-permute-start(f32[16,640]{1,0:T(8,128)S(1)} %pass_on.1), channel_id=1, source_target_pairs={{0,1},{1,0},{2,3},{3,2},{4,5},{5,4},{6,7},{7,6},{8,9},{9,8},{10,11... | collective-permute-start | bytes 122888 | tf_op jit(solution)/shard_map/ppermute | solution.py:367

commit v4 on v2

--- a/solution.py
+++ b/solution.py
@@ -28,6 +28,48 @@
     after = buf[rows, pl.ds(pl.multiple_of(right, LANES), LANES)]
     before = buf[rows, pl.ds(pl.multiple_of(left, LANES), LANES)]
     return jnp.where(lanes < HALF, after, before)
+
+
+def lane_gather(x, index):
+    return jnp.take_along_axis(x, index, axis=1)
+
+
+def interleave(tiles):
+    n, lanes = len(tiles), lane_iota()
+    out = []
+    for p in range(n):
+        column = n * lanes + p
+        index = lax.rem(column, LANES)
+        if n % 2:
+            mixed = tiles[0]
+            for t in range(1, n):
+                mixed = jnp.where(lax.rem(lanes + t * LANES - p + n, n) == 0, tiles[t], mixed)
+            out.append(lane_gather(mixed, index))
+        else:
+            mixed = lane_gather(tiles[0], index)
+            for t in range(1, n):
+                mixed = jnp.where(column // LANES == t, lane_gather(tiles[t], index), mixed)
+            out.append(mixed)
+    return out
+
+
+def natural(tiles, count):
+    n, lanes = len(tiles), lane_iota()
+    if n % 2:
+        inverse = pow(n, -1, LANES)
+        moved = [
+            lane_gather(x, lax.rem(inverse * (lanes - p + LANES), LANES))
+            for p, x in enumerate(tiles)
+        ]
+    out = []
+    for t in range(count):
+        column = t * LANES + lanes
+        part = lambda p: moved[p] if n % 2 else lane_gather(tiles[p], column // n)
+        mixed = part(0)
+        for p in range(1, n):
+            mixed = jnp.where(lax.rem(column, n) == p, part(p), mixed)
+        out.append(mixed)
+    return out
 
 
 def window(start, size, total):
@@ -45,7 +87,7 @@
     params[...] = jnp.where((rows == h) & (lanes < 3), value, 0.0)
 
 
-def pack_kernel(after, cur, con, coo, out, cur_out, con_out, coo_out, buf, held, sems, *, width):
+def pack_kernel(after, cur, con, coo, out, buf, sems, *, width):
     slab, total = cur.shape
     h = lax.axis_index("harm")
     core = lax.rem(h, 2)
@@ -61,16 +103,6 @@
     ]
     for copy in copies:
         copy.start()
-    size_own = held.shape[2]
-    begin_own = window(h * width, size_own, total)
-    own = [
-        pltpu.make_async_copy(
-            ref.at[:, pl.ds(begin_own, size_own)], held.at[i], sems.at[3 + i]
-        )
-        for i, ref in enumerate((cur, con, coo))
-    ]
-    for copy in own:
-        copy.start()
     sub = sublane_iota()
     goes_up = core == 0
     shift = jnp.where(goes_up, 3, 5)
@@ -81,64 +113,78 @@
         offset = first + target * width - begin
         left = jnp.maximum(offset - LANES, 0)
         right = jnp.minimum(offset + width, size - LANES)
-        pieces = []
-        for j in range(width // LANES):
-            at = pl.ds(pl.multiple_of(offset + j * LANES, LANES), LANES)
-            pieces.append([buf[i, :, at] for i in range(3)])
-        pieces.append(
-            [side_tile(buf.at[i], slice(0, TILE), left, right) for i in range(3)]
-        )
+        fields = []
+        for i in range(3):
+            tiles = [
+                buf[i, :, pl.ds(pl.multiple_of(offset + j * LANES, LANES), LANES)]
+                for j in range(width // LANES)
+            ]
+            tiles.append(side_tile(buf.at[i], slice(0, TILE), left, right))
+            fields.append(interleave(tiles))
         base = part * 2 * TILE
-        for j, (a, b, c) in enumerate(pieces):
+        for j, (a, b, c) in enumerate(zip(*fields)):
             at = slice(j * LANES, (j + 1) * LANES)
             out[base : base + TILE, at] = jnp.where(take_cur, a, pltpu.roll(c, shift, 0))
             out[base + TILE : base + 2 * TILE, at] = b
-    offset = h * width - begin_own
+
+
+def arrange_kernel(after, cur, con, coo, cur_out, con_out, coo_out, held, sems, *, width):
+    slab, total = cur.shape
+    h = lax.axis_index("harm")
+    size = held.shape[2]
+    begin = window(h * width, size, total)
+    copies = [
+        pltpu.make_async_copy(ref.at[:, pl.ds(begin, size)], held.at[i], sems.at[i])
+        for i, ref in enumerate((cur, con, coo))
+    ]
+    for copy in copies:
+        copy.start()
+    offset = h * width - begin
     left = jnp.maximum(offset - LANES, 0)
-    right = jnp.minimum(offset + width, size_own - LANES)
+    right = jnp.minimum(offset + width, size - LANES)
     for i, tile in enumerate((cur_out, con_out, coo_out)):
-        own[i].wait()
-        tile[:, :width] = held[i, :, pl.ds(pl.multiple_of(offset, LANES), width)]
-        tile[:, width:] = side_tile(held.at[i], slice(0, slab), left, right)
+        copies[i].wait()
+        for r in range(0, slab, TILE):
+            rows = slice(r, r + TILE)
+            pieces = [
+                held[i, rows, pl.ds(pl.multiple_of(offset + j * LANES, LANES), LANES)]
+                for j in range(width // LANES)
+            ]
+            pieces.append(side_tile(held.at[i], rows, left, right))
+            for j, piece in enumerate(interleave(pieces)):
+                tile[rows, j * LANES : (j + 1) * LANES] = piece
 
 
 def pass_kernel(after, got, passed):
     passed[...] = got[2 * TILE :, :]
 
 
-def sides(tiles, lanes):
-    n = len(tiles)
-    back = [pltpu.roll(t, 1, 1) for t in tiles]
-    fore = [pltpu.roll(t, LANES - 1, 1) for t in tiles]
-    return [
-        jnp.where(lanes == 0, back[j - 1], back[j])
-        + jnp.where(lanes == LANES - 1, fore[(j + 1) % n], fore[j])
-        for j in range(n)
-    ]
-
-
-def fold_harmonics(rows, sub):
-    level = list(rows)
-    for half in (4, 2, 1):
-        low = (sub & half) == 0
-        merged = []
-        for i in range(half):
-            a, b = level[i], level[i + half]
-            if a is None and b is None:
-                merged.append(None)
-                continue
-            a = jnp.zeros((TILE, LANES), F32) if a is None else a
-            b = jnp.zeros((TILE, LANES), F32) if b is None else b
-            keep = jnp.where(low, a, b)
-            move = jnp.where(low, b, a)
-            merged.append(keep + jnp.where(low, pltpu.roll(move, TILE - half, 0), pltpu.roll(move, half, 0)))
-        level = merged
-    return level[0]
+def sides(tiles):
+    line = [pltpu.roll(tiles[-1], 1, 1), *tiles, pltpu.roll(tiles[0], LANES - 1, 1)]
+    return [a + b for a, b in zip(line[:-2], line[2:])]
+
+
+class Fold:
+    def __init__(self, sub):
+        self.low = [(sub & shift) == 0 for shift in (1, 2, 4)]
+        self.held = [None] * 3
+
+    def add(self, value):
+        for level in range(3):
+            first, self.held[level] = self.held[level], None
+            if first is None:
+                self.held[level] = value
+                return None
+            low = self.low[level]
+            value = jnp.where(low, first, value) + pltpu.roll(
+                jnp.where(low, value, first), 1 << level, 0
+            )
+        return value
 
 
 def loss_kernel(
     par_ref, cur, con, coo, near, far, diss, heat,
-    xcur, xcon, xcoo, rr, gg, ss, ra, ha, rb, hb, qq, *, width, harmonics,
+    xcur, xcon, xcoo, rr, gg, ss, ra, ha, rb, hb, qq, results, sems, *, width, harmonics,
 ):
     slab = cur.shape[0]
     nt = width // LANES + 1
@@ -174,8 +220,16 @@
     has_down = (m < last_m).astype(F32)
     has_left = (h > 0).astype(F32)
     has_right = (h < last_h).astype(F32)
-    col_tile = (h * (width // LANES)).astype(F32)
-    zero = jnp.zeros((TILE, LANES), F32)
+    columns = [nt * lanes + j for j in range(nt)]
+    inside = [
+        jnp.where(c < width, 1.0, jnp.where(c < width + HALF, has_right, has_left))
+        for c in columns
+    ]
+
+    def first_block(j):
+        block = jnp.where(columns[j] < width + HALF, columns[j] // LANES, -1)
+        return (block + h * (width // LANES)).astype(F32)
+
 
     for group in range((harmonics + TILE - 1) // TILE):
         at = slice(group * TILE, (group + 1) * TILE)
@@ -187,15 +241,8 @@
         quarter = 0.25 * omega
         weight = (0.5 / harmonics) * omega * amp * amp
         masks = [
-            jnp.where(count > col_tile + j, 0.25, 0.0) for j in range(nt - 1)
+            jnp.where(count > first_block(j), 0.25 * inside[j], 0.0) for j in range(nt)
         ]
-        masks.append(
-            jnp.where(
-                lanes < HALF,
-                jnp.where(count > col_tile + (nt - 1), 0.25 * has_right, 0.0),
-                jnp.where(count > col_tile - 1, 0.25 * has_left, 0.0),
-            )
-        )
 
         def start_rows(base, subs, scale):
             scaled = masks if scale is None else [k * scale for k in masks]
@@ -224,22 +271,33 @@
             start_rows(pl.multiple_of(top + i * TILE, TILE), range(TILE), None)
             return carry
 
-        lax.fori_loop(0, slab // TILE, start_body, 0)
+        lax.fori_loop(0, slab // TILE, start_body, 0, unroll=True)
 
         def load(ref, row):
             return [ref[row, :, j * LANES : (j + 1) * LANES] for j in range(nt)]
 
-        def near_sum(ref, row):
-            mid = sides(load(ref, row), lanes)
+        def cached(ref):
+            rows = {}
+
+            def get(base, s):
+                if s not in rows:
+                    rows[s] = load(ref, base + s)
+                return rows[s]
+
+            return get
+
+        def near_sum(get, base, s):
+            mid = sides(get(base, s))
             return [
                 x + (u + v)
-                for x, u, v in zip(mid, load(ref, row - 1), load(ref, row + 1))
+                for x, u, v in zip(mid, get(base, s - 1), get(base, s + 1))
             ]
 
         def sweep_rows(base, subs):
+            get_r, get_h = cached(ra), cached(ha)
             for s in subs:
                 row = base + s
-                nr, nh = near_sum(ra, row), near_sum(ha, row)
+                nr, nh = near_sum(get_r, base, s), near_sum(get_h, base, s)
                 r, g, src = load(rr, row), load(gg, row), load(ss, row)
                 for j in range(nt):
                     col = slice(j * LANES, (j + 1) * LANES)
@@ -251,20 +309,27 @@
             sweep_rows(TILE - MARGIN + 1 + i * TILE, range(TILE))
             return carry
 
-        lax.fori_loop(0, (slab + 2 * (MARGIN - 1)) // TILE, sweep_body, 0)
+        lax.fori_loop(0, (slab + 2 * (MARGIN - 1)) // TILE, sweep_body, 0, unroll=True)
 
         def loss_rows(base, subs):
-            rows = [[None] * TILE for _ in range(nt)]
-            for s in subs:
+            folds, totals = [Fold(sub) for _ in range(nt)], [None] * nt
+            zero = jnp.zeros((TILE, LANES), F32)
+            get_r, get_h = cached(rb), cached(hb)
+            for s in range(TILE):
+                if s not in subs:
+                    totals = [fold.add(zero) for fold in folds]
+                    continue
                 row = base + s
-                nr, nh = near_sum(rb, row), near_sum(hb, row)
+                nr, nh = near_sum(get_r, base, s), near_sum(get_h, base, s)
                 r, g, src = load(rr, row), load(gg, row), load(ss, row)
                 for j in range(nt):
                     x = src[j] + nr[j]
-                    rows[j][s] = (weight * g[j] * r[j]) * (x * x + nh[j] * nh[j])
+                    totals[j] = folds[j].add(
+                        (weight * g[j] * r[j]) * (x * x + nh[j] * nh[j])
+                    )
             for j in range(nt):
                 col = slice(j * LANES, (j + 1) * LANES)
-                total = fold_harmonics(rows[j], sub)
+                total = totals[j]
                 if group:
                     total = qq[pl.ds(base, TILE), col] + total
                 qq[pl.ds(base, TILE), col] = total
@@ -276,11 +341,20 @@
             loss_rows(pl.multiple_of(top + i * TILE, TILE), range(TILE))
             return carry
 
-        lax.fori_loop(0, slab // TILE, loss_body, 0)
+        lax.fori_loop(0, slab // TILE, loss_body, 0, unroll=True)
 
     ntile = ext // TILE
-    side = jnp.where(lanes < HALF, has_right, has_left)
     q = [[qq[i * TILE : (i + 1) * TILE, j * LANES : (j + 1) * LANES] for j in range(nt)] for i in range(ntile)]
+
+    def hand_out(k, lines):
+        for i in range(1, ntile - 1):
+            for j, tile in enumerate(natural(lines[i], nt - 1)):
+                results[k, (i - 1) * TILE : i * TILE, j * LANES : (j + 1) * LANES] = tile
+        copy = pltpu.make_async_copy(results.at[k], (diss, heat)[k], sems.at[k])
+        copy.start()
+        return copy
+
+    first = hand_out(0, q)
     rec = []
     for i in range(ntile):
         line = []
@@ -290,9 +364,7 @@
                 w = w * has_up
             if i == ntile - 1:
                 w = w * has_down
-            if j == nt - 1:
-                w = w * side
-            line.append(w)
+            line.append(w * inside[j])
         rec.append(line)
     t = [[q[i][j] * rec[i][j] for j in range(nt)] for i in range(ntile)]
     for _ in range(3):
@@ -300,7 +372,7 @@
         fore = [[pltpu.roll(x, TILE - 1, 0) for x in line] for line in t]
         new = []
         for i in range(ntile):
-            mid = sides(t[i], lanes)
+            mid = sides(t[i])
             line = []
             for j in range(nt):
                 above = jnp.where(sub == 0, back[i - 1][j], back[i][j])
@@ -308,11 +380,9 @@
                 line.append((q[i][j] + (mid[j] + (above + below))) * rec[i][j])
             new.append(line)
         t = new
-    for i in range(1, ntile - 1):
-        for j in range(nt - 1):
-            at = (slice((i - 1) * TILE, i * TILE), slice(j * LANES, (j + 1) * LANES))
-            diss[at] = q[i][j]
-            heat[at] = t[i][j]
+    second = hand_out(1, t)
+    first.wait()
+    second.wait()
 
 
 def on_device(current_pattern, conductivity, cooling, harm_order, harm_amp, block_counts):
@@ -339,20 +409,18 @@
         compiler_params=small,
         name="params",
     )(harm_order, harm_amp, block_counts)
-    edges, tile_cur, tile_con, tile_coo = pl.pallas_call(
+    edges = pl.pallas_call(
         functools.partial(pack_kernel, width=width),
-        out_shape=(held_vmem(4 * TILE, wide),) + (held_vmem(slab, wide),) * 3,
+        out_shape=held_vmem(4 * TILE, wide),
         in_specs=[any_space] * 4,
-        out_specs=(vmem,) * 4,
+        out_specs=vmem,
         scratch_shapes=[
             pltpu.VMEM((3, TILE, min(2 * width + 2 * LANES, total)), F32),
-            pltpu.VMEM((3, slab, min(width + 2 * LANES, total)), F32),
-            pltpu.SemaphoreType.DMA((6,)),
+            pltpu.SemaphoreType.DMA((3,)),
         ],
         compiler_params=small,
         name="pack",
     )(params, *map(in_hbm, fields))
-
     axes = ("mesh", "harm")
 
     def permute(value, target):
@@ -373,24 +441,18 @@
         return m + (1 - 2 * c), z, c
 
     known = jnp.maximum(params, swap(params))
-    stages = [known]
-    edges, known = lax.optimization_barrier((edges, known))
+    edges, before = lax.optimization_barrier((edges, known))
     got = permute(edges, beside)
-    if chips & (chips - 1) == 0:
-        step = 1
-        while step < chips:
-            known = jnp.maximum(
-                known, permute(known, lambda m, z, c: (m, z ^ step, c))
-            )
-            stages.append(known)
-            step *= 2
-    else:
-        table = known
-        for step in range(1, chips):
-            known = jnp.maximum(
-                known, permute(table, lambda m, z, c: (m, z + step, c))
-            )
-            stages.append(known)
+    power = chips & (chips - 1) == 0
+    steps = [1 << i for i in range(chips.bit_length() - 1)] if power else range(1, chips)
+    last = table = before
+    for i, step in enumerate(steps):
+        before = jnp.maximum(before, last)
+        if power:
+            table = before
+        sent = jnp.tile(table, (1, 2)) if i else table
+        hop = lambda m, z, c: (m, z ^ step if power else z + step, c)
+        last = permute(sent, hop)[:, :LANES]
     passed = pl.pallas_call(
         pass_kernel,
         out_shape=held_vmem(2 * TILE, wide),
@@ -398,9 +460,24 @@
         out_specs=vmem,
         compiler_params=small,
         name="pass_on",
-    )(stages[min(1, len(stages) - 1)], got)
+    )(before, got)
     far = swap(passed)
 
+    tile_cur, tile_con, tile_coo = pl.pallas_call(
+        functools.partial(arrange_kernel, width=width),
+        out_shape=(held_vmem(slab, wide),) * 3,
+        in_specs=[any_space] * 4,
+        out_specs=(vmem,) * 3,
+        scratch_shapes=[
+            pltpu.VMEM((3, slab, min(width + 2 * LANES, total)), F32),
+            pltpu.SemaphoreType.DMA((3,)),
+        ],
+        compiler_params=small,
+        name="arrange",
+    )(passed, *fields)
+
+    before, tile_cur = lax.optimization_barrier((before, tile_cur))
+    known = jnp.maximum(before, last)
     ext = slab + 2 * TILE
     flat = pltpu.VMEM((ext, wide), F32)
     deep = pltpu.VMEM((ext, TILE, wide), F32)
@@ -408,8 +485,10 @@
         functools.partial(loss_kernel, width=width, harmonics=harm),
         out_shape=(shape(slab, width),) * 2,
         in_specs=[vmem] * 6,
-        out_specs=(vmem,) * 2,
-        scratch_shapes=[flat] * 3 + [deep] * 7 + [flat],
+        out_specs=(any_space,) * 2,
+        scratch_shapes=[flat] * 3
+        + [deep] * 7
+        + [flat, pltpu.VMEM((2, slab, width), F32), pltpu.SemaphoreType.DMA((2,))],
         compiler_params=pltpu.CompilerParams(vmem_limit_bytes=12 * 2**20),
         name="losses",
     )(known, tile_cur, tile_con, tile_coo, got, far)

time: 19.7 us -> 15.9 us (0.81)
  waiting for transfers between devices: 4.47 us -> 1.48 us
  Pallas kernels: 5.02 us -> 3.71 us
  starting transfers between devices: 7.4 us -> 7.86 us
    ppermute x5, waiting for transfers between devices: 4.47 us -> 1.48 us  [permute(): return lax.ppermute(value, axes, pairs)]
    pallas_call x1, Pallas kernels: 3.88 us -> 2.16 us  [on_device(): pl.pallas_call(functools.partial(loss_kernel, width=width, harmonics=harm...]
    ppermute x5, starting transfers between devices: 7.4 us -> 7.86 us  [permute(): return lax.ppermute(value, axes, pairs)]
    pallas_call x1 -> x2, Pallas kernels: 1.12 us -> 1.54 us  [the longest x1 1.01 us: on_device(): pl.pallas_call(functools.partial(pack_kernel, width=width), out_shape=hel...]
  transfers between devices with their start and end apart: 5 -> 5, of which waited for: 3 -> 4; matrix products, arithmetic and copies ran while one was open for 0% -> 0% of each run, Pallas kernels for 6% -> 10%
where the time goes in v4:
time: 15.9 us; the launch traced here: 15.7 us
  starting transfers between devices  7.86 us (49%)
  Pallas kernels  3.71 us (23%)
  between operations  2.66 us (17%)
  waiting for transfers between devices  1.48 us (9%)
    ppermute x5, starting transfers between devices, permute(): return lax.ppermute(value, axes, pairs)  7.86 us
    pallas_call x1, Pallas kernels, on_device(): pl.pallas_call(functools.partial(loss_kernel, width=width, harmonics=harm...  2.16 us
    ppermute x5, waiting for transfers between devices, permute(): return lax.ppermute(value, axes, pairs)  1.48 us
    pallas_call x1, Pallas kernels, on_device(): pl.pallas_call(functools.partial(pack_kernel, width=width), out_shape=hel...  1.01 us
    pallas_call x1, Pallas kernels, on_device(): pl.pallas_call(functools.partial(arrange_kernel, width=width), out_shape=...  0.53 us
  transfers between devices with their start and end apart: 5, of which 4 were waited for; matrix products, arithmetic and copies ran while one was open for 0% of the time, Pallas kernels for 10%

profile of v4, /device:TPU:0, one launch (start us, length us, event | category | flops | bytes accessed | tf_op | source)
XLA Modules:
  0.0 15.7 jit_solution(6212621519546215259)
XLA Ops:
  2.6 0.0 copy-start
  2.6 0.0 copy-start.1
  2.6 0.0 copy-start.2
  2.6 0.5 %collective-permute-start = (f32[8,128]{1,0:T(8,128)S(1)}, f32[8,128]{1,0:T(8,128)S(1)}, u32[]{:S(2)}, u32[]{:S(2)}) collective-permute-start(f32[8,128]{1,0:T(8,128)S(1)} %params.1.after), channel_id=1, source_target_pairs={{0,1},{1,0},{2,3},{3,2},{4,5},{5,4},{6,7},{7,6},{8,9},{9,8},{10,11... | collective-permute-start | bytes 12296 | tf_op jit(solution)/shard_map/ppermute | solution.py:435
  3.1 1.0 %pack.1 = f32[32,640]{1,0:T(8,128)S(1)} custom-call(f32[8,128]{1,0:T(8,128)S(1)} %params.1.after, f32[32,4096]{1,0:T(8,128)} %cur.3, f32[32,4096]{1,0:T(8,128)} %con.3, f32[32,4096]{1,0:T(8,128)} %coo.3), custom_call_target="tpu_custom_call" | custom-call | tf_op jit(solution)/shard_map/pack/pallas_call | solution.py:412
  4.2 0.0 collective-permute-done
  4.2 2.8 %collective-permute-start.1 = (f32[8,128]{1,0:T(8,128)S(1)}, f32[8,128]{1,0:T(8,128)S(1)}, u32[]{:S(2)}, u32[]{:S(2)}) collective-permute-start(f32[8,128]{1,0:T(8,128)S(1)} %max.10), channel_id=1, source_target_pairs={{0,2},{1,3},{2,0},{3,1},{4,6},{5,7},{6,4},{7,5},{8,10},{9,11},{10,... | collective-permute-start | bytes 12296 | tf_op jit(solution)/shard_map/ppermute | solution.py:435
  7.0 1.5 %collective-permute-start.2 = (f32[32,640]{1,0:T(8,128)S(1)}, f32[32,640]{1,0:T(8,128)S(1)}, u32[]{:S(2)}, u32[]{:S(2)}) collective-permute-start(f32[32,640]{1,0:T(8,128)S(1)} %pack.1), channel_id=1, source_target_pairs={{0,8},{1,25},{2,10},{3,27},{4,12},{5,29},{6,14},{7,31},{8,16},{9,1... | collective-permute-start | bytes 245768 | tf_op jit(solution)/shard_map/ppermute | solution.py:435
  8.5 0.1 collective-permute-done.1
  8.5 3.1 %collective-permute-start.3 = (f32[8,256]{1,0:T(8,128)S(1)}, f32[8,256]{1,0:T(8,128)S(1)}, u32[]{:S(2)}, u32[]{:S(2)}) collective-permute-start(f32[8,256]{1,0:T(8,128)S(1)} %broadcast_bitcast_fusion), channel_id=1, source_target_pairs={{0,4},{1,5},{2,6},{3,7},{4,0},{5,1},{6,2},{7,3},{8,12},{9,13},{10,... | collective-permute-start | bytes 24584 | tf_op jit(solution)/shard_map/ppermute | solution.py:435
  11.6 0.8 %collective-permute-done.2.got.near = f32[32,640]{1,0:T(8,128)S(1)} collective-permute-done((f32[32,640]{1,0:T(8,128)S(1)}, f32[32,640]{1,0:T(8,128)S(1)}, u32[]{:S(2)}, u32[]{:S(2)}) %collective-permute-start.2) | collective-permute-done | bytes 81952 | tf_op jit(solution)/shard_map/ppermute | solution.py:435
  12.4 0.0 collective-permute-start.4
  12.4 0.0 copy-done
  12.4 0.0 copy-done.1
  12.4 0.0 copy-done.2
  12.4 0.5 %arrange.1 = (f32[32,640]{1,0:T(8,128)S(1)}, f32[32,640]{1,0:T(8,128)S(1)}, f32[32,640]{1,0:T(8,128)S(1)}) custom-call(f32[16,640]{1,0:T(8,128)S(1)} %pass_on.1.after, f32[32,4096]{1,0:T(8,128)S(1)} %copy-done, f32[32,4096]{1,0:T(8,128)S(1)} %copy-done.1, f32[32,4096]{1,0:T(8,128)S(1)} %copy-done.2), custom_call_target="tpu_custom_call" | custom-call | tf_op jit(solution)/shard_map/arrange/pallas_call | solution.py:466
  12.9 0.3 %collective-permute-done.3 = f32[8,256]{1,0:T(8,128)S(1)} collective-permute-done((f32[8,256]{1,0:T(8,128)S(1)}, f32[8,256]{1,0:T(8,128)S(1)}, u32[]{:S(2)}, u32[]{:S(2)}) %collective-permute-start.3) | collective-permute-done | bytes 8224 | tf_op jit(solution)/shard_map/ppermute | solution.py:435
  13.2 0.3 %collective-permute-done.4.far = f32[16,640]{1,0:T(8,128)S(1)} collective-permute-done((f32[16,640]{1,0:T(8,128)S(1)}, f32[16,640]{1,0:T(8,128)S(1)}, u32[]{:S(2)}, u32[]{:S(2)}) %collective-permute-start.4) | collective-permute-done | bytes 40992 | tf_op jit(solution)/shard_map/ppermute | solution.py:435
  13.6 2.2 %losses.1 = (f32[32,512]{1,0:T(8,128)}, f32[32,512]{1,0:T(8,128)}) custom-call(f32[8,128]{1,0:T(8,128)S(1)} %slice_maximum_fusion.par_ref, f32[32,640]{1,0:T(8,128)S(1)} %get-tuple-element.13.cur, f32[32,640]{1,0:T(8,128)S(1)} %get-tuple-element.14.con, f32[32,640]{1,0:T(8,128)S(1)} %get-tuple-element.15.coo, f32[32,640]{1,0:T(8,128)S(1)} %collective-permute-done.2.got.near, ...), custom_call_target="tpu_custom_call" | custom-call | tf_op jit(solution)/shard_map/losses/pallas_call | solution.py:484
  (6 shorter events, 0.0 us)
Async XLA Ops:
  2.6 9.8 %copy-start = (f32[32,4096]{1,0:T(8,128)S(1)}, f32[32,4096]{1,0:T(8,128)}, u32[]{:S(2)}) copy-start(f32[32,4096]{1,0:T(8,128)} %cur.3) | copy-start | bytes 1572868
  2.6 9.8 %copy-start.1 = (f32[32,4096]{1,0:T(8,128)S(1)}, f32[32,4096]{1,0:T(8,128)}, u32[]{:S(2)}) copy-start(f32[32,4096]{1,0:T(8,128)} %con.3) | copy-start | bytes 1572868
  2.6 9.8 %copy-start.2 = (f32[32,4096]{1,0:T(8,128)S(1)}, f32[32,4096]{1,0:T(8,128)}, u32[]{:S(2)}) copy-start(f32[32,4096]{1,0:T(8,128)} %coo.3) | copy-start | bytes 1572868
  2.6 1.5 %collective-permute-start = (f32[8,128]{1,0:T(8,128)S(1)}, f32[8,128]{1,0:T(8,128)S(1)}, u32[]{:S(2)}, u32[]{:S(2)}) collective-permute-start(f32[8,128]{1,0:T(8,128)S(1)} %params.1.after), channel_id=1, source_target_pairs={{0,1},{1,0},{2,3},{3,2},{4,5},{5,4},{6,7},{7,6},{8,9},{9,8},{10,11... | collective-permute-start | bytes 12296 | tf_op jit(solution)/shard_map/ppermute | solution.py:435
  4.2 4.3 %collective-permute-start.1 = (f32[8,128]{1,0:T(8,128)S(1)}, f32[8,128]{1,0:T(8,128)S(1)}, u32[]{:S(2)}, u32[]{:S(2)}) collective-permute-start(f32[8,128]{1,0:T(8,128)S(1)} %max.10), channel_id=1, source_target_pairs={{0,2},{1,3},{2,0},{3,1},{4,6},{5,7},{6,4},{7,5},{8,10},{9,11},{10,... | collective-permute-start | bytes 12296 | tf_op jit(solution)/shard_map/ppermute | solution.py:435
  7.0 5.4 %collective-permute-start.2 = (f32[32,640]{1,0:T(8,128)S(1)}, f32[32,640]{1,0:T(8,128)S(1)}, u32[]{:S(2)}, u32[]{:S(2)}) collective-permute-start(f32[32,640]{1,0:T(8,128)S(1)} %pack.1), channel_id=1, source_target_pairs={{0,8},{1,25},{2,10},{3,27},{4,12},{5,29},{6,14},{7,31},{8,16},{9,1... | collective-permute-start | bytes 245768 | tf_op jit(solution)/shard_map/ppermute | solution.py:435
  8.5 4.7 %collective-permute-start.3 = (f32[8,256]{1,0:T(8,128)S(1)}, f32[8,256]{1,0:T(8,128)S(1)}, u32[]{:S(2)}, u32[]{:S(2)}) collective-permute-start(f32[8,256]{1,0:T(8,128)S(1)} %broadcast_bitcast_fusion), channel_id=1, source_target_pairs={{0,4},{1,5},{2,6},{3,7},{4,0},{5,1},{6,2},{7,3},{8,12},{9,13},{10,... | collective-permute-start | bytes 24584 | tf_op jit(solution)/shard_map/ppermute | solution.py:435
  12.4 1.2 %collective-permute-start.4 = (f32[16,640]{1,0:T(8,128)S(1)}, f32[16,640]{1,0:T(8,128)S(1)}, u32[]{:S(2)}, u32[]{:S(2)}) collective-permute-start(f32[16,640]{1,0:T(8,128)S(1)} %pass_on.1.after), channel_id=1, source_target_pairs={{0,1},{1,0},{2,3},{3,2},{4,5},{5,4},{6,7},{7,6},{8,9},{9,8},{10,11... | collective-permute-start | bytes 122888 | tf_op jit(solution)/shard_map/ppermute | solution.py:435

commit v5 on v4

--- a/solution.py
+++ b/solution.py
@@ -34,42 +34,57 @@
     return jnp.take_along_axis(x, index, axis=1)
 
 
-def interleave(tiles):
-    n, lanes = len(tiles), lane_iota()
-    out = []
-    for p in range(n):
-        column = n * lanes + p
-        index = lax.rem(column, LANES)
+class Columns:
+    def __init__(self, n):
+        self.n, lanes = n, lane_iota()
+        self.columns = [n * lanes + p for p in range(n)]
         if n % 2:
-            mixed = tiles[0]
-            for t in range(1, n):
-                mixed = jnp.where(lax.rem(lanes + t * LANES - p + n, n) == 0, tiles[t], mixed)
-            out.append(lane_gather(mixed, index))
+            inverse = pow(n, -1, LANES)
+            self.index = [lax.rem(c, LANES) for c in self.columns]
+            self.back = [lax.rem(inverse * (lanes - p + LANES), LANES) for p in range(n)]
+            phase = lax.rem(lanes, n)
+            self.phase = [phase == k for k in range(n)]
         else:
-            mixed = lane_gather(tiles[0], index)
-            for t in range(1, n):
-                mixed = jnp.where(column // LANES == t, lane_gather(tiles[t], index), mixed)
+            self.index = [lax.rem(c, LANES) for c in self.columns]
+            self.back = [(t * LANES + lanes) // n for t in range(n)]
+
+    def interleave(self, tiles):
+        n, out = self.n, []
+        for p in range(n):
+            if n % 2:
+                mixed = tiles[0]
+                for t in range(1, n):
+                    mixed = jnp.where(self.phase[(p - t * LANES) % n], tiles[t], mixed)
+                out.append(lane_gather(mixed, self.index[p]))
+            else:
+                mixed = lane_gather(tiles[0], self.index[p])
+                for t in range(1, n):
+                    mixed = jnp.where(
+                        self.columns[p] // LANES == t,
+                        lane_gather(tiles[t], self.index[p]),
+                        mixed,
+                    )
+                out.append(mixed)
+        return out
+
+    def natural(self, tiles, count):
+        n, out = self.n, []
+        if n % 2:
+            tiles = [lane_gather(x, self.back[p]) for p, x in enumerate(tiles)]
+        for t in range(count):
+            if n % 2:
+                mixed = tiles[0]
+                for p in range(1, n):
+                    mixed = jnp.where(self.phase[(p - t * LANES) % n], tiles[p], mixed)
+            else:
+                lanes = lane_iota()
+                mixed = lane_gather(tiles[0], self.back[t])
+                for p in range(1, n):
+                    mixed = jnp.where(
+                        lax.rem(lanes, n) == p, lane_gather(tiles[p], self.back[t]), mixed
+                    )
             out.append(mixed)
-    return out
-
-
-def natural(tiles, count):
-    n, lanes = len(tiles), lane_iota()
-    if n % 2:
-        inverse = pow(n, -1, LANES)
-        moved = [
-            lane_gather(x, lax.rem(inverse * (lanes - p + LANES), LANES))
-            for p, x in enumerate(tiles)
-        ]
-    out = []
-    for t in range(count):
-        column = t * LANES + lanes
-        part = lambda p: moved[p] if n % 2 else lane_gather(tiles[p], column // n)
-        mixed = part(0)
-        for p in range(1, n):
-            mixed = jnp.where(lax.rem(column, n) == p, part(p), mixed)
-        out.append(mixed)
-    return out
+        return out
 
 
 def window(start, size, total):
@@ -103,6 +118,7 @@
     ]
     for copy in copies:
         copy.start()
+    columns = Columns(width // LANES + 1)
     sub = sublane_iota()
     goes_up = core == 0
     shift = jnp.where(goes_up, 3, 5)
@@ -120,7 +136,7 @@
                 for j in range(width // LANES)
             ]
             tiles.append(side_tile(buf.at[i], slice(0, TILE), left, right))
-            fields.append(interleave(tiles))
+            fields.append(columns.interleave(tiles))
         base = part * 2 * TILE
         for j, (a, b, c) in enumerate(zip(*fields)):
             at = slice(j * LANES, (j + 1) * LANES)
@@ -142,6 +158,7 @@
     offset = h * width - begin
     left = jnp.maximum(offset - LANES, 0)
     right = jnp.minimum(offset + width, size - LANES)
+    columns = Columns(width // LANES + 1)
     for i, tile in enumerate((cur_out, con_out, coo_out)):
         copies[i].wait()
         for r in range(0, slab, TILE):
@@ -151,7 +168,7 @@
                 for j in range(width // LANES)
             ]
             pieces.append(side_tile(held.at[i], rows, left, right))
-            for j, piece in enumerate(interleave(pieces)):
+            for j, piece in enumerate(columns.interleave(pieces)):
                 tile[rows, j * LANES : (j + 1) * LANES] = piece
 
 
@@ -184,7 +201,7 @@
 
 def loss_kernel(
     par_ref, cur, con, coo, near, far, diss, heat,
-    xcur, xcon, xcoo, rr, gg, ss, ra, ha, rb, hb, qq, results, sems, *, width, harmonics,
+    xcur, xcon, xcoo, rr, rb, hb, qq, results, sems, *, width, harmonics,
 ):
     slab = cur.shape[0]
     nt = width // LANES + 1
@@ -196,6 +213,7 @@
     last_m = lax.axis_size("mesh") - 1
     core = lax.rem(h, 2)
     lanes, sub = lane_iota(), sublane_iota()
+    cols = [slice(j * LANES, (j + 1) * LANES) for j in range(nt)]
     xcur[top:bottom, :] = cur[...]
     xcon[top:bottom, :] = con[...]
     xcoo[top:bottom, :] = coo[...]
@@ -220,7 +238,8 @@
     has_down = (m < last_m).astype(F32)
     has_left = (h > 0).astype(F32)
     has_right = (h < last_h).astype(F32)
-    columns = [nt * lanes + j for j in range(nt)]
+    order_of = Columns(nt)
+    columns = order_of.columns
     inside = [
         jnp.where(c < width, 1.0, jnp.where(c < width + HALF, has_right, has_left))
         for c in columns
@@ -231,7 +250,53 @@
         return (block + h * (width // LANES)).astype(F32)
 
 
-    for group in range((harmonics + TILE - 1) // TILE):
+    ntile = ext // TILE
+    losses, weights, levels, copies = [], [], [[], [], [], []], []
+
+    def hand_out(k, i, tiles):
+        rows = slice((i - 1) * TILE, i * TILE)
+        for col, tile in zip(cols, order_of.natural(tiles, nt - 1)):
+            results[k, rows, col] = tile
+        copy = pltpu.make_async_copy(
+            results.at[k, rows, :], (diss, heat)[k].at[rows, :], sems.at[k, i - 1]
+        )
+        copy.start()
+        copies.append(copy)
+
+    def sweep(i, before):
+        rolled = lambda k, shift: [pltpu.roll(x, shift, 0) for x in before[k]]
+        above, below = rolled(i, 1), rolled(i, TILE - 1)
+        if i > 0:
+            above = [jnp.where(sub == 0, p, x) for p, x in zip(rolled(i - 1, 1), above)]
+        if i < ntile - 1:
+            below = [jnp.where(sub == TILE - 1, p, x) for p, x in zip(rolled(i + 1, TILE - 1), below)]
+        return [
+            (q + (x + (a + b))) * w
+            for q, x, a, b, w in zip(losses[i], sides(before[i]), above, below, weights[i])
+        ]
+
+    def conduct(i, q):
+        losses.append(q)
+        scale = has_up if i == 0 else has_down if i == ntile - 1 else None
+        w = [
+            pl.reciprocal(4.0 + xcoo[i * TILE : (i + 1) * TILE, col], approx=True) * x
+            for col, x in zip(cols, inside)
+        ]
+        weights.append(w if scale is None else [x * scale for x in w])
+        levels[0].append([a * b for a, b in zip(q, weights[i])])
+        if 0 < i < ntile - 1:
+            hand_out(0, i, q)
+        for k in range(1, 4):
+            ready = [i - k] if i < ntile - 1 else list(range(max(i - k, 0), ntile))
+            for at in ready:
+                if at >= 0:
+                    outer = at in (0, ntile - 1)
+                    levels[k].append(None if k == 3 and outer else sweep(at, levels[k - 1]))
+                    if k == 3 and not outer:
+                        hand_out(1, at, levels[3][at])
+
+    groups = (harmonics + TILE - 1) // TILE
+    for group in range(groups):
         at = slice(group * TILE, (group + 1) * TILE)
         par = par_ref[at, :]
         order = jnp.broadcast_to(par[:, 0:1], (TILE, LANES))
@@ -239,150 +304,95 @@
         count = jnp.broadcast_to(par[:, 2:3], (TILE, LANES))
         omega = BASE_FREQ * order
         quarter = 0.25 * omega
-        weight = (0.5 / harmonics) * omega * amp * amp
+        scale_of_loss = (0.5 / harmonics) * quarter * omega * amp * amp
+        zero = jnp.zeros((TILE, LANES), F32)
         masks = [
             jnp.where(count > first_block(j), 0.25 * inside[j], 0.0) for j in range(nt)
         ]
 
-        def start_rows(base, subs, scale):
-            scaled = masks if scale is None else [k * scale for k in masks]
-            for j in range(nt):
-                col = slice(j * LANES, (j + 1) * LANES)
-                a = xcur[pl.ds(base, TILE), col]
-                b = xcon[pl.ds(base, TILE), col]
-                for s in subs:
-                    src = jnp.broadcast_to(a[s : s + 1, :], (TILE, LANES))
-                    g = quarter * jnp.broadcast_to(b[s : s + 1, :], (TILE, LANES))
-                    d = 1.0 + g * g
-                    r = pl.reciprocal(d, approx=True)
-                    r = r * (2.0 - d * r)
-                    r = r * scaled[j]
-                    re = src * r
-                    rr[base + s, :, col] = r
-                    gg[base + s, :, col] = g
-                    ss[base + s, :, col] = src
-                    ra[base + s, :, col] = re
-                    ha[base + s, :, col] = g * re
-
-        start_rows(0, range(TILE - MARGIN, TILE), has_up)
-        start_rows(bottom, range(MARGIN), has_down)
-
-        def start_body(i, carry):
-            start_rows(pl.multiple_of(top + i * TILE, TILE), range(TILE), None)
-            return carry
-
-        lax.fori_loop(0, slab // TILE, start_body, 0, unroll=True)
+        def spread(ref, row):
+            return [
+                jnp.broadcast_to(ref[row : row + 1, j * LANES : (j + 1) * LANES], (TILE, LANES))
+                for j in range(nt)
+            ]
 
         def load(ref, row):
             return [ref[row, :, j * LANES : (j + 1) * LANES] for j in range(nt)]
 
-        def cached(ref):
-            rows = {}
-
-            def get(base, s):
-                if s not in rows:
-                    rows[s] = load(ref, base + s)
-                return rows[s]
-
-            return get
-
-        def near_sum(get, base, s):
-            mid = sides(get(base, s))
-            return [
-                x + (u + v)
-                for x, u, v in zip(mid, get(base, s - 1), get(base, s + 1))
+        def store(ref, row, tiles):
+            for j, tile in enumerate(tiles):
+                ref[row, :, j * LANES : (j + 1) * LANES] = tile
+
+        def pair(here, below):
+            below = [*below[1:], pltpu.roll(below[0], LANES - 1, 1)]
+            return [a + b for a, b in zip(here, below)]
+
+        def neighbours(above, here):
+            here = [pltpu.roll(here[-1], 1, 1), *here[:-1]]
+            return [a + b for a, b in zip(above, here)]
+
+        def slope(row):
+            return [quarter * x for x in spread(xcon, row)]
+
+        first, last = top - MARGIN, bottom + MARGIN - 1
+        up = [k * has_up for k in masks]
+        down = [k * has_down for k in masks]
+        old = old_pairs = None
+        for row in range(first, last + 1):
+            scale = up if row < top else down if row >= bottom else masks
+            src, g = spread(xcur, row), slope(row)
+            r = [
+                pl.reciprocal(1.0 + x * x, approx=True) * k for x, k in zip(g, scale)
             ]
-
-        def sweep_rows(base, subs):
-            get_r, get_h = cached(ra), cached(ha)
-            for s in subs:
-                row = base + s
-                nr, nh = near_sum(get_r, base, s), near_sum(get_h, base, s)
-                r, g, src = load(rr, row), load(gg, row), load(ss, row)
-                for j in range(nt):
-                    col = slice(j * LANES, (j + 1) * LANES)
-                    x = src[j] + nr[j]
-                    rb[row, :, col] = r[j] * (x - g[j] * nh[j])
-                    hb[row, :, col] = r[j] * (g[j] * x + nh[j])
-
-        def sweep_body(i, carry):
-            sweep_rows(TILE - MARGIN + 1 + i * TILE, range(TILE))
-            return carry
-
-        lax.fori_loop(0, (slab + 2 * (MARGIN - 1)) // TILE, sweep_body, 0, unroll=True)
-
-        def loss_rows(base, subs):
-            folds, totals = [Fold(sub) for _ in range(nt)], [None] * nt
-            zero = jnp.zeros((TILE, LANES), F32)
-            get_r, get_h = cached(rb), cached(hb)
-            for s in range(TILE):
-                if s not in subs:
-                    totals = [fold.add(zero) for fold in folds]
-                    continue
-                row = base + s
-                nr, nh = near_sum(get_r, base, s), near_sum(get_h, base, s)
-                r, g, src = load(rr, row), load(gg, row), load(ss, row)
-                for j in range(nt):
-                    x = src[j] + nr[j]
-                    totals[j] = folds[j].add(
-                        (weight * g[j] * r[j]) * (x * x + nh[j] * nh[j])
-                    )
-            for j in range(nt):
-                col = slice(j * LANES, (j + 1) * LANES)
-                total = totals[j]
+            re = [a * b for a, b in zip(src, r)]
+            him = [a * b for a, b in zip(g, re)]
+            if first + 2 <= row <= last - 2:
+                store(rr, row, r)
+            if old is not None:
+                pairs = pair(old[0], re), pair(old[1], him)
+                if old_pairs is not None:
+                    nr = neighbours(old_pairs[0], pairs[0])
+                    nh = neighbours(old_pairs[1], pairs[1])
+                    x = [a + b for a, b in zip(old[4], nr)]
+                    store(rb, row - 1, [k * (a - b * c) for k, a, b, c in zip(old[2], x, old[3], nh)])
+                    store(hb, row - 1, [k * (b * a + c) for k, a, b, c in zip(old[2], x, old[3], nh)])
+                old_pairs = pairs
+            old = re, him, r, g, src
+
+        old = old_pairs = None
+        folds, totals = [Fold(sub) for _ in range(nt)], None
+        for row in range(ext):
+            if first + 1 <= row + 1 <= last - 1 and old is None:
+                old = load(rb, row + 1), load(hb, row + 1)
+            elif old is not None and row + 1 <= last - 1:
+                new = load(rb, row + 1), load(hb, row + 1)
+                pairs = pair(old[0], new[0]), pair(old[1], new[1])
+                old = new
+                if old_pairs is not None:
+                    nr = neighbours(old_pairs[0], pairs[0])
+                    nh = neighbours(old_pairs[1], pairs[1])
+                    src, con_row, r = spread(xcur, row), spread(xcon, row), load(rr, row)
+                    for j in range(nt):
+                        x = src[j] + nr[j]
+                        loss = (scale_of_loss * con_row[j] * r[j]) * (x * x + nh[j] * nh[j])
+                        totals = (totals or []) + [folds[j].add(loss)]
+                old_pairs = pairs
+            if totals is None:
+                totals = [fold.add(zero) for fold in folds]
+            if row % TILE == TILE - 1:
+                i = row // TILE
+                rows = slice(i * TILE, (i + 1) * TILE)
                 if group:
-                    total = qq[pl.ds(base, TILE), col] + total
-                qq[pl.ds(base, TILE), col] = total
-
-        loss_rows(0, range(TILE - MARGIN + 2, TILE))
-        loss_rows(bottom, range(MARGIN - 2))
-
-        def loss_body(i, carry):
-            loss_rows(pl.multiple_of(top + i * TILE, TILE), range(TILE))
-            return carry
-
-        lax.fori_loop(0, slab // TILE, loss_body, 0, unroll=True)
-
-    ntile = ext // TILE
-    q = [[qq[i * TILE : (i + 1) * TILE, j * LANES : (j + 1) * LANES] for j in range(nt)] for i in range(ntile)]
-
-    def hand_out(k, lines):
-        for i in range(1, ntile - 1):
-            for j, tile in enumerate(natural(lines[i], nt - 1)):
-                results[k, (i - 1) * TILE : i * TILE, j * LANES : (j + 1) * LANES] = tile
-        copy = pltpu.make_async_copy(results.at[k], (diss, heat)[k], sems.at[k])
-        copy.start()
-        return copy
-
-    first = hand_out(0, q)
-    rec = []
-    for i in range(ntile):
-        line = []
-        for j in range(nt):
-            w = 1.0 / (4.0 + xcoo[i * TILE : (i + 1) * TILE, j * LANES : (j + 1) * LANES])
-            if i == 0:
-                w = w * has_up
-            if i == ntile - 1:
-                w = w * has_down
-            line.append(w * inside[j])
-        rec.append(line)
-    t = [[q[i][j] * rec[i][j] for j in range(nt)] for i in range(ntile)]
-    for _ in range(3):
-        back = [[pltpu.roll(x, 1, 0) for x in line] for line in t]
-        fore = [[pltpu.roll(x, TILE - 1, 0) for x in line] for line in t]
-        new = []
-        for i in range(ntile):
-            mid = sides(t[i])
-            line = []
-            for j in range(nt):
-                above = jnp.where(sub == 0, back[i - 1][j], back[i][j])
-                below = jnp.where(sub == TILE - 1, fore[(i + 1) % ntile][j], fore[i][j])
-                line.append((q[i][j] + (mid[j] + (above + below))) * rec[i][j])
-            new.append(line)
-        t = new
-    second = hand_out(1, t)
-    first.wait()
-    second.wait()
+                    totals = [qq[rows, col] + total for col, total in zip(cols, totals)]
+                if group < groups - 1:
+                    for col, total in zip(cols, totals):
+                        qq[rows, col] = total
+                else:
+                    conduct(i, totals)
+            totals = None
+
+    for copy in copies:
+        copy.wait()
 
 
 def on_device(current_pattern, conductivity, cooling, harm_order, harm_amp, block_counts):
@@ -438,6 +448,8 @@
         return permute(value, lambda m, z, c: (m, z, 1 - c))
 
     def beside(m, z, c):
+        if m == (0 if c else mesh - 1):
+            return m, z, 1 - c
         return m + (1 - 2 * c), z, c
 
     known = jnp.maximum(params, swap(params))
@@ -487,8 +499,8 @@
         in_specs=[vmem] * 6,
         out_specs=(any_space,) * 2,
         scratch_shapes=[flat] * 3
-        + [deep] * 7
-        + [flat, pltpu.VMEM((2, slab, width), F32), pltpu.SemaphoreType.DMA((2,))],
+        + [deep] * 3
+        + [flat, pltpu.VMEM((2, slab, width), F32), pltpu.SemaphoreType.DMA((2, slab // TILE))],
         compiler_params=pltpu.CompilerParams(vmem_limit_bytes=12 * 2**20),
         name="losses",
     )(known, tile_cur, tile_con, tile_coo, got, far)

time: 15.9 us -> 15.4 us (0.969)
  waiting for transfers between devices: 1.48 us -> 1.16 us
    ppermute x5, waiting for transfers between devices: 1.48 us -> 1.16 us  [permute(): return lax.ppermute(value, axes, pairs)]
  transfers between devices with their start and end apart: 5 -> 5, of which waited for: 4 -> 2; matrix products, arithmetic and copies ran while one was open for 0% -> 0% of each run, Pallas kernels for 10% -> 10%
where the time goes in v5:
time: 15.4 us; the launch traced here: 15.2 us
  starting transfers between devices  7.79 us (51%)
  Pallas kernels  3.57 us (23%)
  between operations  2.67 us (17%)
  waiting for transfers between devices  1.16 us (8%)
    ppermute x5, starting transfers between devices, permute(): return lax.ppermute(value, axes, pairs)  7.79 us
    pallas_call x1, Pallas kernels, on_device(): pl.pallas_call(functools.partial(loss_kernel, width=width, harmonics=harm...  2.03 us
    ppermute x5, waiting for transfers between devices, permute(): return lax.ppermute(value, axes, pairs)  1.16 us
    pallas_call x1, Pallas kernels, on_device(): pl.pallas_call(functools.partial(pack_kernel, width=width), out_shape=hel...  1.01 us
    pallas_call x1, Pallas kernels, on_device(): pl.pallas_call(functools.partial(arrange_kernel, width=width), out_shape=...  0.52 us
  transfers between devices with their start and end apart: 5, of which 2 were waited for; matrix products, arithmetic and copies ran while one was open for 0% of the time, Pallas kernels for 10%

profile of v5, /device:TPU:0, one launch (start us, length us, event | category | flops | bytes accessed | tf_op | source)
XLA Modules:
  0.0 15.2 jit_solution(2856558208470852213)
XLA Ops:
  2.6 0.0 copy-start
  2.6 0.0 copy-start.1
  2.6 0.0 copy-start.2
  2.6 0.5 %collective-permute-start = (f32[8,128]{1,0:T(8,128)S(1)}, f32[8,128]{1,0:T(8,128)S(1)}, u32[]{:S(2)}, u32[]{:S(2)}) collective-permute-start(f32[8,128]{1,0:T(8,128)S(1)} %params.1.after), channel_id=1, source_target_pairs={{0,1},{1,0},{2,3},{3,2},{4,5},{5,4},{6,7},{7,6},{8,9},{9,8},{10,11... | collective-permute-start | bytes 12296 | tf_op jit(solution)/shard_map/ppermute | solution.py:445
  3.1 1.0 %pack.1 = f32[32,640]{1,0:T(8,128)S(1)} custom-call(f32[8,128]{1,0:T(8,128)S(1)} %params.1.after, f32[32,4096]{1,0:T(8,128)} %cur.3, f32[32,4096]{1,0:T(8,128)} %con.3, f32[32,4096]{1,0:T(8,128)} %coo.3), custom_call_target="tpu_custom_call" | custom-call | tf_op jit(solution)/shard_map/pack/pallas_call | solution.py:422
  4.2 0.0 collective-permute-done
  4.2 2.8 %collective-permute-start.1 = (f32[8,128]{1,0:T(8,128)S(1)}, f32[8,128]{1,0:T(8,128)S(1)}, u32[]{:S(2)}, u32[]{:S(2)}) collective-permute-start(f32[8,128]{1,0:T(8,128)S(1)} %max.10), channel_id=1, source_target_pairs={{0,2},{1,3},{2,0},{3,1},{4,6},{5,7},{6,4},{7,5},{8,10},{9,11},{10,... | collective-permute-start | bytes 12296 | tf_op jit(solution)/shard_map/ppermute | solution.py:445
  6.9 1.5 %collective-permute-start.2 = (f32[32,640]{1,0:T(8,128)S(1)}, f32[32,640]{1,0:T(8,128)S(1)}, u32[]{:S(2)}, u32[]{:S(2)}) collective-permute-start(f32[32,640]{1,0:T(8,128)S(1)} %pack.1), channel_id=1, source_target_pairs={{0,8},{1,0},{2,10},{3,2},{4,12},{5,4},{6,14},{7,6},{8,16},{9,1},{1... | collective-permute-start | bytes 245768 | tf_op jit(solution)/shard_map/ppermute | solution.py:445
  8.4 0.1 collective-permute-done.1
  8.5 3.0 %collective-permute-start.3 = (f32[8,256]{1,0:T(8,128)S(1)}, f32[8,256]{1,0:T(8,128)S(1)}, u32[]{:S(2)}, u32[]{:S(2)}) collective-permute-start(f32[8,256]{1,0:T(8,128)S(1)} %broadcast_bitcast_fusion), channel_id=1, source_target_pairs={{0,4},{1,5},{2,6},{3,7},{4,0},{5,1},{6,2},{7,3},{8,12},{9,13},{10,... | collective-permute-start | bytes 24584 | tf_op jit(solution)/shard_map/ppermute | solution.py:445
  11.6 0.0 collective-permute-done.2.got.near
  11.6 0.0 collective-permute-start.4
  11.6 0.0 copy-done
  11.6 0.0 copy-done.1
  11.6 0.0 copy-done.2
  11.6 0.5 %arrange.1 = (f32[32,640]{1,0:T(8,128)S(1)}, f32[32,640]{1,0:T(8,128)S(1)}, f32[32,640]{1,0:T(8,128)S(1)}) custom-call(f32[16,640]{1,0:T(8,128)S(1)} %pass_on.1.after, f32[32,4096]{1,0:T(8,128)S(1)} %copy-done, f32[32,4096]{1,0:T(8,128)S(1)} %copy-done.1, f32[32,4096]{1,0:T(8,128)S(1)} %copy-done.2), custom_call_target="tpu_custom_call" | custom-call | tf_op jit(solution)/shard_map/arrange/pallas_call | solution.py:478
  12.1 1.1 %collective-permute-done.3 = f32[8,256]{1,0:T(8,128)S(1)} collective-permute-done((f32[8,256]{1,0:T(8,128)S(1)}, f32[8,256]{1,0:T(8,128)S(1)}, u32[]{:S(2)}, u32[]{:S(2)}) %collective-permute-start.3) | collective-permute-done | bytes 8224 | tf_op jit(solution)/shard_map/ppermute | solution.py:445
  13.2 0.0 collective-permute-done.4.far
  13.2 2.0 %losses.1 = (f32[32,512]{1,0:T(8,128)}, f32[32,512]{1,0:T(8,128)}) custom-call(f32[8,128]{1,0:T(8,128)S(1)} %slice_maximum_fusion.par_ref, f32[32,640]{1,0:T(8,128)S(1)} %get-tuple-element.13.cur, f32[32,640]{1,0:T(8,128)S(1)} %get-tuple-element.14.con, f32[32,640]{1,0:T(8,128)S(1)} %get-tuple-element.15.coo, f32[32,640]{1,0:T(8,128)S(1)} %collective-permute-done.2.got.near, ...), custom_call_target="tpu_custom_call" | custom-call | tf_op jit(solution)/shard_map/losses/pallas_call | solution.py:496
  (6 shorter events, 0.0 us)
Async XLA Ops:
  2.6 9.0 %copy-start = (f32[32,4096]{1,0:T(8,128)S(1)}, f32[32,4096]{1,0:T(8,128)}, u32[]{:S(2)}) copy-start(f32[32,4096]{1,0:T(8,128)} %cur.3) | copy-start | bytes 1572868
  2.6 9.0 %copy-start.1 = (f32[32,4096]{1,0:T(8,128)S(1)}, f32[32,4096]{1,0:T(8,128)}, u32[]{:S(2)}) copy-start(f32[32,4096]{1,0:T(8,128)} %con.3) | copy-start | bytes 1572868
  2.6 9.0 %copy-start.2 = (f32[32,4096]{1,0:T(8,128)S(1)}, f32[32,4096]{1,0:T(8,128)}, u32[]{:S(2)}) copy-start(f32[32,4096]{1,0:T(8,128)} %coo.3) | copy-start | bytes 1572868
  2.6 1.5 %collective-permute-start = (f32[8,128]{1,0:T(8,128)S(1)}, f32[8,128]{1,0:T(8,128)S(1)}, u32[]{:S(2)}, u32[]{:S(2)}) collective-permute-start(f32[8,128]{1,0:T(8,128)S(1)} %params.1.after), channel_id=1, source_target_pairs={{0,1},{1,0},{2,3},{3,2},{4,5},{5,4},{6,7},{7,6},{8,9},{9,8},{10,11... | collective-permute-start | bytes 12296 | tf_op jit(solution)/shard_map/ppermute | solution.py:445
  4.2 4.3 %collective-permute-start.1 = (f32[8,128]{1,0:T(8,128)S(1)}, f32[8,128]{1,0:T(8,128)S(1)}, u32[]{:S(2)}, u32[]{:S(2)}) collective-permute-start(f32[8,128]{1,0:T(8,128)S(1)} %max.10), channel_id=1, source_target_pairs={{0,2},{1,3},{2,0},{3,1},{4,6},{5,7},{6,4},{7,5},{8,10},{9,11},{10,... | collective-permute-start | bytes 12296 | tf_op jit(solution)/shard_map/ppermute | solution.py:445
  6.9 4.6 %collective-permute-start.2 = (f32[32,640]{1,0:T(8,128)S(1)}, f32[32,640]{1,0:T(8,128)S(1)}, u32[]{:S(2)}, u32[]{:S(2)}) collective-permute-start(f32[32,640]{1,0:T(8,128)S(1)} %pack.1), channel_id=1, source_target_pairs={{0,8},{1,0},{2,10},{3,2},{4,12},{5,4},{6,14},{7,6},{8,16},{9,1},{1... | collective-permute-start | bytes 245768 | tf_op jit(solution)/shard_map/ppermute | solution.py:445
  8.5 4.7 %collective-permute-start.3 = (f32[8,256]{1,0:T(8,128)S(1)}, f32[8,256]{1,0:T(8,128)S(1)}, u32[]{:S(2)}, u32[]{:S(2)}) collective-permute-start(f32[8,256]{1,0:T(8,128)S(1)} %broadcast_bitcast_fusion), channel_id=1, source_target_pairs={{0,4},{1,5},{2,6},{3,7},{4,0},{5,1},{6,2},{7,3},{8,12},{9,13},{10,... | collective-permute-start | bytes 24584 | tf_op jit(solution)/shard_map/ppermute | solution.py:445
  11.6 1.6 %collective-permute-start.4 = (f32[16,640]{1,0:T(8,128)S(1)}, f32[16,640]{1,0:T(8,128)S(1)}, u32[]{:S(2)}, u32[]{:S(2)}) collective-permute-start(f32[16,640]{1,0:T(8,128)S(1)} %pass_on.1.after), channel_id=1, source_target_pairs={{0,1},{1,0},{2,3},{3,2},{4,5},{5,4},{6,7},{7,6},{8,9},{9,8},{10,11... | collective-permute-start | bytes 122888 | tf_op jit(solution)/shard_map/ppermute | solution.py:445

commit v6 on v5

--- a/solution.py
+++ b/solution.py
@@ -136,12 +136,15 @@
                 for j in range(width // LANES)
             ]
             tiles.append(side_tile(buf.at[i], slice(0, TILE), left, right))
-            fields.append(columns.interleave(tiles))
-        base = part * 2 * TILE
-        for j, (a, b, c) in enumerate(zip(*fields)):
-            at = slice(j * LANES, (j + 1) * LANES)
-            out[base : base + TILE, at] = jnp.where(take_cur, a, pltpu.roll(c, shift, 0))
-            out[base + TILE : base + 2 * TILE, at] = b
+            fields.append(tiles)
+        joined = [
+            jnp.where(take_cur, a, pltpu.roll(c, shift, 0))
+            for a, c in zip(fields[0], fields[2])
+        ]
+        for i, tiles in enumerate((joined, fields[1])):
+            rows = slice((2 * part + i) * TILE, (2 * part + i + 1) * TILE)
+            for j, tile in enumerate(columns.interleave(tiles)):
+                out[rows, j * LANES : (j + 1) * LANES] = tile
 
 
 def arrange_kernel(after, cur, con, coo, cur_out, con_out, coo_out, held, sems, *, width):
@@ -199,200 +202,253 @@
         return value
 
 
+def load(ref, row, nt):
+    return [ref[row, :, j * LANES : (j + 1) * LANES] for j in range(nt)]
+
+
+def store(ref, row, tiles):
+    for j, tile in enumerate(tiles):
+        ref[row, :, j * LANES : (j + 1) * LANES] = tile
+
+
+def spread(ref, row, nt):
+    return [
+        jnp.broadcast_to(ref[row : row + 1, j * LANES : (j + 1) * LANES], (TILE, LANES))
+        for j in range(nt)
+    ]
+
+
+def pair(here, below):
+    below = [*below[1:], pltpu.roll(below[0], LANES - 1, 1)]
+    return [a + b for a, b in zip(here, below)]
+
+
+def neighbours(above, here):
+    here = [pltpu.roll(here[-1], 1, 1), *here[:-1]]
+    return [a + b for a, b in zip(above, here)]
+
+
+class Place:
+    def __init__(self, width):
+        self.width, self.nt = width, width // LANES + 1
+        self.h, m = lax.axis_index("harm"), lax.axis_index("mesh")
+        self.has_up = (m > 0).astype(F32)
+        self.has_down = (m < lax.axis_size("mesh") - 1).astype(F32)
+        has_left = (self.h > 0).astype(F32)
+        has_right = (self.h < lax.axis_size("harm") - 1).astype(F32)
+        self.order_of = Columns(self.nt)
+        self.inside = [
+            jnp.where(c < width, 1.0, jnp.where(c < width + HALF, has_right, has_left))
+            for c in self.order_of.columns
+        ]
+
+    def first_block(self, j):
+        c = self.order_of.columns[j]
+        block = jnp.where(c < self.width + HALF, c // LANES, -1)
+        return (block + self.h * (self.width // LANES)).astype(F32)
+
+    def edges(self, near, far, put):
+        core = lax.rem(self.h, 2)
+
+        @pl.when(core == 0)
+        def _():
+            put(near, far)
+
+        @pl.when(core == 1)
+        def _():
+            put(far, near)
+
+
+def eddy(place, par, harmonics, start, count_rows, source, conductivity, valid, rr, rb, hb, loss_out):
+    nt = place.nt
+    order, amp, count = [
+        jnp.broadcast_to(par[:, k : k + 1], (TILE, LANES)) for k in range(3)
+    ]
+    omega = BASE_FREQ * order
+    quarter = 0.25 * omega
+    scale_of_loss = (0.5 / harmonics) * quarter * omega * amp * amp
+    masks = [
+        jnp.where(count > place.first_block(j), 0.25 * place.inside[j], 0.0)
+        for j in range(nt)
+    ]
+    scaled = {None: masks}
+
+    old = old_pairs = None
+    if start:
+        zeros = [jnp.zeros((TILE, LANES), F32)] * nt
+        store(rb, start - 1, zeros)
+        store(hb, start - 1, zeros)
+        old = zeros, zeros
+    for row in range(start, count_rows):
+        name, factor = valid(row)
+        if name not in scaled:
+            scaled[name] = [k * factor for k in masks]
+        src = source(row)
+        g = [quarter * x for x in conductivity(row)]
+        r = [
+            pl.reciprocal(1.0 + x * x, approx=True) * k for x, k in zip(g, scaled[name])
+        ]
+        re = [a * b for a, b in zip(src, r)]
+        him = [a * b for a, b in zip(g, re)]
+        if 2 <= row < count_rows - 2:
+            store(rr, row, r)
+        if old is not None:
+            pairs = pair(old[0], re), pair(old[1], him)
+            if old_pairs is not None:
+                nr = neighbours(old_pairs[0], pairs[0])
+                nh = neighbours(old_pairs[1], pairs[1])
+                x = [a + b for a, b in zip(old[4], nr)]
+                store(rb, row - 1, [k * (a - b * c) for k, a, b, c in zip(old[2], x, old[3], nh)])
+                store(hb, row - 1, [k * (b * a + c) for k, a, b, c in zip(old[2], x, old[3], nh)])
+            old_pairs = pairs
+        old = re, him, r, g, src
+
+    begin = max(start - 1, 1)
+    old, old_pairs = (load(rb, begin, nt), load(hb, begin, nt)), None
+    for row in range(begin, count_rows - 2):
+        new = load(rb, row + 1, nt), load(hb, row + 1, nt)
+        pairs = pair(old[0], new[0]), pair(old[1], new[1])
+        old = new
+        if old_pairs is not None:
+            nr = neighbours(old_pairs[0], pairs[0])
+            nh = neighbours(old_pairs[1], pairs[1])
+            src, con, r = source(row), conductivity(row), load(rr, row, nt)
+            losses = []
+            for j in range(nt):
+                x = src[j] + nr[j]
+                losses.append(
+                    (scale_of_loss * con[j] * r[j]) * (x * x + nh[j] * nh[j])
+                )
+            loss_out(row, losses)
+        old_pairs = pairs
+
+
 def loss_kernel(
-    par_ref, cur, con, coo, near, far, diss, heat,
+    table, cur, con, coo, near, far, diss, heat,
     xcur, xcon, xcoo, rr, rb, hb, qq, results, sems, *, width, harmonics,
 ):
-    slab = cur.shape[0]
-    nt = width // LANES + 1
+    slab = coo.shape[0]
     top, bottom = TILE, TILE + slab
     ext = slab + 2 * TILE
-    h = lax.axis_index("harm")
-    m = lax.axis_index("mesh")
-    last_h = lax.axis_size("harm") - 1
-    last_m = lax.axis_size("mesh") - 1
-    core = lax.rem(h, 2)
-    lanes, sub = lane_iota(), sublane_iota()
+    place, nt, sub = Place(width), width // LANES + 1, sublane_iota()
     cols = [slice(j * LANES, (j + 1) * LANES) for j in range(nt)]
     xcur[top:bottom, :] = cur[...]
     xcon[top:bottom, :] = con[...]
     xcoo[top:bottom, :] = coo[...]
 
-    def edges(up, down):
+    def put(up, down):
         xcur[0:TILE, :] = up[:TILE, :]
         xcon[0:TILE, :] = up[TILE : 2 * TILE, :]
-        xcoo[0:TILE, :] = pltpu.roll(up[:TILE, :], TILE - 3, 0)
+        xcoo[0:TILE, :] = jnp.maximum(pltpu.roll(up[:TILE, :], TILE - 3, 0), 0.0)
         xcur[bottom:ext, :] = down[:TILE, :]
         xcon[bottom:ext, :] = down[TILE : 2 * TILE, :]
-        xcoo[bottom:ext, :] = pltpu.roll(down[:TILE, :], TILE - 5, 0)
-
-    @pl.when(core == 0)
-    def _():
-        edges(near, far)
-
-    @pl.when(core == 1)
-    def _():
-        edges(far, near)
-
-    has_up = (m > 0).astype(F32)
-    has_down = (m < last_m).astype(F32)
-    has_left = (h > 0).astype(F32)
-    has_right = (h < last_h).astype(F32)
-    order_of = Columns(nt)
-    columns = order_of.columns
-    inside = [
-        jnp.where(c < width, 1.0, jnp.where(c < width + HALF, has_right, has_left))
-        for c in columns
-    ]
-
-    def first_block(j):
-        block = jnp.where(columns[j] < width + HALF, columns[j] // LANES, -1)
-        return (block + h * (width // LANES)).astype(F32)
-
-
-    ntile = ext // TILE
-    losses, weights, levels, copies = [], [], [[], [], [], []], []
-
-    def hand_out(k, i, tiles):
-        rows = slice((i - 1) * TILE, i * TILE)
-        for col, tile in zip(cols, order_of.natural(tiles, nt - 1)):
-            results[k, rows, col] = tile
-        copy = pltpu.make_async_copy(
-            results.at[k, rows, :], (diss, heat)[k].at[rows, :], sems.at[k, i - 1]
-        )
-        copy.start()
-        copies.append(copy)
-
-    def sweep(i, before):
-        rolled = lambda k, shift: [pltpu.roll(x, shift, 0) for x in before[k]]
-        above, below = rolled(i, 1), rolled(i, TILE - 1)
-        if i > 0:
-            above = [jnp.where(sub == 0, p, x) for p, x in zip(rolled(i - 1, 1), above)]
-        if i < ntile - 1:
-            below = [jnp.where(sub == TILE - 1, p, x) for p, x in zip(rolled(i + 1, TILE - 1), below)]
-        return [
-            (q + (x + (a + b))) * w
-            for q, x, a, b, w in zip(losses[i], sides(before[i]), above, below, weights[i])
-        ]
-
-    def conduct(i, q):
-        losses.append(q)
-        scale = has_up if i == 0 else has_down if i == ntile - 1 else None
-        w = [
-            pl.reciprocal(4.0 + xcoo[i * TILE : (i + 1) * TILE, col], approx=True) * x
-            for col, x in zip(cols, inside)
-        ]
-        weights.append(w if scale is None else [x * scale for x in w])
-        levels[0].append([a * b for a, b in zip(q, weights[i])])
-        if 0 < i < ntile - 1:
-            hand_out(0, i, q)
-        for k in range(1, 4):
-            ready = [i - k] if i < ntile - 1 else list(range(max(i - k, 0), ntile))
-            for at in ready:
-                if at >= 0:
-                    outer = at in (0, ntile - 1)
-                    levels[k].append(None if k == 3 and outer else sweep(at, levels[k - 1]))
-                    if k == 3 and not outer:
-                        hand_out(1, at, levels[3][at])
-
-    groups = (harmonics + TILE - 1) // TILE
-    for group in range(groups):
-        at = slice(group * TILE, (group + 1) * TILE)
-        par = par_ref[at, :]
-        order = jnp.broadcast_to(par[:, 0:1], (TILE, LANES))
-        amp = jnp.broadcast_to(par[:, 1:2], (TILE, LANES))
-        count = jnp.broadcast_to(par[:, 2:3], (TILE, LANES))
-        omega = BASE_FREQ * order
-        quarter = 0.25 * omega
-        scale_of_loss = (0.5 / harmonics) * quarter * omega * amp * amp
+        xcoo[bottom:ext, :] = jnp.maximum(pltpu.roll(down[:TILE, :], TILE - 5, 0), 0.0)
+
+    place.edges(near, far, put)
+
+    def run(start):
+        ntile = ext // TILE
+        losses, weights, levels, copies = [], [], [[], [], [], []], []
+        if start:
+            nothing = [jnp.zeros((TILE, LANES), F32)] * nt
+            losses.append(nothing)
+            weights.append(nothing)
+            for level in levels:
+                level.append(nothing)
+
+        def hand_out(k, i, tiles):
+            rows = slice((i - 1) * TILE, i * TILE)
+            for col, tile in zip(cols, place.order_of.natural(tiles, nt - 1)):
+                results[k, rows, col] = tile
+            copy = pltpu.make_async_copy(
+                results.at[k, rows, :], (diss, heat)[k].at[rows, :], sems.at[k, i - 1]
+            )
+            copy.start()
+            copies.append(copy)
+
+        def sweep(i, before):
+            above = [
+                pltpu.roll(jnp.where(sub == TILE - 1, p, x), 1, 0)
+                for p, x in zip(before[max(i - 1, 0)], before[i])
+            ]
+            below = [
+                pltpu.roll(jnp.where(sub == 0, p, x), TILE - 1, 0)
+                for p, x in zip(before[min(i + 1, ntile - 1)], before[i])
+            ]
+            return [
+                (q + (x + (a + b))) * w
+                for q, x, a, b, w in zip(losses[i], sides(before[i]), above, below, weights[i])
+            ]
+
+        def conduct(i, q):
+            losses.append(q)
+            scale = place.has_up if i == 0 else place.has_down if i == ntile - 1 else None
+            w = [
+                pl.reciprocal(4.0 + xcoo[i * TILE : (i + 1) * TILE, col], approx=True) * x
+                for col, x in zip(cols, place.inside)
+            ]
+            weights.append(w if scale is None else [x * scale for x in w])
+            levels[0].append([a * b for a, b in zip(q, weights[i])])
+            if 0 < i < ntile - 1:
+                hand_out(0, i, q)
+            for k in range(1, 4):
+                ready = [i - k] if i < ntile - 1 else range(i - k, ntile)
+                for at in ready:
+                    if at >= (1 if start else 0):
+                        outer = at in (0, ntile - 1)
+                        levels[k].append(None if k == 3 and outer else sweep(at, levels[k - 1]))
+                        if k == 3 and not outer:
+                            hand_out(1, at, levels[3][at])
+
         zero = jnp.zeros((TILE, LANES), F32)
-        masks = [
-            jnp.where(count > first_block(j), 0.25 * inside[j], 0.0) for j in range(nt)
-        ]
-
-        def spread(ref, row):
-            return [
-                jnp.broadcast_to(ref[row : row + 1, j * LANES : (j + 1) * LANES], (TILE, LANES))
-                for j in range(nt)
-            ]
-
-        def load(ref, row):
-            return [ref[row, :, j * LANES : (j + 1) * LANES] for j in range(nt)]
-
-        def store(ref, row, tiles):
-            for j, tile in enumerate(tiles):
-                ref[row, :, j * LANES : (j + 1) * LANES] = tile
-
-        def pair(here, below):
-            below = [*below[1:], pltpu.roll(below[0], LANES - 1, 1)]
-            return [a + b for a, b in zip(here, below)]
-
-        def neighbours(above, here):
-            here = [pltpu.roll(here[-1], 1, 1), *here[:-1]]
-            return [a + b for a, b in zip(above, here)]
-
-        def slope(row):
-            return [quarter * x for x in spread(xcon, row)]
-
-        first, last = top - MARGIN, bottom + MARGIN - 1
-        up = [k * has_up for k in masks]
-        down = [k * has_down for k in masks]
-        old = old_pairs = None
-        for row in range(first, last + 1):
-            scale = up if row < top else down if row >= bottom else masks
-            src, g = spread(xcur, row), slope(row)
-            r = [
-                pl.reciprocal(1.0 + x * x, approx=True) * k for x, k in zip(g, scale)
-            ]
-            re = [a * b for a, b in zip(src, r)]
-            him = [a * b for a, b in zip(g, re)]
-            if first + 2 <= row <= last - 2:
-                store(rr, row, r)
-            if old is not None:
-                pairs = pair(old[0], re), pair(old[1], him)
-                if old_pairs is not None:
-                    nr = neighbours(old_pairs[0], pairs[0])
-                    nh = neighbours(old_pairs[1], pairs[1])
-                    x = [a + b for a, b in zip(old[4], nr)]
-                    store(rb, row - 1, [k * (a - b * c) for k, a, b, c in zip(old[2], x, old[3], nh)])
-                    store(hb, row - 1, [k * (b * a + c) for k, a, b, c in zip(old[2], x, old[3], nh)])
-                old_pairs = pairs
-            old = re, him, r, g, src
-
-        old = old_pairs = None
-        folds, totals = [Fold(sub) for _ in range(nt)], None
-        for row in range(ext):
-            if first + 1 <= row + 1 <= last - 1 and old is None:
-                old = load(rb, row + 1), load(hb, row + 1)
-            elif old is not None and row + 1 <= last - 1:
-                new = load(rb, row + 1), load(hb, row + 1)
-                pairs = pair(old[0], new[0]), pair(old[1], new[1])
-                old = new
-                if old_pairs is not None:
-                    nr = neighbours(old_pairs[0], pairs[0])
-                    nh = neighbours(old_pairs[1], pairs[1])
-                    src, con_row, r = spread(xcur, row), spread(xcon, row), load(rr, row)
-                    for j in range(nt):
-                        x = src[j] + nr[j]
-                        loss = (scale_of_loss * con_row[j] * r[j]) * (x * x + nh[j] * nh[j])
-                        totals = (totals or []) + [folds[j].add(loss)]
-                old_pairs = pairs
-            if totals is None:
-                totals = [fold.add(zero) for fold in folds]
-            if row % TILE == TILE - 1:
-                i = row // TILE
+        groups = (harmonics + TILE - 1) // TILE
+        first = top - MARGIN
+
+        def valid(row):
+            if row < MARGIN:
+                return "up", place.has_up
+            if row >= MARGIN + slab:
+                return "down", place.has_down
+            return None, None
+
+        for group in range(groups):
+            folds = [Fold(sub) for _ in range(nt)]
+
+            def add(row, values):
+                totals = [fold.add(x) for fold, x in zip(folds, values)]
+                i, at = divmod(row + first, TILE)
+                if at < TILE - 1:
+                    return
                 rows = slice(i * TILE, (i + 1) * TILE)
                 if group:
-                    totals = [qq[rows, col] + total for col, total in zip(cols, totals)]
-                if group < groups - 1:
-                    for col, total in zip(cols, totals):
-                        qq[rows, col] = total
+                    totals = [qq[rows, col] + x for col, x in zip(cols, totals)]
+                if group == groups - 1:
+                    conduct(i, totals)
                 else:
-                    conduct(i, totals)
-            totals = None
-
-    for copy in copies:
-        copy.wait()
+                    for col, x in zip(cols, totals):
+                        qq[rows, col] = x
+
+            if not start:
+                for row in range(-first, 2):
+                    add(row, [zero] * nt)
+            eddy(
+                place, table[group * TILE : (group + 1) * TILE, :], harmonics, start, slab + 2 * MARGIN,
+                lambda row: spread(xcur, row + first, nt), lambda row: spread(xcon, row + first, nt),
+                valid, rr, rb, hb, add,
+            )
+            for row in range(slab + 2 * MARGIN - 2, ext - first):
+                add(row, [zero] * nt)
+
+        for copy in copies:
+            copy.wait()
+
+    @pl.when(lax.axis_index("mesh") == 0)
+    def _():
+        run(MARGIN)
+
+    @pl.when(lax.axis_index("mesh") > 0)
+    def _():
+        run(0)
 
 
 def on_device(current_pattern, conductivity, cooling, harm_order, harm_amp, block_counts):
@@ -488,11 +544,11 @@
         name="arrange",
     )(passed, *fields)
 
+    ext = slab + 2 * TILE
+    flat = pltpu.VMEM((ext, wide), F32)
+    deep = pltpu.VMEM((slab + 2 * MARGIN, TILE, wide), F32)
     before, tile_cur = lax.optimization_barrier((before, tile_cur))
     known = jnp.maximum(before, last)
-    ext = slab + 2 * TILE
-    flat = pltpu.VMEM((ext, wide), F32)
-    deep = pltpu.VMEM((ext, TILE, wide), F32)
     return pl.pallas_call(
         functools.partial(loss_kernel, width=width, harmonics=harm),
         out_shape=(shape(slab, width),) * 2,

time: 15.4 us -> 15.2 us (0.987)
  Pallas kernels: 3.57 us -> 3.4 us
where the time goes in v6:
time: 15.2 us; the launch traced here: 15 us
  starting transfers between devices  7.79 us (51%)
  Pallas kernels  3.4 us (22%)
  between operations  2.67 us (18%)
  waiting for transfers between devices  1.16 us (8%)
    ppermute x5, starting transfers between devices, permute(): return lax.ppermute(value, axes, pairs)  7.79 us
    pallas_call x1, Pallas kernels, on_device(): pl.pallas_call(functools.partial(loss_kernel, width=width, harmonics=harm...  1.89 us
    ppermute x5, waiting for transfers between devices, permute(): return lax.ppermute(value, axes, pairs)  1.16 us
    pallas_call x1, Pallas kernels, on_device(): pl.pallas_call(functools.partial(pack_kernel, width=width), out_shape=hel...  0.98 us
    pallas_call x1, Pallas kernels, on_device(): pl.pallas_call(functools.partial(arrange_kernel, width=width), out_shape=...  0.52 us
  transfers between devices with their start and end apart: 5, of which 2 were waited for; matrix products, arithmetic and copies ran while one was open for 0% of the time, Pallas kernels for 10%

profile of v6, /device:TPU:0, one launch (start us, length us, event | category | flops | bytes accessed | tf_op | source)
XLA Modules:
  0.0 15.0 jit_solution(4793261953813984082)
XLA Ops:
  2.6 0.0 copy-start
  2.6 0.0 copy-start.1
  2.6 0.0 copy-start.2
  2.6 0.5 %collective-permute-start = (f32[8,128]{1,0:T(8,128)S(1)}, f32[8,128]{1,0:T(8,128)S(1)}, u32[]{:S(2)}, u32[]{:S(2)}) collective-permute-start(f32[8,128]{1,0:T(8,128)S(1)} %params.1.after), channel_id=1, source_target_pairs={{0,1},{1,0},{2,3},{3,2},{4,5},{5,4},{6,7},{7,6},{8,9},{9,8},{10,11... | collective-permute-start | bytes 12296 | tf_op jit(solution)/shard_map/ppermute | solution.py:501
  3.1 1.0 %pack.1 = f32[32,640]{1,0:T(8,128)S(1)} custom-call(f32[8,128]{1,0:T(8,128)S(1)} %params.1.after, f32[32,4096]{1,0:T(8,128)} %cur.3, f32[32,4096]{1,0:T(8,128)} %con.3, f32[32,4096]{1,0:T(8,128)} %coo.3), custom_call_target="tpu_custom_call" | custom-call | tf_op jit(solution)/shard_map/pack/pallas_call | solution.py:478
  4.1 0.0 collective-permute-done
  4.1 2.8 %collective-permute-start.1 = (f32[8,128]{1,0:T(8,128)S(1)}, f32[8,128]{1,0:T(8,128)S(1)}, u32[]{:S(2)}, u32[]{:S(2)}) collective-permute-start(f32[8,128]{1,0:T(8,128)S(1)} %max.10), channel_id=1, source_target_pairs={{0,2},{1,3},{2,0},{3,1},{4,6},{5,7},{6,4},{7,5},{8,10},{9,11},{10,... | collective-permute-start | bytes 12296 | tf_op jit(solution)/shard_map/ppermute | solution.py:501
  6.9 1.5 %collective-permute-start.2 = (f32[32,640]{1,0:T(8,128)S(1)}, f32[32,640]{1,0:T(8,128)S(1)}, u32[]{:S(2)}, u32[]{:S(2)}) collective-permute-start(f32[32,640]{1,0:T(8,128)S(1)} %pack.1), channel_id=1, source_target_pairs={{0,8},{1,0},{2,10},{3,2},{4,12},{5,4},{6,14},{7,6},{8,16},{9,1},{1... | collective-permute-start | bytes 245768 | tf_op jit(solution)/shard_map/ppermute | solution.py:501
  8.4 0.1 collective-permute-done.1
  8.5 3.0 %collective-permute-start.3 = (f32[8,256]{1,0:T(8,128)S(1)}, f32[8,256]{1,0:T(8,128)S(1)}, u32[]{:S(2)}, u32[]{:S(2)}) collective-permute-start(f32[8,256]{1,0:T(8,128)S(1)} %broadcast_bitcast_fusion), channel_id=1, source_target_pairs={{0,4},{1,5},{2,6},{3,7},{4,0},{5,1},{6,2},{7,3},{8,12},{9,13},{10,... | collective-permute-start | bytes 24584 | tf_op jit(solution)/shard_map/ppermute | solution.py:501
  11.5 0.0 collective-permute-done.2.got.near
  11.5 0.0 collective-permute-start.4
  11.5 0.0 copy-done
  11.6 0.0 copy-done.1
  11.6 0.0 copy-done.2
  11.6 0.5 %arrange.1 = (f32[32,640]{1,0:T(8,128)S(1)}, f32[32,640]{1,0:T(8,128)S(1)}, f32[32,640]{1,0:T(8,128)S(1)}) custom-call(f32[16,640]{1,0:T(8,128)S(1)} %pass_on.1.after, f32[32,4096]{1,0:T(8,128)S(1)} %copy-done, f32[32,4096]{1,0:T(8,128)S(1)} %copy-done.1, f32[32,4096]{1,0:T(8,128)S(1)} %copy-done.2), custom_call_target="tpu_custom_call" | custom-call | tf_op jit(solution)/shard_map/arrange/pallas_call | solution.py:534
  12.1 1.1 %collective-permute-done.3 = f32[8,256]{1,0:T(8,128)S(1)} collective-permute-done((f32[8,256]{1,0:T(8,128)S(1)}, f32[8,256]{1,0:T(8,128)S(1)}, u32[]{:S(2)}, u32[]{:S(2)}) %collective-permute-start.3) | collective-permute-done | bytes 8224 | tf_op jit(solution)/shard_map/ppermute | solution.py:501
  13.2 0.0 collective-permute-done.4.far
  13.2 1.9 %losses.1 = (f32[32,512]{1,0:T(8,128)}, f32[32,512]{1,0:T(8,128)}) custom-call(f32[8,128]{1,0:T(8,128)S(1)} %slice_maximum_fusion.table, f32[32,640]{1,0:T(8,128)S(1)} %get-tuple-element.13.cur, f32[32,640]{1,0:T(8,128)S(1)} %get-tuple-element.14.con, f32[32,640]{1,0:T(8,128)S(1)} %get-tuple-element.15.coo, f32[32,640]{1,0:T(8,128)S(1)} %collective-permute-done.2.got.near, ...), custom_call_target="tpu_custom_call" | custom-call | tf_op jit(solution)/shard_map/losses/pallas_call | solution.py:552
  (6 shorter events, 0.0 us)
Async XLA Ops:
  2.6 9.0 %copy-start = (f32[32,4096]{1,0:T(8,128)S(1)}, f32[32,4096]{1,0:T(8,128)}, u32[]{:S(2)}) copy-start(f32[32,4096]{1,0:T(8,128)} %cur.3) | copy-start | bytes 1572868
  2.6 9.0 %copy-start.1 = (f32[32,4096]{1,0:T(8,128)S(1)}, f32[32,4096]{1,0:T(8,128)}, u32[]{:S(2)}) copy-start(f32[32,4096]{1,0:T(8,128)} %con.3) | copy-start | bytes 1572868
  2.6 9.0 %copy-start.2 = (f32[32,4096]{1,0:T(8,128)S(1)}, f32[32,4096]{1,0:T(8,128)}, u32[]{:S(2)}) copy-start(f32[32,4096]{1,0:T(8,128)} %coo.3) | copy-start | bytes 1572868
  2.6 1.5 %collective-permute-start = (f32[8,128]{1,0:T(8,128)S(1)}, f32[8,128]{1,0:T(8,128)S(1)}, u32[]{:S(2)}, u32[]{:S(2)}) collective-permute-start(f32[8,128]{1,0:T(8,128)S(1)} %params.1.after), channel_id=1, source_target_pairs={{0,1},{1,0},{2,3},{3,2},{4,5},{5,4},{6,7},{7,6},{8,9},{9,8},{10,11... | collective-permute-start | bytes 12296 | tf_op jit(solution)/shard_map/ppermute | solution.py:501
  4.1 4.3 %collective-permute-start.1 = (f32[8,128]{1,0:T(8,128)S(1)}, f32[8,128]{1,0:T(8,128)S(1)}, u32[]{:S(2)}, u32[]{:S(2)}) collective-permute-start(f32[8,128]{1,0:T(8,128)S(1)} %max.10), channel_id=1, source_target_pairs={{0,2},{1,3},{2,0},{3,1},{4,6},{5,7},{6,4},{7,5},{8,10},{9,11},{10,... | collective-permute-start | bytes 12296 | tf_op jit(solution)/shard_map/ppermute | solution.py:501
  6.9 4.6 %collective-permute-start.2 = (f32[32,640]{1,0:T(8,128)S(1)}, f32[32,640]{1,0:T(8,128)S(1)}, u32[]{:S(2)}, u32[]{:S(2)}) collective-permute-start(f32[32,640]{1,0:T(8,128)S(1)} %pack.1), channel_id=1, source_target_pairs={{0,8},{1,0},{2,10},{3,2},{4,12},{5,4},{6,14},{7,6},{8,16},{9,1},{1... | collective-permute-start | bytes 245768 | tf_op jit(solution)/shard_map/ppermute | solution.py:501
  8.5 4.7 %collective-permute-start.3 = (f32[8,256]{1,0:T(8,128)S(1)}, f32[8,256]{1,0:T(8,128)S(1)}, u32[]{:S(2)}, u32[]{:S(2)}) collective-permute-start(f32[8,256]{1,0:T(8,128)S(1)} %broadcast_bitcast_fusion), channel_id=1, source_target_pairs={{0,4},{1,5},{2,6},{3,7},{4,0},{5,1},{6,2},{7,3},{8,12},{9,13},{10,... | collective-permute-start | bytes 24584 | tf_op jit(solution)/shard_map/ppermute | solution.py:501
  11.5 1.6 %collective-permute-start.4 = (f32[16,640]{1,0:T(8,128)S(1)}, f32[16,640]{1,0:T(8,128)S(1)}, u32[]{:S(2)}, u32[]{:S(2)}) collective-permute-start(f32[16,640]{1,0:T(8,128)S(1)} %pass_on.1.after), channel_id=1, source_target_pairs={{0,1},{1,0},{2,3},{3,2},{4,5},{5,4},{6,7},{7,6},{8,9},{9,8},{10,11... | collective-permute-start | bytes 122888 | tf_op jit(solution)/shard_map/ppermute | solution.py:501

commit v7 on v6

--- a/solution.py
+++ b/solution.py
@@ -92,14 +92,23 @@
     return pl.multiple_of(begin, LANES)
 
 
-def params_kernel(order, amp, count, params):
+def table_rows(harmonics):
+    return 1 if 3 * harmonics <= LANES else 3
+
+
+def table_place(k, harmonics):
+    return (0, k * harmonics) if table_rows(harmonics) == 1 else (k, 0)
+
+
+def params_kernel(order, amp, count, params, *, harmonics):
     h = lax.axis_index("harm")
     rows = lax.broadcasted_iota(jnp.int32, params.shape, 0)
     lanes = lax.broadcasted_iota(jnp.int32, params.shape, 1)
-    value = jnp.where(
-        lanes == 0, order[0], jnp.where(lanes == 1, amp[0], count[0])
-    ).astype(F32)
-    params[...] = jnp.where((rows == h) & (lanes < 3), value, 0.0)
+    value = jnp.zeros(params.shape, jnp.int32)
+    for k, ref in enumerate((order, amp, count)):
+        row, lane = table_place(k, harmonics)
+        value = jnp.where((rows == row) & (lanes == lane + h), ref[0], value)
+    params[...] = value.astype(F32)
 
 
 def pack_kernel(after, cur, con, coo, out, buf, sems, *, width):
@@ -261,8 +270,13 @@
 
 def eddy(place, par, harmonics, start, count_rows, source, conductivity, valid, rr, rb, hb, loss_out):
     nt = place.nt
+    table, group = par
     order, amp, count = [
-        jnp.broadcast_to(par[:, k : k + 1], (TILE, LANES)) for k in range(3)
+        lane_gather(
+            jnp.broadcast_to(table[row : row + 1, :], (TILE, LANES)),
+            lane + group * TILE + sublane_iota(),
+        )
+        for row, lane in (table_place(k, harmonics) for k in range(3))
     ]
     omega = BASE_FREQ * order
     quarter = 0.25 * omega
@@ -432,7 +446,7 @@
                 for row in range(-first, 2):
                     add(row, [zero] * nt)
             eddy(
-                place, table[group * TILE : (group + 1) * TILE, :], harmonics, start, slab + 2 * MARGIN,
+                place, (table, group), harmonics, start, slab + 2 * MARGIN,
                 lambda row: spread(xcur, row + first, nt), lambda row: spread(xcon, row + first, nt),
                 valid, rr, rb, hb, add,
             )
@@ -457,7 +471,6 @@
     width = total // harm
     wide = width + LANES
     chips = harm // 2
-    held = -(-harm // TILE) * TILE
     any_space = pl.BlockSpec(memory_space=pl.ANY)
     vmem = pl.BlockSpec(memory_space=pltpu.VMEM)
     smem = pl.BlockSpec(memory_space=pltpu.SMEM)
@@ -468,8 +481,8 @@
     in_hbm = lambda x: pltpu.with_memory_space_constraint(x, pltpu.HBM)
     held_vmem = lambda *s: pltpu.VMEM(s, F32)
     params = pl.pallas_call(
-        params_kernel,
-        out_shape=held_vmem(held, LANES),
+        functools.partial(params_kernel, harmonics=harm),
+        out_shape=held_vmem(table_rows(harm), LANES),
         in_specs=[smem] * 3,
         out_specs=vmem,
         compiler_params=small,
@@ -518,7 +531,7 @@
         before = jnp.maximum(before, last)
         if power:
             table = before
-        sent = jnp.tile(table, (1, 2)) if i else table
+        sent = jnp.tile(table, (1, 12)) if i else table
         hop = lambda m, z, c: (m, z ^ step if power else z + step, c)
         last = permute(sent, hop)[:, :LANES]
     passed = pl.pallas_call(

time: 15.2 us -> 15.2 us (level)
  transfers between devices with their start and end apart: 5 -> 5, of which waited for: 2 -> 1; matrix products, arithmetic and copies ran while one was open for 0% -> 0% of each run, Pallas kernels for 10% -> 10%
where the time goes in v7:
time: 15.2 us; the launch traced here: 15 us
  starting transfers between devices  7.86 us (52%)
  Pallas kernels  3.4 us (22%)
  between operations  2.67 us (18%)
  waiting for transfers between devices  1.07 us (7%)
    ppermute x5, starting transfers between devices, permute(): return lax.ppermute(value, axes, pairs)  7.86 us
    pallas_call x1, Pallas kernels, on_device(): pl.pallas_call(functools.partial(loss_kernel, width=width, harmonics=harm...  1.89 us
    ppermute x5, waiting for transfers between devices, permute(): return lax.ppermute(value, axes, pairs)  1.07 us
    pallas_call x1, Pallas kernels, on_device(): pl.pallas_call(functools.partial(pack_kernel, width=width), out_shape=hel...  0.98 us
    pallas_call x1, Pallas kernels, on_device(): pl.pallas_call(functools.partial(arrange_kernel, width=width), out_shape=...  0.52 us
  transfers between devices with their start and end apart: 5, of which 1 were waited for; matrix products, arithmetic and copies ran while one was open for 0% of the time, Pallas kernels for 10%

profile of v7, /device:TPU:0, one launch (start us, length us, event | category | flops | bytes accessed | tf_op | source)
XLA Modules:
  0.0 15.0 jit_solution(14939674893950473163)
XLA Ops:
  2.6 0.0 copy-start
  2.6 0.0 copy-start.1
  2.6 0.0 copy-start.2
  2.6 0.5 %collective-permute-start = (f32[1,128]{1,0:T(1,128)S(1)}, f32[1,128]{1,0:T(1,128)S(1)}, u32[]{:S(2)}, u32[]{:S(2)}) collective-permute-start(f32[1,128]{1,0:T(1,128)S(1)} %params.1.after), channel_id=1, source_target_pairs={{0,1},{1,0},{2,3},{3,2},{4,5},{5,4},{6,7},{7,6},{8,9},{9,8},{10,11... | collective-permute-start | bytes 1544 | tf_op jit(solution)/shard_map/ppermute | solution.py:514
  3.1 1.0 %pack.1 = f32[32,640]{1,0:T(8,128)S(1)} custom-call(f32[1,128]{1,0:T(1,128)S(1)} %params.1.after, f32[32,4096]{1,0:T(8,128)} %cur.3, f32[32,4096]{1,0:T(8,128)} %con.3, f32[32,4096]{1,0:T(8,128)} %coo.3), custom_call_target="tpu_custom_call" | custom-call | tf_op jit(solution)/shard_map/pack/pallas_call | solution.py:491
  4.1 0.0 collective-permute-done
  4.1 2.8 %collective-permute-start.1 = (f32[1,128]{1,0:T(1,128)S(1)}, f32[1,128]{1,0:T(1,128)S(1)}, u32[]{:S(2)}, u32[]{:S(2)}) collective-permute-start(f32[1,128]{1,0:T(1,128)S(1)} %max.10), channel_id=1, source_target_pairs={{0,2},{1,3},{2,0},{3,1},{4,6},{5,7},{6,4},{7,5},{8,10},{9,11},{10,... | collective-permute-start | bytes 1544 | tf_op jit(solution)/shard_map/ppermute | solution.py:514
  6.9 1.5 %collective-permute-start.2 = (f32[32,640]{1,0:T(8,128)S(1)}, f32[32,640]{1,0:T(8,128)S(1)}, u32[]{:S(2)}, u32[]{:S(2)}) collective-permute-start(f32[32,640]{1,0:T(8,128)S(1)} %pack.1), channel_id=1, source_target_pairs={{0,8},{1,0},{2,10},{3,2},{4,12},{5,4},{6,14},{7,6},{8,16},{9,1},{1... | collective-permute-start | bytes 245768 | tf_op jit(solution)/shard_map/ppermute | solution.py:514
  8.4 0.0 collective-permute-done.1
  8.4 3.1 %collective-permute-start.3 = (f32[1,1536]{1,0:T(1,128)S(1)}, f32[1,1536]{1,0:T(1,128)S(1)}, u32[]{:S(2)}, u32[]{:S(2)}) collective-permute-start(f32[1,1536]{1,0:T(1,128)S(1)} %bitcast.8), channel_id=1, source_target_pairs={{0,4},{1,5},{2,6},{3,7},{4,0},{5,1},{6,2},{7,3},{8,12},{9,13},{10,... | collective-permute-start | bytes 18440 | tf_op jit(solution)/shard_map/ppermute | solution.py:514
  11.5 0.0 collective-permute-done.2.got.near
  11.5 0.0 collective-permute-start.4
  11.6 0.0 copy-done
  11.6 0.0 copy-done.1
  11.6 0.0 copy-done.2
  11.6 0.5 %arrange.1 = (f32[32,640]{1,0:T(8,128)S(1)}, f32[32,640]{1,0:T(8,128)S(1)}, f32[32,640]{1,0:T(8,128)S(1)}) custom-call(f32[16,640]{1,0:T(8,128)S(1)} %pass_on.1.after, f32[32,4096]{1,0:T(8,128)S(1)} %copy-done, f32[32,4096]{1,0:T(8,128)S(1)} %copy-done.1, f32[32,4096]{1,0:T(8,128)S(1)} %copy-done.2), custom_call_target="tpu_custom_call" | custom-call | tf_op jit(solution)/shard_map/arrange/pallas_call | solution.py:547
  12.1 1.0 %collective-permute-done.3 = f32[1,1536]{1,0:T(1,128)S(1)} collective-permute-done((f32[1,1536]{1,0:T(1,128)S(1)}, f32[1,1536]{1,0:T(1,128)S(1)}, u32[]{:S(2)}, u32[]{:S(2)}) %collective-permute-start.3) | collective-permute-done | bytes 6176 | tf_op jit(solution)/shard_map/ppermute | solution.py:514
  13.1 0.0 collective-permute-done.4.far
  13.2 1.9 %losses.1 = (f32[32,512]{1,0:T(8,128)}, f32[32,512]{1,0:T(8,128)}) custom-call(f32[1,128]{1,0:T(1,128)S(1)} %slice_maximum_fusion.table, f32[32,640]{1,0:T(8,128)S(1)} %get-tuple-element.13.cur, f32[32,640]{1,0:T(8,128)S(1)} %get-tuple-element.14.con, f32[32,640]{1,0:T(8,128)S(1)} %get-tuple-element.15.coo, f32[32,640]{1,0:T(8,128)S(1)} %collective-permute-done.2.got.near, ...), custom_call_target="tpu_custom_call" | custom-call | tf_op jit(solution)/shard_map/losses/pallas_call | solution.py:565
  (7 shorter events, 0.0 us)
Async XLA Ops:
  2.6 9.0 %copy-start = (f32[32,4096]{1,0:T(8,128)S(1)}, f32[32,4096]{1,0:T(8,128)}, u32[]{:S(2)}) copy-start(f32[32,4096]{1,0:T(8,128)} %cur.3) | copy-start | bytes 1572868
  2.6 9.0 %copy-start.1 = (f32[32,4096]{1,0:T(8,128)S(1)}, f32[32,4096]{1,0:T(8,128)}, u32[]{:S(2)}) copy-start(f32[32,4096]{1,0:T(8,128)} %con.3) | copy-start | bytes 1572868
  2.6 9.0 %copy-start.2 = (f32[32,4096]{1,0:T(8,128)S(1)}, f32[32,4096]{1,0:T(8,128)}, u32[]{:S(2)}) copy-start(f32[32,4096]{1,0:T(8,128)} %coo.3) | copy-start | bytes 1572868
  2.6 1.5 %collective-permute-start = (f32[1,128]{1,0:T(1,128)S(1)}, f32[1,128]{1,0:T(1,128)S(1)}, u32[]{:S(2)}, u32[]{:S(2)}) collective-permute-start(f32[1,128]{1,0:T(1,128)S(1)} %params.1.after), channel_id=1, source_target_pairs={{0,1},{1,0},{2,3},{3,2},{4,5},{5,4},{6,7},{7,6},{8,9},{9,8},{10,11... | collective-permute-start | bytes 1544 | tf_op jit(solution)/shard_map/ppermute | solution.py:514
  4.1 4.3 %collective-permute-start.1 = (f32[1,128]{1,0:T(1,128)S(1)}, f32[1,128]{1,0:T(1,128)S(1)}, u32[]{:S(2)}, u32[]{:S(2)}) collective-permute-start(f32[1,128]{1,0:T(1,128)S(1)} %max.10), channel_id=1, source_target_pairs={{0,2},{1,3},{2,0},{3,1},{4,6},{5,7},{6,4},{7,5},{8,10},{9,11},{10,... | collective-permute-start | bytes 1544 | tf_op jit(solution)/shard_map/ppermute | solution.py:514
  6.9 4.6 %collective-permute-start.2 = (f32[32,640]{1,0:T(8,128)S(1)}, f32[32,640]{1,0:T(8,128)S(1)}, u32[]{:S(2)}, u32[]{:S(2)}) collective-permute-start(f32[32,640]{1,0:T(8,128)S(1)} %pack.1), channel_id=1, source_target_pairs={{0,8},{1,0},{2,10},{3,2},{4,12},{5,4},{6,14},{7,6},{8,16},{9,1},{1... | collective-permute-start | bytes 245768 | tf_op jit(solution)/shard_map/ppermute | solution.py:514
  8.4 4.7 %collective-permute-start.3 = (f32[1,1536]{1,0:T(1,128)S(1)}, f32[1,1536]{1,0:T(1,128)S(1)}, u32[]{:S(2)}, u32[]{:S(2)}) collective-permute-start(f32[1,1536]{1,0:T(1,128)S(1)} %bitcast.8), channel_id=1, source_target_pairs={{0,4},{1,5},{2,6},{3,7},{4,0},{5,1},{6,2},{7,3},{8,12},{9,13},{10,... | collective-permute-start | bytes 18440 | tf_op jit(solution)/shard_map/ppermute | solution.py:514
  11.5 1.6 %collective-permute-start.4 = (f32[16,640]{1,0:T(8,128)S(1)}, f32[16,640]{1,0:T(8,128)S(1)}, u32[]{:S(2)}, u32[]{:S(2)}) collective-permute-start(f32[16,640]{1,0:T(8,128)S(1)} %pass_on.1.after), channel_id=1, source_target_pairs={{0,1},{1,0},{2,3},{3,2},{4,5},{5,4},{6,7},{7,6},{8,9},{9,8},{10,11... | collective-permute-start | bytes 122888 | tf_op jit(solution)/shard_map/ppermute | solution.py:514

commit v8 on v7

--- a/solution.py
+++ b/solution.py
@@ -346,17 +346,20 @@
     ext = slab + 2 * TILE
     place, nt, sub = Place(width), width // LANES + 1, sublane_iota()
     cols = [slice(j * LANES, (j + 1) * LANES) for j in range(nt)]
-    xcur[top:bottom, :] = cur[...]
-    xcon[top:bottom, :] = con[...]
-    xcoo[top:bottom, :] = coo[...]
 
     def put(up, down):
-        xcur[0:TILE, :] = up[:TILE, :]
-        xcon[0:TILE, :] = up[TILE : 2 * TILE, :]
-        xcoo[0:TILE, :] = jnp.maximum(pltpu.roll(up[:TILE, :], TILE - 3, 0), 0.0)
-        xcur[bottom:ext, :] = down[:TILE, :]
-        xcon[bottom:ext, :] = down[TILE : 2 * TILE, :]
-        xcoo[bottom:ext, :] = jnp.maximum(pltpu.roll(down[:TILE, :], TILE - 5, 0), 0.0)
+        for rows, side, shift in (
+            (slice(0, TILE), up, TILE - 3),
+            (slice(TILE, 2 * TILE), down, TILE - 5),
+        ):
+            xcur[rows, :] = side[:TILE, :]
+            xcon[rows, :] = side[TILE : 2 * TILE, :]
+            xcoo[rows, :] = jnp.maximum(pltpu.roll(side[:TILE, :], shift, 0), 0.0)
+
+    def of_row(own, margins, row):
+        if top <= row < bottom:
+            return own, row - top
+        return margins, row if row < top else row - slab
 
     place.edges(near, far, put)
 
@@ -397,8 +400,9 @@
         def conduct(i, q):
             losses.append(q)
             scale = place.has_up if i == 0 else place.has_down if i == ntile - 1 else None
+            ref, at = of_row(coo, xcoo, i * TILE)
             w = [
-                pl.reciprocal(4.0 + xcoo[i * TILE : (i + 1) * TILE, col], approx=True) * x
+                pl.reciprocal(4.0 + ref[at : at + TILE, col], approx=True) * x
                 for col, x in zip(cols, place.inside)
             ]
             weights.append(w if scale is None else [x * scale for x in w])
@@ -447,7 +451,8 @@
                     add(row, [zero] * nt)
             eddy(
                 place, (table, group), harmonics, start, slab + 2 * MARGIN,
-                lambda row: spread(xcur, row + first, nt), lambda row: spread(xcon, row + first, nt),
+                lambda row: spread(*of_row(cur, xcur, row + first), nt),
+                lambda row: spread(*of_row(con, xcon, row + first), nt),
                 valid, rr, rb, hb, add,
             )
             for row in range(slab + 2 * MARGIN - 2, ext - first):
@@ -567,7 +572,7 @@
         out_shape=(shape(slab, width),) * 2,
         in_specs=[vmem] * 6,
         out_specs=(any_space,) * 2,
-        scratch_shapes=[flat] * 3
+        scratch_shapes=[pltpu.VMEM((2 * TILE, wide), F32)] * 3
         + [deep] * 3
         + [flat, pltpu.VMEM((2, slab, width), F32), pltpu.SemaphoreType.DMA((2, slab // TILE))],
         compiler_params=pltpu.CompilerParams(vmem_limit_bytes=12 * 2**20),

time: 15.2 us -> 15.3 us (level)
  no operation moved by 1% of the time
where the time goes in v8:
time: 15.3 us; the launch traced here: 15.1 us
  starting transfers between devices  7.86 us (51%)
  Pallas kernels  3.46 us (23%)
  between operations  2.67 us (17%)
  waiting for transfers between devices  1.07 us (7%)
    ppermute x5, starting transfers between devices, permute(): return lax.ppermute(value, axes, pairs)  7.86 us
    pallas_call x1, Pallas kernels, on_device(): pl.pallas_call(functools.partial(loss_kernel, width=width, harmonics=harm...  1.95 us
    ppermute x5, waiting for transfers between devices, permute(): return lax.ppermute(value, axes, pairs)  1.07 us
    pallas_call x1, Pallas kernels, on_device(): pl.pallas_call(functools.partial(pack_kernel, width=width), out_shape=hel...  0.98 us
    pallas_call x1, Pallas kernels, on_device(): pl.pallas_call(functools.partial(arrange_kernel, width=width), out_shape=...  0.52 us
  transfers between devices with their start and end apart: 5, of which 1 were waited for; matrix products, arithmetic and copies ran while one was open for 0% of the time, Pallas kernels for 10%

profile of v8, /device:TPU:0, one launch (start us, length us, event | category | flops | bytes accessed | tf_op | source)
XLA Modules:
  0.0 15.1 jit_solution(4990657754300797074)
XLA Ops:
  2.6 0.0 copy-start
  2.6 0.0 copy-start.1
  2.6 0.0 copy-start.2
  2.6 0.5 %collective-permute-start = (f32[1,128]{1,0:T(1,128)S(1)}, f32[1,128]{1,0:T(1,128)S(1)}, u32[]{:S(2)}, u32[]{:S(2)}) collective-permute-start(f32[1,128]{1,0:T(1,128)S(1)} %params.1.after), channel_id=1, source_target_pairs={{0,1},{1,0},{2,3},{3,2},{4,5},{5,4},{6,7},{7,6},{8,9},{9,8},{10,11... | collective-permute-start | bytes 1544 | tf_op jit(solution)/shard_map/ppermute | solution.py:519
  3.1 1.0 %pack.1 = f32[32,640]{1,0:T(8,128)S(1)} custom-call(f32[1,128]{1,0:T(1,128)S(1)} %params.1.after, f32[32,4096]{1,0:T(8,128)} %cur.3, f32[32,4096]{1,0:T(8,128)} %con.3, f32[32,4096]{1,0:T(8,128)} %coo.3), custom_call_target="tpu_custom_call" | custom-call | tf_op jit(solution)/shard_map/pack/pallas_call | solution.py:496
  4.1 0.0 collective-permute-done
  4.1 2.8 %collective-permute-start.1 = (f32[1,128]{1,0:T(1,128)S(1)}, f32[1,128]{1,0:T(1,128)S(1)}, u32[]{:S(2)}, u32[]{:S(2)}) collective-permute-start(f32[1,128]{1,0:T(1,128)S(1)} %max.10), channel_id=1, source_target_pairs={{0,2},{1,3},{2,0},{3,1},{4,6},{5,7},{6,4},{7,5},{8,10},{9,11},{10,... | collective-permute-start | bytes 1544 | tf_op jit(solution)/shard_map/ppermute | solution.py:519
  6.9 1.5 %collective-permute-start.2 = (f32[32,640]{1,0:T(8,128)S(1)}, f32[32,640]{1,0:T(8,128)S(1)}, u32[]{:S(2)}, u32[]{:S(2)}) collective-permute-start(f32[32,640]{1,0:T(8,128)S(1)} %pack.1), channel_id=1, source_target_pairs={{0,8},{1,0},{2,10},{3,2},{4,12},{5,4},{6,14},{7,6},{8,16},{9,1},{1... | collective-permute-start | bytes 245768 | tf_op jit(solution)/shard_map/ppermute | solution.py:519
  8.4 0.0 collective-permute-done.1
  8.4 3.1 %collective-permute-start.3 = (f32[1,1536]{1,0:T(1,128)S(1)}, f32[1,1536]{1,0:T(1,128)S(1)}, u32[]{:S(2)}, u32[]{:S(2)}) collective-permute-start(f32[1,1536]{1,0:T(1,128)S(1)} %bitcast.8), channel_id=1, source_target_pairs={{0,4},{1,5},{2,6},{3,7},{4,0},{5,1},{6,2},{7,3},{8,12},{9,13},{10,... | collective-permute-start | bytes 18440 | tf_op jit(solution)/shard_map/ppermute | solution.py:519
  11.5 0.0 collective-permute-done.2.got.near
  11.5 0.0 collective-permute-start.4
  11.6 0.0 copy-done
  11.6 0.0 copy-done.1
  11.6 0.0 copy-done.2
  11.6 0.5 %arrange.1 = (f32[32,640]{1,0:T(8,128)S(1)}, f32[32,640]{1,0:T(8,128)S(1)}, f32[32,640]{1,0:T(8,128)S(1)}) custom-call(f32[16,640]{1,0:T(8,128)S(1)} %pass_on.1.after, f32[32,4096]{1,0:T(8,128)S(1)} %copy-done, f32[32,4096]{1,0:T(8,128)S(1)} %copy-done.1, f32[32,4096]{1,0:T(8,128)S(1)} %copy-done.2), custom_call_target="tpu_custom_call" | custom-call | tf_op jit(solution)/shard_map/arrange/pallas_call | solution.py:552
  12.1 1.0 %collective-permute-done.3 = f32[1,1536]{1,0:T(1,128)S(1)} collective-permute-done((f32[1,1536]{1,0:T(1,128)S(1)}, f32[1,1536]{1,0:T(1,128)S(1)}, u32[]{:S(2)}, u32[]{:S(2)}) %collective-permute-start.3) | collective-permute-done | bytes 6176 | tf_op jit(solution)/shard_map/ppermute | solution.py:519
  13.1 0.0 collective-permute-done.4.far
  13.2 1.9 %losses.1 = (f32[32,512]{1,0:T(8,128)}, f32[32,512]{1,0:T(8,128)}) custom-call(f32[1,128]{1,0:T(1,128)S(1)} %slice_maximum_fusion.table, f32[32,640]{1,0:T(8,128)S(1)} %get-tuple-element.13.cur, f32[32,640]{1,0:T(8,128)S(1)} %get-tuple-element.14.con, f32[32,640]{1,0:T(8,128)S(1)} %get-tuple-element.15.coo, f32[32,640]{1,0:T(8,128)S(1)} %collective-permute-done.2.got.near, ...), custom_call_target="tpu_custom_call" | custom-call | tf_op jit(solution)/shard_map/losses/pallas_call | solution.py:570
  (7 shorter events, 0.0 us)
Async XLA Ops:
  2.6 9.0 %copy-start = (f32[32,4096]{1,0:T(8,128)S(1)}, f32[32,4096]{1,0:T(8,128)}, u32[]{:S(2)}) copy-start(f32[32,4096]{1,0:T(8,128)} %cur.3) | copy-start | bytes 1572868
  2.6 9.0 %copy-start.1 = (f32[32,4096]{1,0:T(8,128)S(1)}, f32[32,4096]{1,0:T(8,128)}, u32[]{:S(2)}) copy-start(f32[32,4096]{1,0:T(8,128)} %con.3) | copy-start | bytes 1572868
  2.6 9.0 %copy-start.2 = (f32[32,4096]{1,0:T(8,128)S(1)}, f32[32,4096]{1,0:T(8,128)}, u32[]{:S(2)}) copy-start(f32[32,4096]{1,0:T(8,128)} %coo.3) | copy-start | bytes 1572868
  2.6 1.5 %collective-permute-start = (f32[1,128]{1,0:T(1,128)S(1)}, f32[1,128]{1,0:T(1,128)S(1)}, u32[]{:S(2)}, u32[]{:S(2)}) collective-permute-start(f32[1,128]{1,0:T(1,128)S(1)} %params.1.after), channel_id=1, source_target_pairs={{0,1},{1,0},{2,3},{3,2},{4,5},{5,4},{6,7},{7,6},{8,9},{9,8},{10,11... | collective-permute-start | bytes 1544 | tf_op jit(solution)/shard_map/ppermute | solution.py:519
  4.1 4.3 %collective-permute-start.1 = (f32[1,128]{1,0:T(1,128)S(1)}, f32[1,128]{1,0:T(1,128)S(1)}, u32[]{:S(2)}, u32[]{:S(2)}) collective-permute-start(f32[1,128]{1,0:T(1,128)S(1)} %max.10), channel_id=1, source_target_pairs={{0,2},{1,3},{2,0},{3,1},{4,6},{5,7},{6,4},{7,5},{8,10},{9,11},{10,... | collective-permute-start | bytes 1544 | tf_op jit(solution)/shard_map/ppermute | solution.py:519
  6.9 4.6 %collective-permute-start.2 = (f32[32,640]{1,0:T(8,128)S(1)}, f32[32,640]{1,0:T(8,128)S(1)}, u32[]{:S(2)}, u32[]{:S(2)}) collective-permute-start(f32[32,640]{1,0:T(8,128)S(1)} %pack.1), channel_id=1, source_target_pairs={{0,8},{1,0},{2,10},{3,2},{4,12},{5,4},{6,14},{7,6},{8,16},{9,1},{1... | collective-permute-start | bytes 245768 | tf_op jit(solution)/shard_map/ppermute | solution.py:519
  8.4 4.7 %collective-permute-start.3 = (f32[1,1536]{1,0:T(1,128)S(1)}, f32[1,1536]{1,0:T(1,128)S(1)}, u32[]{:S(2)}, u32[]{:S(2)}) collective-permute-start(f32[1,1536]{1,0:T(1,128)S(1)} %bitcast.8), channel_id=1, source_target_pairs={{0,4},{1,5},{2,6},{3,7},{4,0},{5,1},{6,2},{7,3},{8,12},{9,13},{10,... | collective-permute-start | bytes 18440 | tf_op jit(solution)/shard_map/ppermute | solution.py:519
  11.5 1.6 %collective-permute-start.4 = (f32[16,640]{1,0:T(8,128)S(1)}, f32[16,640]{1,0:T(8,128)S(1)}, u32[]{:S(2)}, u32[]{:S(2)}) collective-permute-start(f32[16,640]{1,0:T(8,128)S(1)} %pass_on.1.after), channel_id=1, source_target_pairs={{0,1},{1,0},{2,3},{3,2},{4,5},{5,4},{6,7},{7,6},{8,9},{9,8},{10,11... | collective-permute-start | bytes 122888 | tf_op jit(solution)/shard_map/ppermute | solution.py:519
